TPU v7x, 128 devices: a whole 4x4x4 slice. The times are simulated.
128 devices in a mesh: section: 4 (over y), vocab: 32 (over x, z, core).
Axes of the slice: x: 4, y: 4, z: 4, core: 2. Of those that a mesh axis runs over, the one named last changes fastest.
Arguments:
- hidden_rows: bfloat16 [1024, 8192], P(('section', 'vocab')), may hold values from -170 to 170
- norm_gain: float32 [8192], replicated, may hold values from 0.5 to 1.5
- head_weight: bfloat16 [8192, 65536], P('section', 'vocab'), may hold values from -1.7 to 1.7
- targets: int32 [1024], P(('section', 'vocab')), may hold values from 0 to 65535
- exit_layer: int32 [4], replicated, may hold values from 0 to 79
- numerators: int32 [80], replicated, may hold values from 1 to 16
Outputs:
- hidden_grad: bfloat16 [1024, 8192], P(('section', 'vocab'))
- gain_grad: float32 [8192], replicated
- head_grad: bfloat16 [8192, 65536], P('section', 'vocab')
- total_loss: float32 [], replicated
All inputs are finite; a program needn't handle non-finite values.
Results may differ from a plain program's by a relative error of at most 0.0082.
Values may be sent and summed in bfloat16 or wider, within the bound.
No kernel may reach another device: no remote copies, remote signals or barrier semaphores. Data moves between devices by JAX's collectives and lax.ppermute only.
A program may use at most 128 MiB of HBM per device.

v0:
```python
import jax
import jax.numpy as jnp
from jax import lax
from jax.sharding import PartitionSpec as P

EPS = 1e-05


def section_weights(exit_layer, numerators):
    layers = numerators.shape[0]
    matches = exit_layer[:, None] == jnp.arange(layers, dtype=jnp.int32)[None, :]
    picked = jnp.sum(jnp.where(matches, numerators[None, :], 0), axis=1).astype(jnp.float32)
    return picked / jnp.sum(picked)


def row_statistics(logits, column_ids, wanted):
    onehot = column_ids[None, :] == wanted[:, None]
    local_max = jnp.max(logits, axis=1)
    picked = jnp.sum(jnp.where(onehot, logits, 0.0), axis=1)
    row_max = lax.pmax(local_max, "vocab")
    local_total = jnp.sum(jnp.exp(logits - row_max[:, None]), axis=1)
    row_total, picked = lax.psum((local_total, picked), "vocab")
    log_total = row_max + jnp.log(row_total)
    return (log_total, picked, onehot)


def logit_grads(logits, log_total, onehot, weight):
    probabilities = jnp.exp(logits - log_total[:, None])
    return (weight[:, None] * (probabilities - onehot.astype(jnp.float32))).astype(jnp.bfloat16)


def local(hidden_rows, norm_gain, head_weight, targets, exit_layer, numerators):
    sections = lax.axis_size("section")
    pieces = lax.axis_size("vocab")
    piece_here = lax.axis_index("vocab")
    own_rows = hidden_rows.shape[0]
    vocab_shard = head_weight.shape[1]
    values = hidden_rows.astype(jnp.float32)
    inverse_rms = lax.rsqrt(jnp.mean(values * values, axis=1, keepdims=True) + EPS)
    normed = (values * inverse_rms * norm_gain[None, :]).astype(jnp.bfloat16)
    spread = lax.all_to_all(normed, "section", split_axis=1, concat_axis=0, tiled=True)
    columns = lax.all_gather(spread, "vocab", axis=0, tiled=True)
    total_rows = columns.shape[0]
    gathered_targets = lax.all_gather(targets, ("section", "vocab"), axis=0, tiled=True)
    all_targets = jnp.transpose(
        gathered_targets.reshape(sections, pieces, own_rows), (1, 0, 2)
    ).reshape(total_rows)
    weights = section_weights(exit_layer, numerators)
    row_weight = jnp.broadcast_to(weights[None, :, None], (pieces, sections, own_rows)).reshape(
        total_rows
    )
    column_ids = piece_here * vocab_shard + jnp.arange(vocab_shard, dtype=jnp.int32)
    logits = lax.psum(jnp.dot(columns, head_weight, preferred_element_type=jnp.float32), "section")
    log_total, picked, onehot = row_statistics(logits, column_ids, all_targets)
    dlogit = logit_grads(logits, log_total, onehot, row_weight)
    total_loss = jnp.sum(row_weight * (log_total - picked))
    head_grad = lax.dot_general(
        columns, dlogit, (((0,), (0,)), ((), ())), preferred_element_type=jnp.float32
    ).astype(jnp.bfloat16)
    reduced = lax.psum_scatter(
        lax.dot_general(
            dlogit, head_weight, (((1,), (1,)), ((), ())), preferred_element_type=jnp.float32
        ),
        "vocab",
        scatter_dimension=0,
        tiled=True,
    )
    dnormed = lax.all_to_all(reduced, "section", split_axis=0, concat_axis=1, tiled=True)
    gained = dnormed * norm_gain[None, :]
    inner_mean = jnp.mean(gained * values, axis=1, keepdims=True)
    hidden_grad = (
        inverse_rms * gained - values * (inverse_rms * inverse_rms * inverse_rms) * inner_mean
    ).astype(jnp.bfloat16)
    gain_part = jnp.sum(dnormed * values * inverse_rms, axis=0)
    gain_grad = lax.psum(gain_part, ("section", "vocab"))
    return (hidden_grad, gain_grad, head_grad, total_loss)


def solution(mesh):
    return jax.shard_map(
        local,
        mesh=mesh,
        in_specs=(
            P(("section", "vocab"), None),
            P(),
            P("section", "vocab"),
            P(("section", "vocab")),
            P(),
            P(),
        ),
        out_specs=(P(("section", "vocab"), None), P(), P("section", "vocab"), P()),
        check_vma=False,
    )
```

profile of v0, /device:TPU:0, one launch (start us, length us, event | category | flops | bytes accessed | tf_op | source)
XLA Modules:
  0.0 579.3 jit_solution(16204253856503052066)
XLA Ops:
  7.2 0.0 all-gather.2.cloned.1.call-start
  7.2 1.1 fusion.4
  8.3 1.0 fusion.6
  9.3 10.4 %all_to_all.38 = bf16[8,4,2048]{2,0,1:T(8,128)(2,1)} all-to-all(bf16[8,4,2048]{2,0,1:T(8,128)(2,1)S(1)} %bitcast.16), channel_id=1, replica_groups=mesh['section'=4,'vocab'=32] {'section'}, dimensions={1} | all-to-all | bytes 262144 | tf_op jit(solution)/shard_map/all_to_all | solution.py:41
  19.8 0.0 all-gather.2.cloned.1.call-update
  19.8 0.0 all-reduce.4.cloned.1.call-start
  19.8 46.8 %all-gather.2.cloned.1.call-done = bf16[1024,2048]{1,0:T(8,128)(2,1)} async-done(((bf16[32,2048]{1,0:T(8,128)(2,1)}), bf16[1024,2048]{1,0:T(8,128)(2,1)}) %all-gather.2.cloned.1.call-update) | async-done | bytes 4194320 | tf_op jit(solution)/shard_map/all_gather | solution.py:42
  66.7 14.5 %fusion.16 = f32[1024,2048]{1,0:T(8,128)} fusion(bf16[1024,2048]{1,0:T(8,128)(2,1)} %all-gather.2.cloned.1.call-done, bf16[2048,2048]{1,0:T(8,128)(2,1)} %param.8), kind=kOutput, calls=%fused_computation.33 | convolution fusion | flops 8589934592 | bytes 20971520 | tf_op jit(solution)/shard_map/dot_general | solution.py:53
  81.1 0.0 copy-start.2
  81.1 0.0 copy-start.3
  81.1 0.0 copy-start.4
  81.1 0.0 all-reduce.4.cloned.1.call-update
  81.2 0.0 reduce-scatter.2.cloned.1.call-start
  81.2 0.6 copy-done.2
  81.8 0.0 copy-done.3
  81.8 0.2 select_reduce_fusion
  82.0 0.6 convert_reduce_fusion
  82.6 0.6 convert_divide_fusion
  83.3 0.1 broadcast_in_dim.20
  83.3 0.1 mul.93
  83.5 0.0 copy-done.4
  83.5 0.2 dynamic-update-slice
  83.7 68.2 %all-reduce = s32[1024]{0:T(1024)S(1)} all-reduce(s32[1024]{0:T(1024)S(1)} %dynamic-update-slice), channel_id=1, replica_groups=mesh['section'=4,'vocab'=32] {'section','vocab'}, use_global_device_ids=true, to_apply=%add | all-reduce | flops 1024 | bytes 8192
  151.9 0.1 reshape.51
  152.0 0.1 eq.32
  152.1 90.1 %all-reduce.4.cloned.1.call-done = f32[1024,2048]{1,0:T(8,128)} async-done(((f32[1024,2048]{1,0:T(8,128)}), f32[1024,2048]{1,0:T(8,128)}) %all-reduce.4.cloned.1.call-update) | async-done | bytes 8388624 | tf_op jit(solution)/shard_map/psum | solution.py:53
  242.3 3.8 reduce_max.9
  246.1 67.2 %pmax.7 = f32[1024]{0:T(1024)S(1)} all-reduce(f32[1024]{0:T(1024)S(1)} %reduce_max.9), channel_id=1, replica_groups=mesh['section'=4,'vocab'=32] {'vocab'}, use_global_device_ids=true, to_apply=%region_5.6 | all-reduce | flops 1024 | bytes 8192 | tf_op jit(solution)/shard_map/pmax | solution.py:20
  313.3 4.7 fusion.3
  318.0 63.7 %all-reduce.1 = (f32[1024]{0:T(1024)S(1)}, f32[1024]{0:T(1024)S(1)}) all-reduce(f32[1024]{0:T(1024)S(1)} %get-tuple-element.5, f32[1024]{0:T(1024)S(1)} %get-tuple-element.4), channel_id=1, replica_groups=mesh['section'=4,'vocab'=32] {'vocab'}, use_global_device_ids=true, to_apply=%region_7.8 | all-reduce | flops 2048 | bytes 16384 | tf_op jit(solution)/shard_map/psum | solution.py:22
  381.7 0.6 multiply_reduce_fusion
  382.3 16.3 %fusion.14 = f32[1024,2048]{1,0:T(8,128)} fusion(bf16[2048,2048]{1,0:T(8,128)(2,1)} %param.8, f32[1024,2048]{1,0:T(8,128)} %all-reduce.4.cloned.1.call-done, s32[2048]{0:T(1024)S(1)} %iota_add_fusion, f32[1024]{0:T(1024)S(1)} %get-tuple-element.11, f32[1024]{0:T(1024)S(1)} %mul.93, s32[1024]{0:T(1024)S(1)} %eq.32), kind=kOutput, calls=%fused_computation.32 | convolution fusion | flops 8602517504 | bytes 25186304 | tf_op jit(solution)/shard_map/dot_general | solution.py:61
  398.6 0.0 reduce-scatter.2.cloned.1.call-update
  398.6 87.8 %reduce-scatter.2.cloned.1.call-done = f32[32,2048]{1,0:T(8,128)} async-done(((f32[1024,2048]{1,0:T(8,128)}), f32[32,2048]{1,0:T(8,128)}) %reduce-scatter.2.cloned.1.call-update) | async-done | bytes 262160 | tf_op jit(solution)/shard_map/reduce_scatter | solution.py:60
  486.4 4.3 all-to-all-start.1
  490.7 0.0 copy-start
  490.7 0.0 copy-start.1
  490.7 15.7 %convolution_convert_fusion = bf16[2048,2048]{1,0:T(8,128)(2,1)} fusion(bf16[1024,2048]{1,0:T(8,128)(2,1)} %all-gather.2.cloned.1.call-done, f32[1024,2048]{1,0:T(8,128)} %all-reduce.4.cloned.1.call-done, s32[2048]{0:T(1024)S(1)} %iota_add_fusion, f32[1024]{0:T(1024)S(1)} %get-tuple-element.11, f32[1024]{0:T(1024)S(1)} %mul.93, s32[1024]{0:T(1024)S(1)} %eq.32), kind=kOutput, calls=%fused_computation.7 | convolution fusion | flops 8606711808 | bytes 20992000 | tf_op jit(solution)/shard_map/dot_general | solution.py:57
  506.4 0.0 all-to-all-done.1
  506.4 0.0 copy-done
  506.4 0.0 copy-done.1
  506.4 0.3 fusion.12
  506.7 65.3 %psum.30 = f32[8192]{0:T(1024)} all-reduce(f32[8192]{0:T(1024)S(1)} %get-tuple-element.6), channel_id=1, replica_groups=mesh['section'=4,'vocab'=32] {'section','vocab'}, use_global_device_ids=true, to_apply=%region_11.12 | all-reduce | flops 8192 | bytes 65536 | tf_op jit(solution)/shard_map/psum | solution.py:75
  572.0 0.8 fusion.9
  (5 shorter events, 0.1 us)
Async XLA Ops:
  7.2 59.5 %all-gather.2.cloned.1.call-start = ((), (), s32[]{:S(2)}) async-start(), calls=%async_computation.3 | async-start | bytes 4325376 | tf_op jit(solution)/shard_map/all_gather | solution.py:42
  19.8 222.5 %all-reduce.4.cloned.1.call-start = ((), (), s32[]{:S(2)}) async-start(), calls=%async_computation.4 | async-start | bytes 16777216 | tf_op jit(solution)/shard_map/psum | solution.py:53
  81.1 0.7 copy-start.2
  81.1 0.7 copy-start.3
  81.1 2.3 copy-start.4
  81.2 405.2 %reduce-scatter.2.cloned.1.call-start = ((), (), s32[]{:S(2)}) async-start(), calls=%async_computation.5 | async-start | bytes 8650752 | tf_op jit(solution)/shard_map/reduce_scatter | solution.py:60
  486.4 20.0 %all-to-all-start.1 = ((f32[4,8,2048]{2,1,0:T(8,128)}), f32[4,8,2048]{2,1,0:T(8,128)S(1)}, u32[]{:S(2)}, u32[]{:S(2)}) async-start(f32[4,8,2048]{2,1,0:T(8,128)} %bitcast.17), calls=%async_computation.2 | async-start | bytes 524288 | tf_op jit(solution)/shard_map/all_to_all | solution.py:68
  490.7 15.7 %copy-start = (bf16[8,8192]{1,0:T(8,128)(2,1)S(1)}, bf16[8,8192]{1,0:T(8,128)(2,1)}, u32[]{:S(2)}) copy-start(bf16[8,8192]{1,0:T(8,128)(2,1)} %param.6) | copy-start | bytes 393220
  490.7 15.7 %copy-start.1 = (f32[8192]{0:T(1024)S(1)}, f32[8192]{0:T(1024)}, u32[]{:S(2)}) copy-start(f32[8192]{0:T(1024)} %param.7) | copy-start | bytes 98308
Sparse Core Ops, SparseCore 0:
  19.9 46.7 all-gather.1
  81.3 160.9 all-reduce.3
  398.8 87.6 reduce-scatter.1
where the time goes:
time: 580 us; the launch traced here: 579 us
  blocking collectives  275 us (47%)
  waiting for transfers between devices  225 us (39%)
  matrix products  46.5 us (8%)
  between operations  13.9 us (2%)
  other arithmetic  13.7 us (2%)
    psum x1, waiting for transfers between devices, local(): lax.psum(jnp.dot(columns, head_weight, preferred_element_type=jnp.float32...  90.1 us
    reduce_scatter x1, waiting for transfers between devices, local(): lax.psum_scatter(lax.dot_general(dlogit, head_weight, (((1,), (1,)), ((),...  87.8 us
    unnamed x1, blocking collectives  68.2 us
    pmax x1, blocking collectives, row_statistics(): row_max = lax.pmax(local_max, 'vocab')  67.2 us
    psum x1, blocking collectives, local(): gain_grad = lax.psum(gain_part, ('section', 'vocab'))  65.3 us
    psum x1, blocking collectives, row_statistics(): row_total, picked = lax.psum((local_total, picked), 'vocab')  63.7 us
    all_gather x1, waiting for transfers between devices, local(): columns = lax.all_gather(spread, 'vocab', axis=0, tiled=True)  46.8 us
    dot_general x1, matrix products, local(): lax.dot_general(dlogit, head_weight, (((1,), (1,)), ((), ())), preferred_...  16.3 us
  transfers between devices with their start and end apart: 4, of which 3 were waited for; matrix products, arithmetic and copies ran while one was open for 3% of the time, Pallas kernels for 0%

commit v1 on v0

v1 whole, which is shorter than its diff:
```python
import functools
import jax
import jax.numpy as jnp
from jax import lax
from jax.experimental import pallas as pl
from jax.experimental.pallas import tpu as pltpu
from jax.sharding import PartitionSpec as P

EPS = 1e-05
SIDE = 4
TAIL = 128
TILE = 256
F32 = jnp.float32
BF16 = jnp.bfloat16
ANY = pl.BlockSpec(memory_space=pl.ANY)
VMEM = pl.BlockSpec(memory_space=pltpu.VMEM)
SMEM = pl.BlockSpec(memory_space=pltpu.SMEM)
PARAMS = pltpu.CompilerParams(vmem_limit_bytes=22 * 2**20)


def over_section(x, step):
    return lax.ppermute(x, "section", [(i, (i + step) % SIDE) for i in range(SIDE)])


def over_vocab(x, dx=0, dz=0, dc=0):
    pairs = []
    for px in range(SIDE):
        for pz in range(SIDE):
            for pc in range(2):
                to = (((px + dx) % SIDE) * SIDE + (pz + dz) % SIDE) * 2 + (pc ^ dc)
                pairs.append(((px * SIDE + pz) * 2 + pc, to))
    return lax.ppermute(x, "vocab", pairs)


def shape(*dims, dtype=F32):
    return jax.ShapeDtypeStruct(dims, dtype)


def cost(flops, moved):
    return pl.CostEstimate(flops=flops, bytes_accessed=moved, transcendentals=0)


def in_vmem(x):
    return pltpu.with_memory_space_constraint(x, pltpu.VMEM)


def in_hbm(x):
    return pltpu.with_memory_space_constraint(x, pltpu.HBM)


def launch(kernel, operands, after=(), *, in_specs, scratch_shapes=(), name, **options):
    used, ignored = len(operands), len(after)

    def body(*refs):
        kernel(*refs[:used], *refs[used + ignored :])

    return pl.pallas_call(
        body,
        in_specs=[*in_specs, *[ANY] * ignored],
        scratch_shapes=list(scratch_shapes),
        compiler_params=PARAMS,
        name=name,
        **options,
    )(*operands, *after)


def encode(x, message, at):
    rows, width = x.shape
    largest = jnp.max(jnp.abs(x), axis=1, keepdims=True)
    power = jnp.clip(jnp.floor(jnp.log2(jnp.maximum(largest, 1e-30))) + 1.0, -100.0, 100.0)
    codes = jnp.clip(jnp.round(x * jnp.exp2(15.0 - power)), -32767.0, 32767.0)
    message[pl.ds(at, rows), :width] = codes.astype(jnp.int32).astype(jnp.int16)
    tail = jnp.broadcast_to(power, (rows, TAIL)).astype(jnp.int32)
    message[pl.ds(at, rows), width:] = tail.astype(jnp.int16)


def decode(message, at, rows):
    width = message.shape[1] - TAIL
    power = message[pl.ds(at, rows), width:].astype(jnp.int32).astype(F32)[:, :1]
    codes = message[pl.ds(at, rows), :width].astype(jnp.int32).astype(F32)
    return codes * jnp.exp2(power - 15.0)


def hold_kernel(head, held, sem):
    copy = pltpu.make_async_copy(head, held, sem)
    copy.start()
    copy.wait()


def hold(head, after=()):
    return launch(
        hold_kernel,
        (in_hbm(head),),
        after,
        out_shape=pltpu.VMEM(head.shape, head.dtype),
        in_specs=[ANY],
        out_specs=VMEM,
        scratch_shapes=[pltpu.SemaphoreType.DMA(())],
        cost_estimate=cost(0, 2 * head.size),
        name="hold_head",
    )


def normalise_kernel(place, hidden, gain, targets, *blocks):
    rows, width = hidden.shape
    depth = width // SIDE
    values = hidden[...].astype(F32)
    inverse = lax.rsqrt(jnp.mean(values * values, axis=1, keepdims=True) + EPS)
    lane = lax.broadcasted_iota(jnp.int32, (rows, TAIL), 1)
    row = lax.broadcasted_iota(jnp.int32, (rows, TAIL), 0)
    digits = jnp.zeros((rows, TAIL), jnp.int32)
    for i in range(rows):
        high = targets[i] // 256
        low = targets[i] - high * 256
        digits = jnp.where(row == i, jnp.where(lane == 0, high, jnp.where(lane == 1, low, 0)), digits)
    digits = digits.astype(F32).astype(BF16)
    for step in range(SIDE):
        at = pl.multiple_of(lax.rem(place[0] + step, SIDE) * depth, depth)
        cut = hidden[:, pl.ds(at, depth)].astype(F32) * inverse * gain[:, pl.ds(at, depth)]
        blocks[step][:, :depth] = cut.astype(BF16)
        blocks[step][:, depth:] = digits


def normalise(place, hidden, gain, targets, after=()):
    rows, width = hidden.shape
    return launch(
        normalise_kernel,
        (place, hidden, gain, targets,),
        after,
        out_shape=[shape(rows, width // SIDE + TAIL, dtype=BF16)] * SIDE,
        in_specs=[SMEM, VMEM, VMEM, SMEM],
        out_specs=[VMEM] * SIDE,
        cost_estimate=cost(10 * rows * width, 8 * rows * width),
        name="normalise",
    )


def logits_kernel(offsets, count, *refs):
    pieces, head, refs = refs[:count], refs[count], refs[count + 1 :]
    depth, columns = head.shape
    outs, (rows, sems) = refs[:2], refs[-2:]
    per = rows.shape[1]
    step = pl.program_id(0)

    @pl.when(step == 0)
    def _():
        copies = []
        for i, ds in enumerate(offsets):
            at = 0
            for piece in pieces:
                span = piece.shape[1]
                to = rows.at[i, pl.ds(at, span), :]
                sem = sems.at[len(copies)]
                copies.append(pltpu.make_async_copy(piece.at[ds, :, pl.ds(0, depth)], to, sem))
                at += span
        for copy in copies:
            copy.start()
        for copy in copies:
            copy.wait()

    cut = pl.ds(pl.multiple_of(step * TILE, TILE), TILE)
    part = jnp.dot(rows[...].reshape(-1, depth), head[:, cut], preferred_element_type=F32)
    if offsets != (2,):
        for i in range(len(offsets)):
            outs[i][...] = part[i * per : (i + 1) * per]
        return
    far = refs[2]
    far[:, cut] = part

    @pl.when(step == pl.num_programs(0) - 1)
    def _():
        half = per // 2
        for at in range(0, half, 32):
            encode(far[pl.ds(at, 32), :], outs[0], at)
            encode(far[pl.ds(half + at, 32), :], outs[1], at)


def logits_of(offsets, pieces, head, after=()):
    depth, columns = head.shape
    count, per = len(offsets), sum(p.shape[1] for p in pieces)
    if offsets == (2,):
        outs = [shape(per // 2, columns + TAIL, dtype=jnp.int16)] * 2
        specs = [pl.BlockSpec((per // 2, columns + TAIL), lambda j: (0, 0))] * 2
        scratch = [pltpu.VMEM((per, columns), F32)]
    else:
        outs = [shape(per, columns)] * count
        specs = [pl.BlockSpec((per, TILE), lambda j: (0, j))] * count
        scratch = []
    scratch += [pltpu.VMEM((count, per, depth), BF16), pltpu.SemaphoreType.DMA((count * len(pieces),))]
    kernel = functools.partial(logits_kernel, offsets, len(pieces))
    if count == 1 and offsets != (2,):
        def kernel(*refs):
            at = len(pieces) + 1
            logits_kernel(offsets, len(pieces), *refs[: at + 1], None, *refs[at + 1 :])

    return launch(
        kernel,
        (*pieces, in_vmem(head)),
        after,
        grid=(columns // TILE,),
        out_shape=outs,
        in_specs=[ANY] * len(pieces) + [VMEM],
        out_specs=specs,
        scratch_shapes=scratch,
        cost_estimate=cost(0, 2 * depth * columns + 4 * count * per * columns),
        name="partial_logits",
    )


def pass_on_kernel(first, last, up, down, to_first, to_last):
    per = first.shape[0]
    half = per // 2
    for at in range(0, half, 32):
        encode(first[pl.ds(at, 32), :] + decode(up, at, 32), to_first, at)
        encode(last[pl.ds(at, 32), :], to_last, at)
        encode(first[pl.ds(half + at, 32), :], to_first, half + at)
        encode(last[pl.ds(half + at, 32), :] + decode(down, at, 32), to_last, half + at)


def pass_on(first, last, up, down, after=()):
    per, columns = first.shape
    return launch(
        pass_on_kernel,
        (first, last, up, down,),
        after,
        out_shape=[shape(per, columns + TAIL, dtype=jnp.int16)] * 2,
        in_specs=[VMEM] * 4,
        out_specs=[VMEM] * 2,
        cost_estimate=cost(20 * per * columns, 14 * per * columns),
        name="pass_on",
    )


def onehot_of(place, digits, columns):
    want = digits[:, :1].astype(F32) * 256.0 + digits[:, 1:2].astype(F32)
    want = want.astype(jnp.int32) - place[4]
    return lax.broadcasted_iota(jnp.int32, (digits.shape[0], columns), 1) == want


def own_logits_kernel(count, place, own, below, above, *refs):
    digits, (exps, stats) = refs[: 2 * count], refs[2 * count :]
    per, columns = own.shape
    at = 0
    for digit in digits:
        span = digit.shape[1]
        lane = lax.broadcasted_iota(jnp.int32, (span, TAIL), 1)
        x = own[pl.ds(at, span), :] + (decode(below, at, span) + decode(above, at, span))
        top = jnp.max(x, axis=1, keepdims=True)
        exp = jnp.exp(x - top)
        exps[at // (per // 2), pl.ds(at % (per // 2), span), :] = exp.astype(BF16)
        total = jnp.sum(exp, axis=1, keepdims=True)
        pick = jnp.sum(jnp.where(onehot_of(place, digit[0], columns), x, 0.0), axis=1, keepdims=True)
        stats[pl.ds(at, span), :] = jnp.where(lane == 0, top, jnp.where(lane == 1, total, pick))
        at += span


def digit_specs(pieces):
    at = pieces[0].shape[2] // TAIL - 1
    return [pl.BlockSpec((1, p.shape[1], TAIL), lambda j: (0, 0, at)) for p in pieces]


def own_logits(place, own, below, above, mine, theirs, after=()):
    per, columns = own.shape
    full = pl.BlockSpec((per, columns), lambda j: (0, 0))
    coded = pl.BlockSpec((per, columns + TAIL), lambda j: (0, 0))
    return launch(
        functools.partial(own_logits_kernel, len(mine)),
        (place, own, below, above, *mine, *theirs),
        after,
        grid=(1,),
        out_shape=[shape(2, per // 2, columns, dtype=BF16), shape(per, TAIL)],
        in_specs=[SMEM, full, coded, coded] + digit_specs([*mine, *theirs]),
        out_specs=[pl.BlockSpec((2, per // 2, columns), lambda j: (0, 0, 0)), pl.BlockSpec((per, TAIL), lambda j: (0, 0))],
        cost_estimate=cost(20 * per * columns, 12 * per * columns),
        name="own_logits",
    )


def at_owner(place, dz, dc, dx, size):
    z = lax.rem(place[2] + dz, SIDE)
    x = lax.rem(place[1] + dx, SIDE)
    c = lax.rem(place[3] + dc, 2)
    return pl.multiple_of(((z * 2 + c) * SIDE + x) * size, size)


def walk(groups, size):
    for g, offsets in enumerate(groups):
        at = 0
        for dc in range(2):
            for dz in offsets:
                for dx in range(SIDE):
                    yield g, at, dz, dc, dx
                    at += size


def pack_kernel(groups, size, place, *refs):
    stats, (message, ordered) = refs[: len(groups)], refs[len(groups) :]
    for g, at, dz, dc, dx in walk(groups, size):
        ordered[pl.ds(at_owner(place, dz, dc, dx, size), size), :] = stats[g][pl.ds(at, size), :]
    message[...] = jnp.transpose(ordered[...])[:8]


def pack(place, stats, groups, size, after=()):
    rows = sum(s.shape[0] for s in stats)
    return launch(
        functools.partial(pack_kernel, groups, size),
        (place, *stats,),
        after,
        out_shape=shape(8, rows),
        in_specs=[SMEM] + [VMEM] * len(stats),
        out_specs=VMEM,
        scratch_shapes=[pltpu.VMEM((rows, TAIL), F32)],
        cost_estimate=cost(rows * TAIL, rows * TAIL * 4),
        name="pack_statistics",
    )


def merged(stats):
    tops = [x[:1] for x in stats]
    top = functools.reduce(jnp.maximum, tops)
    totals = [x[1:2] * jnp.exp(t - top) for x, t in zip(stats, tops)]
    picks = [x[2:3] for x in stats]
    if len(stats) == 4:
        totals, picks = ([x[0] + x[2], x[1] + x[3]] for x in (totals, picks))
    return top, totals[0] + totals[1], picks[0] + picks[1]


def merge_kernel(*refs):
    top, total, pick = merged([ref[...] for ref in refs[:-1]])
    row = lax.broadcasted_iota(jnp.int32, refs[-1].shape, 0)
    refs[-1][...] = jnp.where(row == 0, top, jnp.where(row == 1, total, pick))


def merge(stats, after=()):
    return launch(
        merge_kernel,
        (*stats,),
        after,
        out_shape=shape(*stats[0].shape),
        in_specs=[VMEM] * len(stats),
        out_specs=VMEM,
        cost_estimate=cost(64 * stats[0].size, 32 * stats[0].size),
        name="merge_statistics",
    )


def combine_kernel(offsets, size, count, place, weight, *refs):
    parts, (stats, message, ordered, scale) = refs[:count], refs[count:]
    top, total, pick = merged([ref[...] for ref in parts])
    log_total = top + jnp.log(total)
    loss = weight[0] * jnp.sum(log_total - pick, axis=1, keepdims=True)
    ordered[...] = jnp.transpose(jnp.broadcast_to(log_total, (TAIL, log_total.shape[1])))
    for _, at, dz, dc, dx in walk((offsets,), size):
        rows = ordered[pl.ds(at_owner(place, dz, dc, dx, size), size), :]
        scale[pl.ds(at, size), :] = weight[0] * jnp.exp(stats[pl.ds(at, size), :1] - rows)
    scales = jnp.transpose(scale[...])[:8]
    row = lax.broadcasted_iota(jnp.int32, scales.shape, 0)
    message[...] = jnp.where(row == 0, scales, jnp.where(row == 1, weight[0], loss))


def combine(place, weight, parts, stats, offsets, size, after=()):
    rows = stats.shape[0]
    return launch(
        functools.partial(combine_kernel, offsets, size, len(parts)),
        (place, weight, *parts, stats),
        after,
        out_shape=shape(8, rows),
        in_specs=[SMEM, SMEM] + [VMEM] * (len(parts) + 1),
        out_specs=VMEM,
        scratch_shapes=[pltpu.VMEM((rows, TAIL), F32)] * 2,
        cost_estimate=cost(rows * TAIL, rows * TAIL * 4),
        name="combine_statistics",
    )


def halves_kernel(below, above, first, last):
    first[...] = below[0]
    last[...] = above[1]


def halves(below, above, after=()):
    out = shape(*below.shape[1:], dtype=below.dtype)
    return launch(
        halves_kernel,
        (below, above),
        after,
        out_shape=[out] * 2,
        in_specs=[VMEM] * 2,
        out_specs=[VMEM] * 2,
        cost_estimate=cost(0, 4 * below.size),
        name="halves",
    )


def dlogit_kernel(dc, place, *refs):
    scales, (own, above, far, below), digits, out = refs[:SIDE], refs[SIDE : 2 * SIDE], refs[2 * SIDE : -1], refs[-1]
    half, columns = far.shape
    for ds in range(SIDE):
        scale = jnp.transpose(jnp.broadcast_to(scales[ds][:1], (TAIL, 2 * half)))
        weight = scales[ds][1:2, :1]
        at = 0
        for digit in digits:
            span = digit.shape[1]
            exp = far[pl.ds(at, span), :] if ds == 2 else (own, above, None, below)[ds][0, pl.ds(at, span), :]
            hit = onehot_of(place, digit[ds], columns)
            factor = scale[dc * half + at : dc * half + at + span, :1]
            grad = exp.astype(F32) * factor - jnp.where(hit, weight, 0.0)
            out[ds, pl.ds(at, span), :] = grad.astype(BF16)
            at += span


def dlogit_of(dc, place, scales, own, above, far, below, pieces, after=()):
    half, columns = far.shape
    at = pieces[0].shape[2] // TAIL - 1
    one = pl.BlockSpec((1, half, columns), lambda j: (dc, 0, 0))
    return launch(
        functools.partial(dlogit_kernel, dc),
        (place, *scales, own, above, far, below, *pieces),
        after,
        grid=(1,),
        out_shape=shape(SIDE, half, columns, dtype=BF16),
        in_specs=[SMEM]
        + [pl.BlockSpec(scales[0].shape, lambda j: (0, 0))] * SIDE
        + [one, one, pl.BlockSpec((half, columns), lambda j: (0, 0)), one]
        + [pl.BlockSpec((SIDE, p.shape[1], TAIL), lambda j: (0, 0, at)) for p in pieces],
        out_specs=pl.BlockSpec((SIDE, half, columns), lambda j: (0, 0, 0)),
        cost_estimate=cost(40 * half * columns, 16 * half * columns),
        name="dlogit",
    )


def dnormed_kernel(first, count, left, right, head, other, *refs):
    normed, outs, gain = refs[: -1 - count], refs[-1 - count : -1], refs[-1]
    columns = head.shape[1]
    dims = (((1,), (1,)), ((), ()))
    cut = pl.ds(pl.multiple_of(pl.program_id(0) * TILE, TILE), TILE)
    span = outs[0].shape[1]
    rows = pl.ds(first, count * span)
    part = lax.dot_general(left[:, rows, :].reshape(-1, columns), head[cut, :], dims, preferred_element_type=F32)
    part = part + lax.dot_general(
        right[:, rows, :].reshape(-1, columns), other[cut, :], dims, preferred_element_type=F32
    )
    x = jnp.concatenate([n[...] for n in normed], axis=1).reshape(part.shape).astype(F32)
    gain[...] = jnp.sum((part * x).reshape(-1, 8, TILE), axis=0)
    part = part.reshape(SIDE, count, -1, TILE)
    for k in range(count):
        outs[k][...] = part[:, k].astype(outs[k].dtype)


def dnormed_of(first, left, right, head, other, normed, span, dtype, after=()):
    depth, columns = head.shape
    count = sum(n.shape[1] for n in normed) // span
    block = pl.BlockSpec((SIDE, span, TILE), lambda j: (0, 0, j))
    return launch(
        functools.partial(dnormed_kernel, first, count),
        (left, right, in_vmem(head), in_vmem(other), *normed),
        after,
        grid=(depth // TILE,),
        out_shape=[shape(SIDE, span, depth, dtype=dtype)] * count + [shape(8, depth)],
        in_specs=[VMEM] * 4 + [pl.BlockSpec((SIDE, n.shape[1], TILE), lambda j: (0, 0, j)) for n in normed],
        out_specs=[block] * count + [pl.BlockSpec((8, TILE), lambda j: (0, j))],
        cost_estimate=cost(0, 4 * depth * columns),
        name="dnormed",
    )


def head_grad_kernel(count, *refs):
    pieces, (ours, others) = refs[:count], refs[count : count + 2]
    out, token, grads, sems = refs[-4:]
    token[...] = jnp.zeros_like(token)

    @pl.when(pl.program_id(0) == 0)
    def _():
        copies = [(ours, grads.at[:, 0]), (others, grads.at[:, 1])]
        copies = [pltpu.make_async_copy(a, b, sems.at[i]) for i, (a, b) in enumerate(copies)]
        for copy in copies:
            copy.start()
        for copy in copies:
            copy.wait()

    x = jnp.concatenate([piece[...] for piece in pieces], axis=1).reshape(-1, TILE)
    y = grads[...].reshape(x.shape[0], -1)
    out[...] = lax.dot_general(x, y, (((0,), (0,)), ((), ())), preferred_element_type=F32).astype(BF16)


def head_grad_of(pieces, ours, others, depth, start, stop, into=None, after=()):
    columns, rows = ours.shape[2], 2 * SIDE * ours.shape[1]
    inputs = [in_hbm(x) for x in (*pieces, ours, others)]
    specs = [pl.BlockSpec((SIDE, p.shape[1], TILE), lambda j: (0, 0, start + j)) for p in pieces] + [ANY] * 2
    aliases = {}
    if into is not None:
        aliases = {len(inputs): 0}
        inputs.append(in_hbm(into))
        specs.append(ANY)
    return launch(
        functools.partial(head_grad_kernel, len(pieces)),
        (*inputs,),
        after,
        grid=(stop - start,),
        input_output_aliases=aliases,
        out_shape=[shape(depth, columns, dtype=BF16), shape(8, TAIL)],
        in_specs=specs,
        out_specs=[pl.BlockSpec((TILE, columns), lambda j: (start + j, 0)), pl.BlockSpec((8, TAIL), lambda j: (0, 0))],
        scratch_shapes=[pltpu.VMEM((SIDE, 2, *ours.shape[1:]), BF16), pltpu.SemaphoreType.DMA((2,))],
        cost_estimate=cost(2 * rows * (stop - start) * TILE * columns, depth * columns + 4 * rows * depth),
        name="head_grad",
    )


def spread_kernel(near, own, out):
    gain = jnp.sum(near[...] + own[...], axis=0, keepdims=True)
    wide = out.shape[2]
    gain = jnp.concatenate([gain[:, i * wide : (i + 1) * wide] for i in range(out.shape[1])], axis=0)
    out[...] = jnp.broadcast_to(gain, out.shape)


def spread(near, own, after=()):
    rows, depth = near.shape
    return launch(
        spread_kernel,
        (near, own),
        after,
        out_shape=shape(8 * SIDE, rows, depth // rows),
        in_specs=[VMEM] * 2,
        out_specs=VMEM,
        cost_estimate=cost(rows * depth, 4 * 8 * SIDE * depth),
        name="gain_parts",
    )


def to_x_kernel(own, far, up, down, block, *messages):
    total = (own[...] + far[...].astype(F32)) + (up[...].astype(F32) + down[...].astype(F32))
    rows = own.shape[1] // SIDE
    for dx in range(SIDE):
        cut = jnp.concatenate([total[ds, dx * rows : (dx + 1) * rows] for ds in range(SIDE)], axis=0)
        if dx == 0:
            block[...] = cut
        else:
            messages[dx - 1][...] = cut.astype(BF16)


def to_x(own, far, up, down, after=()):
    _, span, depth = own.shape
    return launch(
        to_x_kernel,
        (own, far, up, down),
        after,
        out_shape=[shape(span, depth)] + [shape(span, depth, dtype=BF16)] * 3,
        in_specs=[VMEM] * 4,
        out_specs=[VMEM] * 4,
        cost_estimate=cost(8 * span * depth, 48 * span * depth),
        name="over_x",
    )


def to_y_kernel(place, block, up, far, down, gains, loss, message):
    span, depth = block.shape
    total = (block[...] + far[...].astype(F32)) + (up[...].astype(F32) + down[...].astype(F32))
    gain = jnp.sum(gains[...], axis=0)
    gain = jnp.concatenate([gain[i : i + 1] for i in range(gain.shape[0])], axis=1)
    rows = span // SIDE
    row = lax.broadcasted_iota(jnp.int32, (rows, depth), 0)
    extra = jnp.where(row == 0, gain, jnp.where(row == 1, loss[2:3, :1], 0.0))
    for ds in range(SIDE):
        filled = jnp.concatenate([total[ds * rows : (ds + 1) * rows], extra], axis=0)
        message[lax.rem(place[0] + ds, SIDE)] = filled


def to_y(place, block, up, far, down, gains, loss, after=()):
    span, depth = block.shape
    return launch(
        to_y_kernel,
        (place, block, up, far, down, gains, loss),
        after,
        out_shape=shape(SIDE, 2 * span // SIDE, depth),
        in_specs=[SMEM] + [VMEM] * 6,
        out_specs=VMEM,
        cost_estimate=cost(8 * span * depth, 16 * span * depth),
        name="over_y",
    )


def finish_kernel(hidden, gain, message, out, gain_out, loss_out, dnormed):
    rows, width = hidden.shape
    depth = width // SIDE
    for s in range(SIDE):
        cut = pl.ds(s * depth, depth)
        dnormed[:, cut] = message[s, :rows]
        gain_out[:, cut] = message[s, rows : rows + 1] / gain[:, cut]
    loss = message[:, rows + 1, :TAIL]
    loss_out[...] = jnp.sum(loss, axis=0, keepdims=True)
    values = hidden[...].astype(F32)
    inverse = lax.rsqrt(jnp.mean(values * values, axis=1, keepdims=True) + EPS)
    gained = dnormed[...] * gain[...]
    inner = jnp.mean(gained * values, axis=1, keepdims=True)
    out[...] = (inverse * gained - values * (inverse * inverse * inverse) * inner).astype(BF16)


def finish(hidden, gain, message, after=()):
    rows, width = hidden.shape
    return launch(
        finish_kernel,
        (hidden, gain, message),
        after,
        out_shape=[shape(rows, width, dtype=BF16), shape(1, width), shape(1, TAIL)],
        in_specs=[VMEM] * 3,
        out_specs=[VMEM] * 3,
        scratch_shapes=[pltpu.VMEM((rows, width), F32)],
        cost_estimate=cost(12 * rows * width, 16 * rows * width),
        name="finish",
    )


def section_weights(exit_layer, numerators):
    layers = numerators.shape[0]
    matches = exit_layer[:, None] == jnp.arange(layers, dtype=jnp.int32)[None, :]
    picked = jnp.sum(jnp.where(matches, numerators[None, :], 0), axis=1).astype(F32)
    return picked / jnp.sum(picked)


def local(hidden_rows, norm_gain, head_weight, targets, exit_layer, numerators):
    section, piece = lax.axis_index("section"), lax.axis_index("vocab")
    own_rows, width = hidden_rows.shape
    depth, columns = head_weight.shape
    place = jnp.stack([section, piece // 8, (piece // 2) % SIDE, piece % 2, piece * columns]).astype(jnp.int32)
    gain_row = norm_gain.reshape(1, width)
    weights = section_weights(exit_layer, numerators)
    weight = jnp.sum(jnp.where(jnp.arange(SIDE) == section, weights, 0.0)).reshape(1)

    cuts = normalise(place, hidden_rows, gain_row, targets, (weight,))
    own = jnp.stack([cuts[0], over_section(cuts[3], -1), over_section(cuts[2], 2), over_section(cuts[1], 1)])
    def along_x(x):
        return [x, over_vocab(x, dx=-1), over_vocab(x, dx=2), over_vocab(x, dx=1)]

    pair = jnp.stack([over_vocab(own, dz=-1), over_vocab(own, dz=1)], axis=1)
    mine = [jnp.concatenate(along_x(own), axis=1)]
    mine.append(jnp.stack(along_x(pair), axis=2).reshape(SIDE, -1, own.shape[2]))
    mine.append(over_vocab(mine[0], dz=2))
    theirs = [over_vocab(m, dc=1) for m in mine]
    pieces = (*mine, *theirs)
    groups = ((0,), (1, 3), (2,))
    everything = (sum(groups, ()),)

    held_head = hold(head_weight, (own,))
    up, down = logits_of((2,), pieces, held_head)
    head_ready, _ = lax.optimization_barrier((head_weight, up))
    other_head = over_vocab(head_ready, dc=1)
    first, last = logits_of((1, 3), pieces, held_head, (up,))
    up, down = over_section(up, 1), over_section(down, -1)
    first, last = pass_on(first, last, up, down)
    (kept,) = logits_of((0,), pieces, held_head, (first,))
    held_other = hold(other_head, (kept,))
    below, above = over_section(first, 1), over_section(last, -1)
    exps, stats = own_logits(place, kept, below, above, mine, theirs)

    below, above = over_section(exps, 1), over_section(exps, -1)
    parts = pack(place, [stats], everything, own_rows, (held_other,))
    parts = merge([parts, over_vocab(parts, dc=1)])
    parts = merge(along_x(parts))
    far_first, far_last = halves(below, above, (parts,))
    far_first, far_last = over_section(far_first, 1), over_section(far_last, -1)
    parts = [parts, over_vocab(parts, dz=-1), over_vocab(parts, dz=2), over_vocab(parts, dz=1)]
    scales = combine(place, weight, parts, stats, everything[0], own_rows)
    loss = scales
    scales = [scales, over_section(scales, -1), over_section(scales, 2), over_section(scales, 1)]

    others = dlogit_of(1, place, scales, exps, above, far_last, below, theirs, (far_first,))
    swapped = over_vocab(others, dc=1)
    ours = dlogit_of(0, place, scales, exps, above, far_first, below, mine, (others,))
    span = mine[0].shape[1]
    to_up, to_down, to_far, gain_near = dnormed_of(
        span, ours, swapped, held_head, held_other, mine[1:], span, BF16
    )
    moved = [over_vocab(to_far, dz=2), over_vocab(to_up, dz=1), over_vocab(to_down, dz=-1)]
    kept, gain_own = dnormed_of(0, ours, swapped, held_head, held_other, mine[:1], span, F32, (gain_near,))

    gains = lax.all_to_all(spread(gain_near, gain_own), "vocab", 0, 0)
    tiles = depth // TILE
    grad, token = head_grad_of(pieces, ours, others, depth, 0, tiles // 2, None, (gain_own,))
    block, *cuts = to_x(kept, *moved, (token,))
    cuts = [over_vocab(cuts[0], dx=1), over_vocab(cuts[1], dx=2), over_vocab(cuts[2], dx=-1)]
    grad, token = head_grad_of(pieces, ours, others, depth, tiles // 2, 3 * tiles // 4, grad, (block,))
    message = to_y(place, block, *cuts, gains, loss, (token,))
    got = lax.all_to_all(message, "section", 0, 0)
    head_grad, token = head_grad_of(pieces, ours, others, depth, 3 * tiles // 4, tiles, grad, (message,))
    hidden_grad, gain_grad, total_loss = finish(hidden_rows, gain_row, got, (token,))
    return (hidden_grad, gain_grad.reshape(width), head_grad, total_loss[0, 0])


def solution(mesh):
    return jax.shard_map(
        local,
        mesh=mesh,
        in_specs=(
            P(("section", "vocab"), None),
            P(),
            P("section", "vocab"),
            P(("section", "vocab")),
            P(),
            P(),
        ),
        out_specs=(P(("section", "vocab"), None), P(), P("section", "vocab"), P()),
        check_vma=False,
    )
```

time: 580 us -> 220 us (0.38)
  blocking collectives: 275 us -> 0 us
  waiting for transfers between devices: 225 us -> 71.1 us
  Pallas kernels: 0 us -> 78.2 us
  starting transfers between devices: 4.38 us -> 63.4 us
  matrix products: 46.5 us -> 0 us
  between operations: 13.9 us -> 1.11 us
  other arithmetic: 13.7 us -> 3.12 us
    psum x2 -> x0, blocking collectives: 129 us -> none  [the longest x1 65.3 us: local(): gain_grad = lax.psum(gain_part, ('section', 'vocab'))]
    psum x1 -> x0, waiting for transfers between devices: 90.1 us -> none  [local(): lax.psum(jnp.dot(columns, head_weight, preferred_element_type=jnp.float32...]
    reduce_scatter x1 -> x0, waiting for transfers between devices: 87.8 us -> none  [local(): lax.psum_scatter(lax.dot_general(dlogit, head_weight, (((1,), (1,)), ((),...]
    pallas_call x0 -> x24, Pallas kernels: none -> 78.2 us  [launch(): pl.pallas_call(body, in_specs=[*in_specs, *[ANY] * ignored], scratch_shap...]
    ppermute x0 -> x41, waiting for transfers between devices: none -> 68.8 us  [the longest x14 42 us: over_section(): lax.ppermute(x, 'section', [(i, (i + step) % SIDE) for i in range(SIDE)])]
    unnamed x1 -> x0, blocking collectives: 68.2 us -> none
    pmax x1 -> x0, blocking collectives: 67.2 us -> none  [row_statistics(): row_max = lax.pmax(local_max, 'vocab')]
    ppermute x0 -> x41, starting transfers between devices: none -> 54.1 us  [the longest x27 33.2 us: over_vocab(): return lax.ppermute(x, 'vocab', pairs)]
  transfers between devices with their start and end apart: 4 -> 43, of which waited for: 3 -> 25; matrix products, arithmetic and copies ran while one was open for 3% -> 0% of each run, Pallas kernels for 0% -> 27%
where the time goes in v1:
time: 220 us
  Pallas kernels  78.2 us (36%)
  waiting for transfers between devices  71.1 us (32%)
  starting transfers between devices  63.4 us (29%)
  other arithmetic  3.12 us (1%)
  local copies, waits for them, and re-layouts  2.55 us (1%)
    pallas_call x24, Pallas kernels, launch(): pl.pallas_call(body, in_specs=[*in_specs, *[ANY] * ignored], scratch_shap...  78.2 us
    ppermute x14, waiting for transfers between devices, over_section(): lax.ppermute(x, 'section', [(i, (i + step) % SIDE) for i in range(SIDE)])  42 us
    ppermute x27, starting transfers between devices, over_vocab(): return lax.ppermute(x, 'vocab', pairs)  33.2 us
    ppermute x27, waiting for transfers between devices, over_vocab(): return lax.ppermute(x, 'vocab', pairs)  26.9 us
    ppermute x14, starting transfers between devices, over_section(): lax.ppermute(x, 'section', [(i, (i + step) % SIDE) for i in range(SIDE)])  20.9 us
    all_to_all x1, starting transfers between devices, local(): gains = lax.all_to_all(spread(gain_near, gain_own), 'vocab', 0, 0)  5.91 us
  transfers between devices with their start and end apart: 43, of which 25 were waited for; matrix products, arithmetic and copies ran while one was open for 0% of the time, Pallas kernels for 27%

profile of v1, /device:TPU:0, one launch (start us, length us, event | category | flops | bytes accessed | tf_op | source)
XLA Modules:
  0.0 219.5 jit_solution(17756596114261828133)
XLA Ops:
  7.3 1.7 collective-permute-start.2
  9.0 2.9 %collective-permute-start.1 = (bf16[8,2176]{1,0:T(8,128)(2,1)S(1)}, bf16[8,2176]{1,0:T(8,128)(2,1)S(1)}, u32[]{:S(2)}, u32[]{:S(2)}) collective-permute-start(bf16[8,2176]{1,0:T(8,128)(2,1)S(1)} %get-tuple-element.40), channel_id=1, source_target_pairs={{0,64},{32,96},{64,0},{96,32},{1,65},{33,97},{65,1},{97,33},{2,66}... | collective-permute-start | bytes 104456 | tf_op jit(solution)/shard_map/ppermute | solution.py:22
  15.9 2.0 collective-permute-start.7
  17.8 2.2 %collective-permute-start.6 = (bf16[4,8,2176]{2,1,0:T(8,128)(2,1)S(1)}, bf16[4,8,2176]{2,1,0:T(8,128)(2,1)S(1)}, u32[]{:S(2)}, u32[]{:S(2)}) collective-permute-start(bf16[4,8,2176]{2,1,0:T(8,128)(2,1)S(1)} %pad_maximum_fusion.3.refs_1_), channel_id=1, source_target_pairs={{0,6},{1,7},{2,0},{3,1},{4,2},{5,3},{6,4},{7,5},{8,14},{9,15},{10,... | collective-permute-start | bytes 417800 | tf_op jit(solution)/shard_map/ppermute | solution.py:32
  20.1 1.5 collective-permute-start.5
  21.5 2.7 %collective-permute-start.4 = (bf16[4,8,2176]{2,1,0:T(8,128)(2,1)S(1)}, bf16[4,8,2176]{2,1,0:T(8,128)(2,1)S(1)}, u32[]{:S(2)}, u32[]{:S(2)}) collective-permute-start(bf16[4,8,2176]{2,1,0:T(8,128)(2,1)S(1)} %pad_maximum_fusion.3.refs_1_), channel_id=1, source_target_pairs={{0,16},{1,17},{2,18},{3,19},{4,20},{5,21},{6,22},{7,23},{8,24},{9,... | collective-permute-start | bytes 417800 | tf_op jit(solution)/shard_map/ppermute | solution.py:32
  27.9 1.5 collective-permute-start.8
  29.4 2.4 %collective-permute-done.4 = bf16[4,8,2176]{2,1,0:T(8,128)(2,1)S(1)} collective-permute-done((bf16[4,8,2176]{2,1,0:T(8,128)(2,1)S(1)}, bf16[4,8,2176]{2,1,0:T(8,128)(2,1)S(1)}, u32[]{:S(2)}, u32[]{:S(2)}) %collective-permute-start.4) | collective-permute-done | bytes 139296 | tf_op jit(solution)/shard_map/ppermute | solution.py:32
  31.8 2.1 collective-permute-done.3
  34.7 3.1 %collective-permute-done.10 = bf16[4,2,8,2176]{3,2,0,1:T(8,128)(2,1)S(1)} collective-permute-done((bf16[4,2,8,2176]{3,2,0,1:T(8,128)(2,1)S(1)}, bf16[4,2,8,2176]{3,2,0,1:T(8,128)(2,1)S(1)}, u32[]{:S(2)}, u32[]{:S(2)}) %collective-permute-start.10) | collective-permute-done | bytes 278560 | tf_op jit(solution)/shard_map/ppermute | solution.py:32
  37.8 3.1 %collective-permute-done.9 = bf16[4,2,8,2176]{3,2,0,1:T(8,128)(2,1)S(1)} collective-permute-done((bf16[4,2,8,2176]{3,2,0,1:T(8,128)(2,1)S(1)}, bf16[4,2,8,2176]{3,2,0,1:T(8,128)(2,1)S(1)}, u32[]{:S(2)}, u32[]{:S(2)}) %collective-permute-start.9) | collective-permute-done | bytes 278560 | tf_op jit(solution)/shard_map/ppermute | solution.py:32
  41.8 3.3 %collective-permute-done.11.refs_2_.refs_6_.refs_11_.refs_5_ = bf16[4,32,2176]{2,1,0:T(8,128)(2,1)S(1)} collective-permute-done((bf16[4,32,2176]{2,1,0:T(8,128)(2,1)S(1)}, bf16[4,32,2176]{2,1,0:T(8,128)(2,1)S(1)}, u32[]{:S(2)}, u32[]{:S(2)}) %collective-permute-start.11) | collective-permute-done | bytes 557088 | tf_op jit(solution)/shard_map/ppermute | solution.py:32
  45.1 3.6 %hold_head.2.refs_6_.refs_2_ = bf16[2048,2048]{1,0:T(8,128)(2,1)S(1)} custom-call(bf16[2048,2048]{1,0:T(8,128)(2,1)} %refs_0_.2, bf16[4,8,2176]{2,1,0:T(8,128)(2,1)S(1)} %pad_maximum_fusion.3.refs_1_), custom_call_target="tpu_custom_call" | custom-call | bytes 8388608 | tf_op jit(solution)/shard_map/hold_head/pallas_call | solution.py:57
  48.8 4.5 %partial_logits.3 = (s16[128,2176]{1,0:T(8,128)(2,1)S(1)}, s16[128,2176]{1,0:T(8,128)(2,1)S(1)}) custom-call(bf16[4,32,2176]{2,1,0:T(8,128)(2,1)S(1)} %pad_maximum_fusion.1.refs_0_.refs_4_.refs_9_, bf16[4,64,2176]{2,1,0:T(8,128)(2,1)S(1)} %bitcast.23, bf16[4,32,2176]{2,1,0:T(8,128)(2,1)S(1)} %collective-permute-done.11.refs_2_.refs_6_.refs_11_.refs_5_, ...), custom_call_target="tpu_custom_call" | custom-call | bytes 10485760 | tf_op jit(solution)/shard_map/partial_logits/pallas_call | solution.py:57
  53.9 3.1 %collective-permute-start.16 = (s16[128,2176]{1,0:T(8,128)(2,1)S(1)}, s16[128,2176]{1,0:T(8,128)(2,1)S(1)}, u32[]{:S(2)}, u32[]{:S(2)}) collective-permute-start(s16[128,2176]{1,0:T(8,128)(2,1)S(1)} %get-tuple-element.45), channel_id=1, source_target_pairs={{0,96},{32,0},{64,32},{96,64},{1,97},{33,1},{65,33},{97,65},{2,98}... | collective-permute-start | bytes 1671176 | tf_op jit(solution)/shard_map/ppermute | solution.py:22
  57.0 6.7 %partial_logits.4 = (f32[256,2048]{1,0:T(8,128)S(1)}, f32[256,2048]{1,0:T(8,128)S(1)}) custom-call(bf16[4,32,2176]{2,1,0:T(8,128)(2,1)S(1)} %pad_maximum_fusion.1.refs_0_.refs_4_.refs_9_, bf16[4,64,2176]{2,1,0:T(8,128)(2,1)S(1)} %bitcast.24, bf16[4,32,2176]{2,1,0:T(8,128)(2,1)S(1)} %collective-permute-done.11.refs_2_.refs_6_.refs_11_.refs_5_, ...), custom_call_target="tpu_custom_call" | custom-call | bytes 12582912 | tf_op jit(solution)/shard_map/partial_logits/pallas_call | solution.py:57
  63.6 6.0 %collective-permute-done.15.refs_2_ = s16[128,2176]{1,0:T(8,128)(2,1)S(1)} collective-permute-done((s16[128,2176]{1,0:T(8,128)(2,1)S(1)}, s16[128,2176]{1,0:T(8,128)(2,1)S(1)}, u32[]{:S(2)}, u32[]{:S(2)}) %collective-permute-start.15) | collective-permute-done | bytes 557088 | tf_op jit(solution)/shard_map/ppermute | solution.py:22
  71.0 3.0 %collective-permute-start.18 = (s16[256,2176]{1,0:T(8,128)(2,1)S(1)}, s16[256,2176]{1,0:T(8,128)(2,1)S(1)}, u32[]{:S(2)}, u32[]{:S(2)}) collective-permute-start(s16[256,2176]{1,0:T(8,128)(2,1)S(1)} %get-tuple-element.47), channel_id=1, source_target_pairs={{0,96},{32,0},{64,32},{96,64},{1,97},{33,1},{65,33},{97,65},{2,98}... | collective-permute-start | bytes 3342344 | tf_op jit(solution)/shard_map/ppermute | solution.py:22
  74.0 4.1 %partial_logits.5.refs_1_ = f32[256,2048]{1,0:T(8,128)S(1)} custom-call(bf16[4,32,2176]{2,1,0:T(8,128)(2,1)S(1)} %pad_maximum_fusion.1.refs_0_.refs_4_.refs_9_, bf16[4,64,2176]{2,1,0:T(8,128)(2,1)S(1)} %bitcast.25, bf16[4,32,2176]{2,1,0:T(8,128)(2,1)S(1)} %collective-permute-done.11.refs_2_.refs_6_.refs_11_.refs_5_, ...), custom_call_target="tpu_custom_call" | custom-call | bytes 10485760 | tf_op jit(solution)/shard_map/partial_logits/pallas_call | solution.py:57
  78.2 19.7 %collective-permute-done.17.refs_2_ = s16[256,2176]{1,0:T(8,128)(2,1)S(1)} collective-permute-done((s16[256,2176]{1,0:T(8,128)(2,1)S(1)}, s16[256,2176]{1,0:T(8,128)(2,1)S(1)}, u32[]{:S(2)}, u32[]{:S(2)}) %collective-permute-start.17) | collective-permute-done | bytes 1114144 | tf_op jit(solution)/shard_map/ppermute | solution.py:22
  97.9 2.5 %own_logits.1 = (bf16[2,128,2048]{2,1,0:T(8,128)(2,1)S(1)}, f32[256,128]{1,0:T(8,128)S(1)}) custom-call(s32[5]{0:T(128)S(1)} %stack.62.refs_0_, f32[256,2048]{1,0:T(8,128)S(1)} %partial_logits.5.refs_1_, s16[256,2176]{1,0:T(8,128)(2,1)S(1)} %collective-permute-done.17.refs_2_, s16[256,2176]{1,0:T(8,128)(2,1)S(1)} %collective-permute-done.18.refs_3_, ...), custom_call_target="tpu_custom_call" | custom-call | flops 10485760 | bytes 6291456 | tf_op jit(solution)/shard_map/own_logits/pallas_call | solution.py:57
  100.4 3.0 %collective-permute-start.30 = (bf16[2,128,2048]{2,1,0:T(8,128)(2,1)S(1)}, bf16[2,128,2048]{2,1,0:T(8,128)(2,1)S(1)}, u32[]{:S(2)}, u32[]{:S(2)}) collective-permute-start(bf16[2,128,2048]{2,1,0:T(8,128)(2,1)S(1)} %get-tuple-element.50.refs_5_), channel_id=1, source_target_pairs={{0,96},{32,0},{64,32},{96,64},{1,97},{33,1},{65,33},{97,65},{2,98}... | collective-permute-start | bytes 3145736 | tf_op jit(solution)/shard_map/ppermute | solution.py:22
  103.4 3.4 %hold_head.3.refs_2_.refs_3_ = bf16[2048,2048]{1,0:T(8,128)(2,1)S(1)} custom-call(bf16[2048,2048]{1,0:T(8,128)(2,1)} %collective-permute-done.19.refs_0_, f32[256,2048]{1,0:T(8,128)S(1)} %partial_logits.5.refs_1_), custom_call_target="tpu_custom_call" | custom-call | bytes 8388608 | tf_op jit(solution)/shard_map/hold_head/pallas_call | solution.py:57
  108.7 4.3 %collective-permute-start.21 = (f32[8,256]{1,0:T(8,128)S(1)}, f32[8,256]{1,0:T(8,128)S(1)}, u32[]{:S(2)}, u32[]{:S(2)}) collective-permute-start(f32[8,256]{1,0:T(8,128)S(1)} %merge_statistics.2.refs_0_), channel_id=1, source_target_pairs={{0,24},{1,25},{2,26},{3,27},{4,28},{5,29},{6,30},{7,31},{8,0},{9,1... | collective-permute-start | bytes 24584 | tf_op jit(solution)/shard_map/ppermute | solution.py:32
  114.4 3.8 %collective-permute-done.22.refs_2_ = f32[8,256]{1,0:T(8,128)S(1)} collective-permute-done((f32[8,256]{1,0:T(8,128)S(1)}, f32[8,256]{1,0:T(8,128)S(1)}, u32[]{:S(2)}, u32[]{:S(2)}) %collective-permute-start.22) | collective-permute-done | bytes 8224 | tf_op jit(solution)/shard_map/ppermute | solution.py:32
  118.2 6.0 %collective-permute-done.30.refs_1_.refs_6_ = bf16[2,128,2048]{2,1,0:T(8,128)(2,1)S(1)} collective-permute-done((bf16[2,128,2048]{2,1,0:T(8,128)(2,1)S(1)}, bf16[2,128,2048]{2,1,0:T(8,128)(2,1)S(1)}, u32[]{:S(2)}, u32[]{:S(2)}) %collective-permute-start.30) | collective-permute-done | bytes 1048608 | tf_op jit(solution)/shard_map/ppermute | solution.py:22
  124.2 3.4 %collective-permute-done.31.refs_0_.refs_8_ = bf16[2,128,2048]{2,1,0:T(8,128)(2,1)S(1)} collective-permute-done((bf16[2,128,2048]{2,1,0:T(8,128)(2,1)S(1)}, bf16[2,128,2048]{2,1,0:T(8,128)(2,1)S(1)}, u32[]{:S(2)}, u32[]{:S(2)}) %collective-permute-start.31) | collective-permute-done | bytes 1048608 | tf_op jit(solution)/shard_map/ppermute | solution.py:22
  127.7 3.2 %collective-permute-start.33 = (bf16[128,2048]{1,0:T(8,128)(2,1)S(1)}, bf16[128,2048]{1,0:T(8,128)(2,1)S(1)}, u32[]{:S(2)}, u32[]{:S(2)}) collective-permute-start(bf16[128,2048]{1,0:T(8,128)(2,1)S(1)} %get-tuple-element.52), channel_id=1, source_target_pairs={{0,96},{32,0},{64,32},{96,64},{1,97},{33,1},{65,33},{97,65},{2,98}... | collective-permute-start | bytes 1572872 | tf_op jit(solution)/shard_map/ppermute | solution.py:22
  133.2 1.4 collective-permute-done.24.refs_3_
  134.6 2.6 %collective-permute-done.25.refs_4_ = f32[8,256]{1,0:T(8,128)S(1)} collective-permute-done((f32[8,256]{1,0:T(8,128)S(1)}, f32[8,256]{1,0:T(8,128)S(1)}, u32[]{:S(2)}, u32[]{:S(2)}) %collective-permute-start.25) | collective-permute-done | bytes 8224 | tf_op jit(solution)/shard_map/ppermute | solution.py:32
  140.8 1.6 collective-permute-done.27.refs_2_
  142.4 1.6 collective-permute-done.28.refs_3_
  145.1 2.1 dlogit.2.refs_12_.refs_7_
  147.4 2.1 dlogit.3.refs_0_.refs_6_
  149.5 2.0 collective-permute-done.34.refs_1_
  151.5 9.6 %dnormed.2 = (bf16[4,32,2048]{2,1,0:T(8,128)(2,1)}, bf16[4,32,2048]{2,1,0:T(8,128)(2,1)}, bf16[4,32,2048]{2,1,0:T(8,128)(2,1)}, f32[8,2048]{1,0:T(8,128)S(1)}) custom-call(bf16[4,128,2048]{2,1,0:T(8,128)(2,1)S(1)} %dlogit.3.refs_0_.refs_6_, bf16[4,128,2048]{2,1,0:T(8,128)(2,1)S(1)} %collective-permute-done.34.refs_1_, ...), custom_call_target="tpu_custom_call" | custom-call | bytes 16777216 | tf_op jit(solution)/shard_map/dnormed/pallas_call | solution.py:57
  161.1 1.9 collective-permute-start.35
  163.9 2.3 %collective-permute-start.37 = (bf16[4,32,2048]{2,1,0:T(8,128)(2,1)}, bf16[4,32,2048]{2,1,0:T(8,128)(2,1)}, u32[]{:S(2)}, u32[]{:S(2)}) collective-permute-start(bf16[4,32,2048]{2,1,0:T(8,128)(2,1)} %get-tuple-element.57), channel_id=1, source_target_pairs={{0,6},{1,7},{2,0},{3,1},{4,2},{5,3},{6,4},{7,5},{8,14},{9,15},{10,... | collective-permute-start | bytes 1572872 | tf_op jit(solution)/shard_map/ppermute | solution.py:32
  166.3 7.0 %dnormed.3 = (f32[4,32,2048]{2,1,0:T(8,128)S(1)}, f32[8,2048]{1,0:T(8,128)S(1)}) custom-call(bf16[4,128,2048]{2,1,0:T(8,128)(2,1)S(1)} %dlogit.3.refs_0_.refs_6_, bf16[4,128,2048]{2,1,0:T(8,128)(2,1)S(1)} %collective-permute-done.34.refs_1_, bf16[2048,2048]{1,0:T(8,128)(2,1)S(1)} %hold_head.2.refs_6_.refs_2_, ...), custom_call_target="tpu_custom_call" | custom-call | bytes 16777216 | tf_op jit(solution)/shard_map/dnormed/pallas_call | solution.py:57
  174.0 5.9 %all-to-all-start = ((f32[32,8,256]{2,1,0:T(8,128)}), f32[32,8,256]{2,1,0:T(8,128)S(1)}, u32[]{:S(2)}, u32[]{:S(2)}) async-start(f32[32,8,256]{2,1,0:T(8,128)} %gain_parts.1), calls=%async_computation | async-start | bytes 524288 | tf_op jit(solution)/shard_map/all_to_all | solution.py:677
  179.9 9.7 %head_grad.3 = (bf16[2048,2048]{1,0:T(8,128)(2,1)}, f32[8,128]{1,0:T(8,128)S(1)}) custom-call(bf16[4,32,2176]{2,1,0:T(8,128)(2,1)} %copy-done.3, bf16[4,64,2176]{2,1,0:T(8,128)(2,1)} %bitcast.29, bf16[4,32,2176]{2,1,0:T(8,128)(2,1)} %copy-done.4, bf16[4,32,2176]{2,1,0:T(8,128)(2,1)} %copy-done.6, bf16[4,64,2176]{2,1,0:T(8,128)(2,1)} %copy-done.1, ...), custom_call_target="tpu_custom_call" | custom-call | flops 4294967296 | bytes 12582912 | tf_op jit(solution)/shard_map/head_grad/pallas_call | solution.py:57
  191.6 2.5 %collective-permute-start.38 = (bf16[32,2048]{1,0:T(8,128)(2,1)S(1)}, bf16[32,2048]{1,0:T(8,128)(2,1)S(1)}, u32[]{:S(2)}, u32[]{:S(2)}) collective-permute-start(bf16[32,2048]{1,0:T(8,128)(2,1)S(1)} %get-tuple-element.61), channel_id=1, source_target_pairs={{0,8},{1,9},{2,10},{3,11},{4,12},{5,13},{6,14},{7,15},{8,16},{9,17... | collective-permute-start | bytes 393224 | tf_op jit(solution)/shard_map/ppermute | solution.py:32
  194.1 3.3 %collective-permute-start.39 = (bf16[32,2048]{1,0:T(8,128)(2,1)S(1)}, bf16[32,2048]{1,0:T(8,128)(2,1)S(1)}, u32[]{:S(2)}, u32[]{:S(2)}) collective-permute-start(bf16[32,2048]{1,0:T(8,128)(2,1)S(1)} %get-tuple-element.62), channel_id=1, source_target_pairs={{0,16},{1,17},{2,18},{3,19},{4,20},{5,21},{6,22},{7,23},{8,24},{9,... | collective-permute-start | bytes 393224 | tf_op jit(solution)/shard_map/ppermute | solution.py:32
  197.4 6.9 %head_grad.4 = (bf16[2048,2048]{1,0:T(8,128)(2,1)}, f32[8,128]{1,0:T(8,128)S(1)}) custom-call(bf16[4,32,2176]{2,1,0:T(8,128)(2,1)} %copy-done.3, bf16[4,64,2176]{2,1,0:T(8,128)(2,1)} %bitcast.30, bf16[4,32,2176]{2,1,0:T(8,128)(2,1)} %copy-done.4, bf16[4,32,2176]{2,1,0:T(8,128)(2,1)} %copy-done.6, ...), custom_call_target="tpu_custom_call", output_to_operand_aliasing={{0}: (8, {})} | custom-call | flops 2147483648 | bytes 12582912 | tf_op jit(solution)/shard_map/head_grad/pallas_call | solution.py:57
  204.4 1.5 over_y.1.refs_9_
  205.9 3.5 %all-to-all-start.1 = ((f32[4,16,2048]{2,1,0:T(8,128)}), f32[4,16,2048]{2,1,0:T(8,128)S(1)}, u32[]{:S(2)}, u32[]{:S(2)}) async-start(f32[4,16,2048]{2,1,0:T(8,128)} %over_y.1.refs_9_), calls=%async_computation.1 | async-start | bytes 1048576 | tf_op jit(solution)/shard_map/all_to_all | solution.py:684
  209.4 7.0 %head_grad.5 = (bf16[2048,2048]{1,0:T(8,128)(2,1)}, f32[8,128]{1,0:T(8,128)S(1)}) custom-call(bf16[4,32,2176]{2,1,0:T(8,128)(2,1)} %copy-done.3, bf16[4,64,2176]{2,1,0:T(8,128)(2,1)} %bitcast.31, bf16[4,32,2176]{2,1,0:T(8,128)(2,1)} %copy-done.4, bf16[4,32,2176]{2,1,0:T(8,128)(2,1)} %copy-done.6, ...), custom_call_target="tpu_custom_call", output_to_operand_aliasing={{0}: (8, {})} | custom-call | flops 2147483648 | bytes 12582912 | tf_op jit(solution)/shard_map/head_grad/pallas_call | solution.py:57
  216.4 2.2 %all-to-all-done.1.refs_2_ = f32[4,16,2048]{2,1,0:T(8,128)S(1)} async-done(((f32[4,16,2048]{2,1,0:T(8,128)}), f32[4,16,2048]{2,1,0:T(8,128)S(1)}, u32[]{:S(2)}, u32[]{:S(2)}) %all-to-all-start.1) | async-done | bytes 524320 | tf_op jit(solution)/shard_map/all_to_all | solution.py:684
  (102 shorter events, 32.6 us)
Async XLA Ops:
  7.3 6.0 %collective-permute-start.2 = (bf16[8,2176]{1,0:T(8,128)(2,1)S(1)}, bf16[8,2176]{1,0:T(8,128)(2,1)S(1)}, u32[]{:S(2)}, u32[]{:S(2)}) collective-permute-start(bf16[8,2176]{1,0:T(8,128)(2,1)S(1)} %get-tuple-element.41), channel_id=1, source_target_pairs={{0,32},{32,64},{64,96},{96,0},{1,33},{33,65},{65,97},{97,1},{2,34}... | collective-permute-start | bytes 104456 | tf_op jit(solution)/shard_map/ppermute | solution.py:22
  9.0 5.4 %collective-permute-start.1 = (bf16[8,2176]{1,0:T(8,128)(2,1)S(1)}, bf16[8,2176]{1,0:T(8,128)(2,1)S(1)}, u32[]{:S(2)}, u32[]{:S(2)}) collective-permute-start(bf16[8,2176]{1,0:T(8,128)(2,1)S(1)} %get-tuple-element.40), channel_id=1, source_target_pairs={{0,64},{32,96},{64,0},{96,32},{1,65},{33,97},{65,1},{97,33},{2,66}... | collective-permute-start | bytes 104456 | tf_op jit(solution)/shard_map/ppermute | solution.py:22
  11.9 3.9 %collective-permute-start = (bf16[8,2176]{1,0:T(8,128)(2,1)S(1)}, bf16[8,2176]{1,0:T(8,128)(2,1)S(1)}, u32[]{:S(2)}, u32[]{:S(2)}) collective-permute-start(bf16[8,2176]{1,0:T(8,128)(2,1)S(1)} %get-tuple-element.39), channel_id=1, source_target_pairs={{0,96},{32,0},{64,32},{96,64},{1,97},{33,1},{65,33},{97,65},{2,98}... | collective-permute-start | bytes 104456 | tf_op jit(solution)/shard_map/ppermute | solution.py:22
  15.9 9.8 %collective-permute-start.7 = (bf16[4,8,2176]{2,1,0:T(8,128)(2,1)S(1)}, bf16[4,8,2176]{2,1,0:T(8,128)(2,1)S(1)}, u32[]{:S(2)}, u32[]{:S(2)}) collective-permute-start(bf16[4,8,2176]{2,1,0:T(8,128)(2,1)S(1)} %pad_maximum_fusion.3.refs_1_), channel_id=1, source_target_pairs={{0,2},{1,3},{2,4},{3,5},{4,6},{5,7},{6,0},{7,1},{8,10},{9,11},{10,... | collective-permute-start | bytes 417800 | tf_op jit(solution)/shard_map/ppermute | solution.py:32
  17.8 7.9 %collective-permute-start.6 = (bf16[4,8,2176]{2,1,0:T(8,128)(2,1)S(1)}, bf16[4,8,2176]{2,1,0:T(8,128)(2,1)S(1)}, u32[]{:S(2)}, u32[]{:S(2)}) collective-permute-start(bf16[4,8,2176]{2,1,0:T(8,128)(2,1)S(1)} %pad_maximum_fusion.3.refs_1_), channel_id=1, source_target_pairs={{0,6},{1,7},{2,0},{3,1},{4,2},{5,3},{6,4},{7,5},{8,14},{9,15},{10,... | collective-permute-start | bytes 417800 | tf_op jit(solution)/shard_map/ppermute | solution.py:32
  20.1 7.9 %collective-permute-start.5 = (bf16[4,8,2176]{2,1,0:T(8,128)(2,1)S(1)}, bf16[4,8,2176]{2,1,0:T(8,128)(2,1)S(1)}, u32[]{:S(2)}, u32[]{:S(2)}) collective-permute-start(bf16[4,8,2176]{2,1,0:T(8,128)(2,1)S(1)} %pad_maximum_fusion.3.refs_1_), channel_id=1, source_target_pairs={{0,8},{1,9},{2,10},{3,11},{4,12},{5,13},{6,14},{7,15},{8,16},{9,17... | collective-permute-start | bytes 417800 | tf_op jit(solution)/shard_map/ppermute | solution.py:32
  21.5 10.3 %collective-permute-start.4 = (bf16[4,8,2176]{2,1,0:T(8,128)(2,1)S(1)}, bf16[4,8,2176]{2,1,0:T(8,128)(2,1)S(1)}, u32[]{:S(2)}, u32[]{:S(2)}) collective-permute-start(bf16[4,8,2176]{2,1,0:T(8,128)(2,1)S(1)} %pad_maximum_fusion.3.refs_1_), channel_id=1, source_target_pairs={{0,16},{1,17},{2,18},{3,19},{4,20},{5,21},{6,22},{7,23},{8,24},{9,... | collective-permute-start | bytes 417800 | tf_op jit(solution)/shard_map/ppermute | solution.py:32
  24.3 9.7 %collective-permute-start.3 = (bf16[4,8,2176]{2,1,0:T(8,128)(2,1)S(1)}, bf16[4,8,2176]{2,1,0:T(8,128)(2,1)S(1)}, u32[]{:S(2)}, u32[]{:S(2)}) collective-permute-start(bf16[4,8,2176]{2,1,0:T(8,128)(2,1)S(1)} %pad_maximum_fusion.3.refs_1_), channel_id=1, source_target_pairs={{0,24},{1,25},{2,26},{3,27},{4,28},{5,29},{6,30},{7,31},{8,0},{9,1... | collective-permute-start | bytes 417800 | tf_op jit(solution)/shard_map/ppermute | solution.py:32
  25.8 12.0 %collective-permute-start.10 = (bf16[4,2,8,2176]{3,2,0,1:T(8,128)(2,1)S(1)}, bf16[4,2,8,2176]{3,2,0,1:T(8,128)(2,1)S(1)}, u32[]{:S(2)}, u32[]{:S(2)}) collective-permute-start(bf16[4,2,8,2176]{3,2,0,1:T(8,128)(2,1)S(1)} %get-tuple-element.73), channel_id=1, source_target_pairs={{0,8},{1,9},{2,10},{3,11},{4,12},{5,13},{6,14},{7,15},{8,16},{9,17... | collective-permute-start | bytes 835592 | tf_op jit(solution)/shard_map/ppermute | solution.py:32
  26.4 14.5 %collective-permute-start.9 = (bf16[4,2,8,2176]{3,2,0,1:T(8,128)(2,1)S(1)}, bf16[4,2,8,2176]{3,2,0,1:T(8,128)(2,1)S(1)}, u32[]{:S(2)}, u32[]{:S(2)}) collective-permute-start(bf16[4,2,8,2176]{3,2,0,1:T(8,128)(2,1)S(1)} %get-tuple-element.73), channel_id=1, source_target_pairs={{0,16},{1,17},{2,18},{3,19},{4,20},{5,21},{6,22},{7,23},{8,24},{9,... | collective-permute-start | bytes 835592 | tf_op jit(solution)/shard_map/ppermute | solution.py:32
  27.9 13.0 %collective-permute-start.8 = (bf16[4,2,8,2176]{3,2,0,1:T(8,128)(2,1)S(1)}, bf16[4,2,8,2176]{3,2,0,1:T(8,128)(2,1)S(1)}, u32[]{:S(2)}, u32[]{:S(2)}) collective-permute-start(bf16[4,2,8,2176]{3,2,0,1:T(8,128)(2,1)S(1)} %get-tuple-element.73), channel_id=1, source_target_pairs={{0,24},{1,25},{2,26},{3,27},{4,28},{5,29},{6,30},{7,31},{8,0},{9,1... | collective-permute-start | bytes 835592 | tf_op jit(solution)/shard_map/ppermute | solution.py:32
  34.0 132.3 %copy-start.3 = (bf16[4,32,2176]{2,1,0:T(8,128)(2,1)}, bf16[4,32,2176]{2,1,0:T(8,128)(2,1)S(1)}, u32[]{:S(2)}) copy-start(bf16[4,32,2176]{2,1,0:T(8,128)(2,1)S(1)} %pad_maximum_fusion.1.refs_0_.refs_4_.refs_9_) | copy-start | bytes 1671172
  34.0 11.1 %collective-permute-start.11 = (bf16[4,32,2176]{2,1,0:T(8,128)(2,1)S(1)}, bf16[4,32,2176]{2,1,0:T(8,128)(2,1)S(1)}, u32[]{:S(2)}, u32[]{:S(2)}) collective-permute-start(bf16[4,32,2176]{2,1,0:T(8,128)(2,1)S(1)} %pad_maximum_fusion.1.refs_0_.refs_4_.refs_9_), channel_id=1, source_target_pairs={{0,4},{1,5},{2,6},{3,7},{4,0},{5,1},{6,2},{7,3},{8,12},{9,13},{10,... | collective-permute-start | bytes 1671176 | tf_op jit(solution)/shard_map/ppermute | solution.py:32
  41.2 110.3 %copy-start = (bf16[4,2,4,8,2176]{4,3,2,1,0:T(8,128)(2,1)}, bf16[4,2,4,8,2176]{4,3,2,1,0:T(8,128)(2,1)S(1)}, u32[]{:S(2)}) copy-start(bf16[4,2,4,8,2176]{4,3,2,1,0:T(8,128)(2,1)S(1)} %copy.13) | copy-start | bytes 3342340
  41.2 7.5 %collective-permute-start.13 = (bf16[4,64,2176]{2,1,0:T(8,128)(2,1)S(1)}, bf16[4,64,2176]{2,1,0:T(8,128)(2,1)S(1)}, u32[]{:S(2)}, u32[]{:S(2)}) collective-permute-start(bf16[4,64,2176]{2,1,0:T(8,128)(2,1)S(1)} %bitcast.22), channel_id=1, source_target_pairs={{0,1},{1,0},{2,3},{3,2},{4,5},{5,4},{6,7},{7,6},{8,9},{9,8},{10,11... | collective-permute-start | bytes 3342344 | tf_op jit(solution)/shard_map/ppermute | solution.py:32
  41.3 7.4 %collective-permute-start.12 = (bf16[4,32,2176]{2,1,0:T(8,128)(2,1)S(1)}, bf16[4,32,2176]{2,1,0:T(8,128)(2,1)S(1)}, u32[]{:S(2)}, u32[]{:S(2)}) collective-permute-start(bf16[4,32,2176]{2,1,0:T(8,128)(2,1)S(1)} %pad_maximum_fusion.1.refs_0_.refs_4_.refs_9_), channel_id=1, source_target_pairs={{0,1},{1,0},{2,3},{3,2},{4,5},{5,4},{6,7},{7,6},{8,9},{9,8},{10,11... | collective-permute-start | bytes 1671176 | tf_op jit(solution)/shard_map/ppermute | solution.py:32
  45.1 106.4 %copy-start.4 = (bf16[4,32,2176]{2,1,0:T(8,128)(2,1)}, bf16[4,32,2176]{2,1,0:T(8,128)(2,1)S(1)}, u32[]{:S(2)}) copy-start(bf16[4,32,2176]{2,1,0:T(8,128)(2,1)S(1)} %collective-permute-done.11.refs_2_.refs_6_.refs_11_.refs_5_) | copy-start | bytes 1671172
  45.1 3.6 %collective-permute-start.14 = (bf16[4,32,2176]{2,1,0:T(8,128)(2,1)S(1)}, bf16[4,32,2176]{2,1,0:T(8,128)(2,1)S(1)}, u32[]{:S(2)}, u32[]{:S(2)}) collective-permute-start(bf16[4,32,2176]{2,1,0:T(8,128)(2,1)S(1)} %collective-permute-done.11.refs_2_.refs_6_.refs_11_.refs_5_), channel_id=1, source_target_pairs={{0,1},{1,0},{2,3},{3,2},{4,5},{5,4},{6,7},{7,6},{8,9},{9,8},{10,11... | collective-permute-start | bytes 1671176 | tf_op jit(solution)/shard_map/ppermute | solution.py:32
  48.8 96.4 %copy-start.6 = (bf16[4,32,2176]{2,1,0:T(8,128)(2,1)}, bf16[4,32,2176]{2,1,0:T(8,128)(2,1)S(1)}, u32[]{:S(2)}) copy-start(bf16[4,32,2176]{2,1,0:T(8,128)(2,1)S(1)} %collective-permute-done.12.refs_3_.refs_7_.refs_9_) | copy-start | bytes 1671172
  48.8 96.3 %copy-start.7 = (bf16[4,32,2176]{2,1,0:T(8,128)(2,1)}, bf16[4,32,2176]{2,1,0:T(8,128)(2,1)S(1)}, u32[]{:S(2)}) copy-start(bf16[4,32,2176]{2,1,0:T(8,128)(2,1)S(1)} %collective-permute-done.14.refs_5_.refs_9_.refs_11_) | copy-start | bytes 1671172
  53.3 50.1 %collective-permute-start.19 = (bf16[2048,2048]{1,0:T(8,128)(2,1)S(1)}, bf16[2048,2048]{1,0:T(8,128)(2,1)}, u32[]{:S(2)}, u32[]{:S(2)}) collective-permute-start(bf16[2048,2048]{1,0:T(8,128)(2,1)S(1)} %bitcast.37), channel_id=1, source_target_pairs={{0,1},{1,0},{2,3},{3,2},{4,5},{5,4},{6,7},{7,6},{8,9},{9,8},{10,11... | collective-permute-start | bytes 25165832 | tf_op jit(solution)/shard_map/ppermute | solution.py:32
  53.7 15.9 %collective-permute-start.15 = (s16[128,2176]{1,0:T(8,128)(2,1)S(1)}, s16[128,2176]{1,0:T(8,128)(2,1)S(1)}, u32[]{:S(2)}, u32[]{:S(2)}) collective-permute-start(s16[128,2176]{1,0:T(8,128)(2,1)S(1)} %get-tuple-element.42.refs_7_), channel_id=1, source_target_pairs={{0,32},{32,64},{64,96},{96,0},{1,33},{33,65},{65,97},{97,1},{2,34}... | collective-permute-start | bytes 1671176 | tf_op jit(solution)/shard_map/ppermute | solution.py:22
  53.9 15.8 %collective-permute-start.16 = (s16[128,2176]{1,0:T(8,128)(2,1)S(1)}, s16[128,2176]{1,0:T(8,128)(2,1)S(1)}, u32[]{:S(2)}, u32[]{:S(2)}) collective-permute-start(s16[128,2176]{1,0:T(8,128)(2,1)S(1)} %get-tuple-element.45), channel_id=1, source_target_pairs={{0,96},{32,0},{64,32},{96,64},{1,97},{33,1},{65,33},{97,65},{2,98}... | collective-permute-start | bytes 1671176 | tf_op jit(solution)/shard_map/ppermute | solution.py:22
  70.7 27.1 %collective-permute-start.17 = (s16[256,2176]{1,0:T(8,128)(2,1)S(1)}, s16[256,2176]{1,0:T(8,128)(2,1)S(1)}, u32[]{:S(2)}, u32[]{:S(2)}) collective-permute-start(s16[256,2176]{1,0:T(8,128)(2,1)S(1)} %get-tuple-element.46.refs_7_), channel_id=1, source_target_pairs={{0,32},{32,64},{64,96},{96,0},{1,33},{33,65},{65,97},{97,1},{2,34}... | collective-permute-start | bytes 3342344 | tf_op jit(solution)/shard_map/ppermute | solution.py:22
  71.0 26.8 %collective-permute-start.18 = (s16[256,2176]{1,0:T(8,128)(2,1)S(1)}, s16[256,2176]{1,0:T(8,128)(2,1)S(1)}, u32[]{:S(2)}, u32[]{:S(2)}) collective-permute-start(s16[256,2176]{1,0:T(8,128)(2,1)S(1)} %get-tuple-element.47), channel_id=1, source_target_pairs={{0,96},{32,0},{64,32},{96,64},{1,97},{33,1},{65,33},{97,65},{2,98}... | collective-permute-start | bytes 3342344 | tf_op jit(solution)/shard_map/ppermute | solution.py:22
  100.4 23.8 %collective-permute-start.30 = (bf16[2,128,2048]{2,1,0:T(8,128)(2,1)S(1)}, bf16[2,128,2048]{2,1,0:T(8,128)(2,1)S(1)}, u32[]{:S(2)}, u32[]{:S(2)}) collective-permute-start(bf16[2,128,2048]{2,1,0:T(8,128)(2,1)S(1)} %get-tuple-element.50.refs_5_), channel_id=1, source_target_pairs={{0,96},{32,0},{64,32},{96,64},{1,97},{33,1},{65,33},{97,65},{2,98}... | collective-permute-start | bytes 3145736 | tf_op jit(solution)/shard_map/ppermute | solution.py:22
  103.4 24.2 %collective-permute-start.31 = (bf16[2,128,2048]{2,1,0:T(8,128)(2,1)S(1)}, bf16[2,128,2048]{2,1,0:T(8,128)(2,1)S(1)}, u32[]{:S(2)}, u32[]{:S(2)}) collective-permute-start(bf16[2,128,2048]{2,1,0:T(8,128)(2,1)S(1)} %get-tuple-element.50.refs_5_), channel_id=1, source_target_pairs={{0,32},{32,64},{64,96},{96,0},{1,33},{33,65},{65,97},{97,1},{2,34}... | collective-permute-start | bytes 3145736 | tf_op jit(solution)/shard_map/ppermute | solution.py:22
  107.5 1.2 collective-permute-start.20
  108.7 5.7 %collective-permute-start.21 = (f32[8,256]{1,0:T(8,128)S(1)}, f32[8,256]{1,0:T(8,128)S(1)}, u32[]{:S(2)}, u32[]{:S(2)}) collective-permute-start(f32[8,256]{1,0:T(8,128)S(1)} %merge_statistics.2.refs_0_), channel_id=1, source_target_pairs={{0,24},{1,25},{2,26},{3,27},{4,28},{5,29},{6,30},{7,31},{8,0},{9,1... | collective-permute-start | bytes 24584 | tf_op jit(solution)/shard_map/ppermute | solution.py:32
  113.0 5.2 %collective-permute-start.22 = (f32[8,256]{1,0:T(8,128)S(1)}, f32[8,256]{1,0:T(8,128)S(1)}, u32[]{:S(2)}, u32[]{:S(2)}) collective-permute-start(f32[8,256]{1,0:T(8,128)S(1)} %merge_statistics.2.refs_0_), channel_id=1, source_target_pairs={{0,16},{1,17},{2,18},{3,19},{4,20},{5,21},{6,22},{7,23},{8,24},{9,... | collective-permute-start | bytes 24584 | tf_op jit(solution)/shard_map/ppermute | solution.py:32
  113.0 5.2 %collective-permute-start.23 = (f32[8,256]{1,0:T(8,128)S(1)}, f32[8,256]{1,0:T(8,128)S(1)}, u32[]{:S(2)}, u32[]{:S(2)}) collective-permute-start(f32[8,256]{1,0:T(8,128)S(1)} %merge_statistics.2.refs_0_), channel_id=1, source_target_pairs={{0,8},{1,9},{2,10},{3,11},{4,12},{5,13},{6,14},{7,15},{8,16},{9,17... | collective-permute-start | bytes 24584 | tf_op jit(solution)/shard_map/ppermute | solution.py:32
  127.6 17.5 %collective-permute-start.32 = (bf16[128,2048]{1,0:T(8,128)(2,1)S(1)}, bf16[128,2048]{1,0:T(8,128)(2,1)S(1)}, u32[]{:S(2)}, u32[]{:S(2)}) collective-permute-start(bf16[128,2048]{1,0:T(8,128)(2,1)S(1)} %get-tuple-element.51), channel_id=1, source_target_pairs={{0,32},{32,64},{64,96},{96,0},{1,33},{33,65},{65,97},{97,1},{2,34}... | collective-permute-start | bytes 1572872 | tf_op jit(solution)/shard_map/ppermute | solution.py:22
  127.7 17.4 %collective-permute-start.33 = (bf16[128,2048]{1,0:T(8,128)(2,1)S(1)}, bf16[128,2048]{1,0:T(8,128)(2,1)S(1)}, u32[]{:S(2)}, u32[]{:S(2)}) collective-permute-start(bf16[128,2048]{1,0:T(8,128)(2,1)S(1)} %get-tuple-element.52), channel_id=1, source_target_pairs={{0,96},{32,0},{64,32},{96,64},{1,97},{33,1},{65,33},{97,65},{2,98}... | collective-permute-start | bytes 1572872 | tf_op jit(solution)/shard_map/ppermute | solution.py:22
  130.9 3.7 %collective-permute-start.24 = (f32[8,256]{1,0:T(8,128)S(1)}, f32[8,256]{1,0:T(8,128)S(1)}, u32[]{:S(2)}, u32[]{:S(2)}) collective-permute-start(f32[8,256]{1,0:T(8,128)S(1)} %merge_statistics.3.refs_2_), channel_id=1, source_target_pairs={{0,6},{1,7},{2,0},{3,1},{4,2},{5,3},{6,4},{7,5},{8,14},{9,15},{10,... | collective-permute-start | bytes 24584 | tf_op jit(solution)/shard_map/ppermute | solution.py:32
  132.1 5.2 %collective-permute-start.25 = (f32[8,256]{1,0:T(8,128)S(1)}, f32[8,256]{1,0:T(8,128)S(1)}, u32[]{:S(2)}, u32[]{:S(2)}) collective-permute-start(f32[8,256]{1,0:T(8,128)S(1)} %merge_statistics.3.refs_2_), channel_id=1, source_target_pairs={{0,4},{1,5},{2,6},{3,7},{4,0},{5,1},{6,2},{7,3},{8,12},{9,13},{10,... | collective-permute-start | bytes 24584 | tf_op jit(solution)/shard_map/ppermute | solution.py:32
  132.1 5.2 %collective-permute-start.26 = (f32[8,256]{1,0:T(8,128)S(1)}, f32[8,256]{1,0:T(8,128)S(1)}, u32[]{:S(2)}, u32[]{:S(2)}) collective-permute-start(f32[8,256]{1,0:T(8,128)S(1)} %merge_statistics.3.refs_2_), channel_id=1, source_target_pairs={{0,2},{1,3},{2,4},{3,5},{4,6},{5,7},{6,0},{7,1},{8,10},{9,11},{10,... | collective-permute-start | bytes 24584 | tf_op jit(solution)/shard_map/ppermute | solution.py:32
  138.7 3.7 %collective-permute-start.27 = (f32[8,256]{1,0:T(8,128)S(1)}, f32[8,256]{1,0:T(8,128)S(1)}, u32[]{:S(2)}, u32[]{:S(2)}) collective-permute-start(f32[8,256]{1,0:T(8,128)S(1)} %combine_statistics.1.refs_1_.refs_6_), channel_id=1, source_target_pairs={{0,96},{32,0},{64,32},{96,64},{1,97},{33,1},{65,33},{97,65},{2,98}... | collective-permute-start | bytes 24584 | tf_op jit(solution)/shard_map/ppermute | solution.py:22
  138.8 5.2 %collective-permute-start.28 = (f32[8,256]{1,0:T(8,128)S(1)}, f32[8,256]{1,0:T(8,128)S(1)}, u32[]{:S(2)}, u32[]{:S(2)}) collective-permute-start(f32[8,256]{1,0:T(8,128)S(1)} %combine_statistics.1.refs_1_.refs_6_), channel_id=1, source_target_pairs={{0,64},{32,96},{64,0},{96,32},{1,65},{33,97},{65,1},{97,33},{2,66}... | collective-permute-start | bytes 24584 | tf_op jit(solution)/shard_map/ppermute | solution.py:22
  139.7 5.4 %collective-permute-start.29 = (f32[8,256]{1,0:T(8,128)S(1)}, f32[8,256]{1,0:T(8,128)S(1)}, u32[]{:S(2)}, u32[]{:S(2)}) collective-permute-start(f32[8,256]{1,0:T(8,128)S(1)} %combine_statistics.1.refs_1_.refs_6_), channel_id=1, source_target_pairs={{0,32},{32,64},{64,96},{96,0},{1,33},{33,65},{65,97},{97,1},{2,34}... | collective-permute-start | bytes 24584 | tf_op jit(solution)/shard_map/ppermute | solution.py:22
  147.3 4.2 %collective-permute-start.34 = (bf16[4,128,2048]{2,1,0:T(8,128)(2,1)S(1)}, bf16[4,128,2048]{2,1,0:T(8,128)(2,1)S(1)}, u32[]{:S(2)}, u32[]{:S(2)}) collective-permute-start(bf16[4,128,2048]{2,1,0:T(8,128)(2,1)S(1)} %dlogit.2.refs_12_.refs_7_), channel_id=1, source_target_pairs={{0,1},{1,0},{2,3},{3,2},{4,5},{5,4},{6,7},{7,6},{8,9},{9,8},{10,11... | collective-permute-start | bytes 6291464 | tf_op jit(solution)/shard_map/ppermute | solution.py:32
  161.1 28.6 %collective-permute-start.35 = (bf16[4,32,2048]{2,1,0:T(8,128)(2,1)}, bf16[4,32,2048]{2,1,0:T(8,128)(2,1)S(1)}, u32[]{:S(2)}, u32[]{:S(2)}) collective-permute-start(bf16[4,32,2048]{2,1,0:T(8,128)(2,1)} %get-tuple-element.55), channel_id=1, source_target_pairs={{0,4},{1,5},{2,6},{3,7},{4,0},{5,1},{6,2},{7,3},{8,12},{9,13},{10,... | collective-permute-start | bytes 1572872 | tf_op jit(solution)/shard_map/ppermute | solution.py:32
  163.0 27.3 %collective-permute-start.36 = (bf16[4,32,2048]{2,1,0:T(8,128)(2,1)}, bf16[4,32,2048]{2,1,0:T(8,128)(2,1)S(1)}, u32[]{:S(2)}, u32[]{:S(2)}) collective-permute-start(bf16[4,32,2048]{2,1,0:T(8,128)(2,1)} %get-tuple-element.56), channel_id=1, source_target_pairs={{0,2},{1,3},{2,4},{3,5},{4,6},{5,7},{6,0},{7,1},{8,10},{9,11},{10,... | collective-permute-start | bytes 1572872 | tf_op jit(solution)/shard_map/ppermute | solution.py:32
  163.9 26.4 %collective-permute-start.37 = (bf16[4,32,2048]{2,1,0:T(8,128)(2,1)}, bf16[4,32,2048]{2,1,0:T(8,128)(2,1)}, u32[]{:S(2)}, u32[]{:S(2)}) collective-permute-start(bf16[4,32,2048]{2,1,0:T(8,128)(2,1)} %get-tuple-element.57), channel_id=1, source_target_pairs={{0,6},{1,7},{2,0},{3,1},{4,2},{5,3},{6,4},{7,5},{8,14},{9,15},{10,... | collective-permute-start | bytes 1572872 | tf_op jit(solution)/shard_map/ppermute | solution.py:32
  174.0 30.4 %all-to-all-start = ((f32[32,8,256]{2,1,0:T(8,128)}), f32[32,8,256]{2,1,0:T(8,128)S(1)}, u32[]{:S(2)}, u32[]{:S(2)}) async-start(f32[32,8,256]{2,1,0:T(8,128)} %gain_parts.1), calls=%async_computation | async-start | bytes 524288 | tf_op jit(solution)/shard_map/all_to_all | solution.py:677
  191.6 12.7 %collective-permute-start.38 = (bf16[32,2048]{1,0:T(8,128)(2,1)S(1)}, bf16[32,2048]{1,0:T(8,128)(2,1)S(1)}, u32[]{:S(2)}, u32[]{:S(2)}) collective-permute-start(bf16[32,2048]{1,0:T(8,128)(2,1)S(1)} %get-tuple-element.61), channel_id=1, source_target_pairs={{0,8},{1,9},{2,10},{3,11},{4,12},{5,13},{6,14},{7,15},{8,16},{9,17... | collective-permute-start | bytes 393224 | tf_op jit(solution)/shard_map/ppermute | solution.py:32
  194.1 10.3 %collective-permute-start.39 = (bf16[32,2048]{1,0:T(8,128)(2,1)S(1)}, bf16[32,2048]{1,0:T(8,128)(2,1)S(1)}, u32[]{:S(2)}, u32[]{:S(2)}) collective-permute-start(bf16[32,2048]{1,0:T(8,128)(2,1)S(1)} %get-tuple-element.62), channel_id=1, source_target_pairs={{0,16},{1,17},{2,18},{3,19},{4,20},{5,21},{6,22},{7,23},{8,24},{9,... | collective-permute-start | bytes 393224 | tf_op jit(solution)/shard_map/ppermute | solution.py:32
  197.4 7.0 %collective-permute-start.40 = (bf16[32,2048]{1,0:T(8,128)(2,1)S(1)}, bf16[32,2048]{1,0:T(8,128)(2,1)S(1)}, u32[]{:S(2)}, u32[]{:S(2)}) collective-permute-start(bf16[32,2048]{1,0:T(8,128)(2,1)S(1)} %get-tuple-element.63), channel_id=1, source_target_pairs={{0,24},{1,25},{2,26},{3,27},{4,28},{5,29},{6,30},{7,31},{8,0},{9,1... | collective-permute-start | bytes 393224 | tf_op jit(solution)/shard_map/ppermute | solution.py:32
  205.9 12.7 %all-to-all-start.1 = ((f32[4,16,2048]{2,1,0:T(8,128)}), f32[4,16,2048]{2,1,0:T(8,128)S(1)}, u32[]{:S(2)}, u32[]{:S(2)}) async-start(f32[4,16,2048]{2,1,0:T(8,128)} %over_y.1.refs_9_), calls=%async_computation.1 | async-start | bytes 1048576 | tf_op jit(solution)/shard_map/all_to_all | solution.py:684
  (10 other events, 160.4 us)

commit v2 on v1

--- a/solution.py
+++ b/solution.py
@@ -81,20 +81,21 @@
     return codes * jnp.exp2(power - 15.0)
 
 
-def hold_kernel(head, held, sem):
+def hold_kernel(head, held, token, sem):
     copy = pltpu.make_async_copy(head, held, sem)
     copy.start()
+    token[...] = jnp.zeros_like(token)
     copy.wait()
 
 
 def hold(head, after=()):
     return launch(
         hold_kernel,
-        (in_hbm(head),),
-        after,
-        out_shape=pltpu.VMEM(head.shape, head.dtype),
+        (head,),
+        after,
+        out_shape=[pltpu.VMEM(head.shape, head.dtype), shape(8, TAIL)],
         in_specs=[ANY],
-        out_specs=VMEM,
+        out_specs=[VMEM] * 2,
         scratch_shapes=[pltpu.SemaphoreType.DMA(())],
         cost_estimate=cost(0, 2 * head.size),
         name="hold_head",
@@ -627,21 +628,22 @@
     weights = section_weights(exit_layer, numerators)
     weight = jnp.sum(jnp.where(jnp.arange(SIDE) == section, weights, 0.0)).reshape(1)
 
-    cuts = normalise(place, hidden_rows, gain_row, targets, (weight,))
+    cuts = normalise(place, in_hbm(hidden_rows), in_hbm(gain_row), targets)
     own = jnp.stack([cuts[0], over_section(cuts[3], -1), over_section(cuts[2], 2), over_section(cuts[1], 1)])
     def along_x(x):
         return [x, over_vocab(x, dx=-1), over_vocab(x, dx=2), over_vocab(x, dx=1)]
 
     pair = jnp.stack([over_vocab(own, dz=-1), over_vocab(own, dz=1)], axis=1)
     mine = [jnp.concatenate(along_x(own), axis=1)]
-    mine.append(jnp.stack(along_x(pair), axis=2).reshape(SIDE, -1, own.shape[2]))
+    held_head, token = hold(head_weight, (own,))
+    *pair, _ = lax.optimization_barrier((*along_x(pair), token))
+    mine.append(jnp.stack(pair, axis=2).reshape(SIDE, -1, own.shape[2]))
     mine.append(over_vocab(mine[0], dz=2))
     theirs = [over_vocab(m, dc=1) for m in mine]
     pieces = (*mine, *theirs)
     groups = ((0,), (1, 3), (2,))
     everything = (sum(groups, ()),)
 
-    held_head = hold(head_weight, (own,))
     up, down = logits_of((2,), pieces, held_head)
     head_ready, _ = lax.optimization_barrier((head_weight, up))
     other_head = over_vocab(head_ready, dc=1)
@@ -649,15 +651,15 @@
     up, down = over_section(up, 1), over_section(down, -1)
     first, last = pass_on(first, last, up, down)
     (kept,) = logits_of((0,), pieces, held_head, (first,))
-    held_other = hold(other_head, (kept,))
     below, above = over_section(first, 1), over_section(last, -1)
     exps, stats = own_logits(place, kept, below, above, mine, theirs)
 
     below, above = over_section(exps, 1), over_section(exps, -1)
-    parts = pack(place, [stats], everything, own_rows, (held_other,))
+    held_other, token = hold(other_head, (stats,))
+    parts = pack(place, [stats], everything, own_rows, (token,))
     parts = merge([parts, over_vocab(parts, dc=1)])
     parts = merge(along_x(parts))
-    far_first, far_last = halves(below, above, (parts,))
+    far_first, far_last = halves(below, above, (parts, token))
     far_first, far_last = over_section(far_first, 1), over_section(far_last, -1)
     parts = [parts, over_vocab(parts, dz=-1), over_vocab(parts, dz=2), over_vocab(parts, dz=1)]
     scales = combine(place, weight, parts, stats, everything[0], own_rows)

time: 220 us -> 215 us (0.977)
  waiting for transfers between devices: 71.1 us -> 67 us
    ppermute x27, waiting for transfers between devices: 26.9 us -> 21.7 us  [over_vocab(): return lax.ppermute(x, 'vocab', pairs)]
  transfers between devices with their start and end apart: 43 -> 43, of which waited for: 25 -> 21; matrix products, arithmetic and copies ran while one was open for 0% -> 1% of each run, Pallas kernels for 27% -> 28%
where the time goes in v2:
time: 215 us
  Pallas kernels  78.9 us (37%)
  waiting for transfers between devices  67 us (31%)
  starting transfers between devices  63.5 us (30%)
  other arithmetic  2.31 us (1%)
    pallas_call x24, Pallas kernels, launch(): pl.pallas_call(body, in_specs=[*in_specs, *[ANY] * ignored], scratch_shap...  78.9 us
    ppermute x14, waiting for transfers between devices, over_section(): lax.ppermute(x, 'section', [(i, (i + step) % SIDE) for i in range(SIDE)])  43.3 us
    ppermute x27, starting transfers between devices, over_vocab(): return lax.ppermute(x, 'vocab', pairs)  34.5 us
    ppermute x27, waiting for transfers between devices, over_vocab(): return lax.ppermute(x, 'vocab', pairs)  21.7 us
    ppermute x14, starting transfers between devices, over_section(): lax.ppermute(x, 'section', [(i, (i + step) % SIDE) for i in range(SIDE)])  20.9 us
    all_to_all x1, starting transfers between devices, local(): gains = lax.all_to_all(spread(gain_near, gain_own), 'vocab', 0, 0)  4.72 us
  transfers between devices with their start and end apart: 43, of which 21 were waited for; matrix products, arithmetic and copies ran while one was open for 1% of the time, Pallas kernels for 28%

profile of v2, /device:TPU:0, one launch (start us, length us, event | category | flops | bytes accessed | tf_op | source)
XLA Modules:
  0.0 214.6 jit_solution(9184456591760084941)
XLA Ops:
  2.5 1.7 collective-permute-start.2
  4.2 2.9 %collective-permute-start.1 = (bf16[8,2176]{1,0:T(8,128)(2,1)S(1)}, bf16[8,2176]{1,0:T(8,128)(2,1)S(1)}, u32[]{:S(2)}, u32[]{:S(2)}) collective-permute-start(bf16[8,2176]{1,0:T(8,128)(2,1)S(1)} %get-tuple-element.47), channel_id=1, source_target_pairs={{0,64},{32,96},{64,0},{96,32},{1,65},{33,97},{65,1},{97,33},{2,66}... | collective-permute-start | bytes 104456 | tf_op jit(solution)/shard_map/ppermute | solution.py:22
  11.1 2.0 collective-permute-start.7
  13.1 2.2 %collective-permute-start.6 = (bf16[4,8,2176]{2,1,0:T(8,128)(2,1)S(1)}, bf16[4,8,2176]{2,1,0:T(8,128)(2,1)S(1)}, u32[]{:S(2)}, u32[]{:S(2)}) collective-permute-start(bf16[4,8,2176]{2,1,0:T(8,128)(2,1)S(1)} %pad_maximum_fusion.3.refs_1_), channel_id=1, source_target_pairs={{0,6},{1,7},{2,0},{3,1},{4,2},{5,3},{6,4},{7,5},{8,14},{9,15},{10,... | collective-permute-start | bytes 417800 | tf_op jit(solution)/shard_map/ppermute | solution.py:32
  15.3 1.5 collective-permute-start.5
  16.8 2.7 %collective-permute-start.4 = (bf16[4,8,2176]{2,1,0:T(8,128)(2,1)S(1)}, bf16[4,8,2176]{2,1,0:T(8,128)(2,1)S(1)}, u32[]{:S(2)}, u32[]{:S(2)}) collective-permute-start(bf16[4,8,2176]{2,1,0:T(8,128)(2,1)S(1)} %pad_maximum_fusion.3.refs_1_), channel_id=1, source_target_pairs={{0,16},{1,17},{2,18},{3,19},{4,20},{5,21},{6,22},{7,23},{8,24},{9,... | collective-permute-start | bytes 417800 | tf_op jit(solution)/shard_map/ppermute | solution.py:32
  21.1 2.6 %collective-permute-start.9 = (bf16[4,2,8,2176]{3,2,0,1:T(8,128)(2,1)S(1)}, bf16[4,2,8,2176]{3,2,0,1:T(8,128)(2,1)S(1)}, u32[]{:S(2)}, u32[]{:S(2)}) collective-permute-start(bf16[4,2,8,2176]{3,2,0,1:T(8,128)(2,1)S(1)} %pad_maximum_fusion.2), channel_id=1, source_target_pairs={{0,16},{1,17},{2,18},{3,19},{4,20},{5,21},{6,22},{7,23},{8,24},{9,... | collective-permute-start | bytes 835592 | tf_op jit(solution)/shard_map/ppermute | solution.py:32
  23.7 2.1 collective-permute-done.4
  27.0 1.9 collective-permute-start.11
  28.9 4.0 %collective-permute-done.8 = bf16[4,2,8,2176]{3,2,0,1:T(8,128)(2,1)S(1)} collective-permute-done((bf16[4,2,8,2176]{3,2,0,1:T(8,128)(2,1)S(1)}, bf16[4,2,8,2176]{3,2,0,1:T(8,128)(2,1)S(1)}, u32[]{:S(2)}, u32[]{:S(2)}) %collective-permute-start.8) | collective-permute-done | bytes 278560 | tf_op jit(solution)/shard_map/ppermute | solution.py:32
  32.9 3.2 %collective-permute-done.10 = bf16[4,2,8,2176]{3,2,0,1:T(8,128)(2,1)S(1)} collective-permute-done((bf16[4,2,8,2176]{3,2,0,1:T(8,128)(2,1)S(1)}, bf16[4,2,8,2176]{3,2,0,1:T(8,128)(2,1)S(1)}, u32[]{:S(2)}, u32[]{:S(2)}) %collective-permute-start.10) | collective-permute-done | bytes 278560 | tf_op jit(solution)/shard_map/ppermute | solution.py:32
  38.1 4.2 %hold_head.2 = (bf16[2048,2048]{1,0:T(8,128)(2,1)S(1)}, f32[8,128]{1,0:T(8,128)}) custom-call(bf16[2048,2048]{1,0:T(8,128)(2,1)} %refs_0_.2, bf16[4,8,2176]{2,1,0:T(8,128)(2,1)S(1)} %pad_maximum_fusion.3.refs_1_), custom_call_target="tpu_custom_call" | custom-call | bytes 8388608 | tf_op jit(solution)/shard_map/hold_head/pallas_call | solution.py:57
  42.4 4.5 %partial_logits.3 = (s16[128,2176]{1,0:T(8,128)(2,1)S(1)}, s16[128,2176]{1,0:T(8,128)(2,1)S(1)}) custom-call(bf16[4,32,2176]{2,1,0:T(8,128)(2,1)S(1)} %pad_maximum_fusion.1.refs_0_.refs_4_.refs_9_, bf16[4,64,2176]{2,1,0:T(8,128)(2,1)S(1)} %bitcast.22, bf16[4,32,2176]{2,1,0:T(8,128)(2,1)S(1)} %collective-permute-done.11.refs_2_.refs_6_.refs_11_.refs_5_, ...), custom_call_target="tpu_custom_call" | custom-call | bytes 10485760 | tf_op jit(solution)/shard_map/partial_logits/pallas_call | solution.py:57
  47.4 3.1 %collective-permute-start.16 = (s16[128,2176]{1,0:T(8,128)(2,1)S(1)}, s16[128,2176]{1,0:T(8,128)(2,1)S(1)}, u32[]{:S(2)}, u32[]{:S(2)}) collective-permute-start(s16[128,2176]{1,0:T(8,128)(2,1)S(1)} %get-tuple-element.57), channel_id=1, source_target_pairs={{0,96},{32,0},{64,32},{96,64},{1,97},{33,1},{65,33},{97,65},{2,98}... | collective-permute-start | bytes 1671176 | tf_op jit(solution)/shard_map/ppermute | solution.py:22
  50.5 6.7 %partial_logits.4 = (f32[256,2048]{1,0:T(8,128)S(1)}, f32[256,2048]{1,0:T(8,128)S(1)}) custom-call(bf16[4,32,2176]{2,1,0:T(8,128)(2,1)S(1)} %pad_maximum_fusion.1.refs_0_.refs_4_.refs_9_, bf16[4,64,2176]{2,1,0:T(8,128)(2,1)S(1)} %bitcast.23, bf16[4,32,2176]{2,1,0:T(8,128)(2,1)S(1)} %collective-permute-done.11.refs_2_.refs_6_.refs_11_.refs_5_, ...), custom_call_target="tpu_custom_call" | custom-call | bytes 12582912 | tf_op jit(solution)/shard_map/partial_logits/pallas_call | solution.py:57
  57.2 6.0 %collective-permute-done.15.refs_2_ = s16[128,2176]{1,0:T(8,128)(2,1)S(1)} collective-permute-done((s16[128,2176]{1,0:T(8,128)(2,1)S(1)}, s16[128,2176]{1,0:T(8,128)(2,1)S(1)}, u32[]{:S(2)}, u32[]{:S(2)}) %collective-permute-start.15) | collective-permute-done | bytes 557088 | tf_op jit(solution)/shard_map/ppermute | solution.py:22
  65.2 2.4 %collective-permute-start.18 = (s16[256,2176]{1,0:T(8,128)(2,1)S(1)}, s16[256,2176]{1,0:T(8,128)(2,1)S(1)}, u32[]{:S(2)}, u32[]{:S(2)}) collective-permute-start(s16[256,2176]{1,0:T(8,128)(2,1)S(1)} %get-tuple-element.59), channel_id=1, source_target_pairs={{0,96},{32,0},{64,32},{96,64},{1,97},{33,1},{65,33},{97,65},{2,98}... | collective-permute-start | bytes 3342344 | tf_op jit(solution)/shard_map/ppermute | solution.py:22
  67.6 4.1 %partial_logits.5.refs_1_ = f32[256,2048]{1,0:T(8,128)S(1)} custom-call(bf16[4,32,2176]{2,1,0:T(8,128)(2,1)S(1)} %pad_maximum_fusion.1.refs_0_.refs_4_.refs_9_, bf16[4,64,2176]{2,1,0:T(8,128)(2,1)S(1)} %bitcast.24, bf16[4,32,2176]{2,1,0:T(8,128)(2,1)S(1)} %collective-permute-done.11.refs_2_.refs_6_.refs_11_.refs_5_, ...), custom_call_target="tpu_custom_call" | custom-call | bytes 10485760 | tf_op jit(solution)/shard_map/partial_logits/pallas_call | solution.py:57
  71.7 19.7 %collective-permute-done.17.refs_2_ = s16[256,2176]{1,0:T(8,128)(2,1)S(1)} collective-permute-done((s16[256,2176]{1,0:T(8,128)(2,1)S(1)}, s16[256,2176]{1,0:T(8,128)(2,1)S(1)}, u32[]{:S(2)}, u32[]{:S(2)}) %collective-permute-start.17) | collective-permute-done | bytes 1114144 | tf_op jit(solution)/shard_map/ppermute | solution.py:22
  91.4 2.5 %own_logits.1 = (bf16[2,128,2048]{2,1,0:T(8,128)(2,1)S(1)}, f32[256,128]{1,0:T(8,128)S(1)}) custom-call(s32[5]{0:T(128)S(1)} %stack.62.refs_0_, f32[256,2048]{1,0:T(8,128)S(1)} %partial_logits.5.refs_1_, s16[256,2176]{1,0:T(8,128)(2,1)S(1)} %collective-permute-done.17.refs_2_, s16[256,2176]{1,0:T(8,128)(2,1)S(1)} %collective-permute-done.18.refs_3_, ...), custom_call_target="tpu_custom_call" | custom-call | flops 10485760 | bytes 6291456 | tf_op jit(solution)/shard_map/own_logits/pallas_call | solution.py:57
  93.9 3.0 %collective-permute-start.30 = (bf16[2,128,2048]{2,1,0:T(8,128)(2,1)S(1)}, bf16[2,128,2048]{2,1,0:T(8,128)(2,1)S(1)}, u32[]{:S(2)}, u32[]{:S(2)}) collective-permute-start(bf16[2,128,2048]{2,1,0:T(8,128)(2,1)S(1)} %get-tuple-element.63.refs_5_), channel_id=1, source_target_pairs={{0,96},{32,0},{64,32},{96,64},{1,97},{33,1},{65,33},{97,65},{2,98}... | collective-permute-start | bytes 3145736 | tf_op jit(solution)/shard_map/ppermute | solution.py:22
  96.9 3.4 %hold_head.3 = (bf16[2048,2048]{1,0:T(8,128)(2,1)S(1)}, f32[8,128]{1,0:T(8,128)S(1)}) custom-call(bf16[2048,2048]{1,0:T(8,128)(2,1)} %collective-permute-done.19.refs_0_, f32[256,128]{1,0:T(8,128)S(1)} %get-tuple-element.60.refs_1_.refs_6_), custom_call_target="tpu_custom_call" | custom-call | bytes 8388608 | tf_op jit(solution)/shard_map/hold_head/pallas_call | solution.py:57
  102.3 2.4 %collective-permute-start.21 = (f32[8,256]{1,0:T(8,128)S(1)}, f32[8,256]{1,0:T(8,128)S(1)}, u32[]{:S(2)}, u32[]{:S(2)}) collective-permute-start(f32[8,256]{1,0:T(8,128)S(1)} %merge_statistics.2.refs_0_), channel_id=1, source_target_pairs={{0,24},{1,25},{2,26},{3,27},{4,28},{5,29},{6,30},{7,31},{8,0},{9,1... | collective-permute-start | bytes 24584 | tf_op jit(solution)/shard_map/ppermute | solution.py:32
  106.8 3.0 %collective-permute-done.22.refs_2_ = f32[8,256]{1,0:T(8,128)S(1)} collective-permute-done((f32[8,256]{1,0:T(8,128)S(1)}, f32[8,256]{1,0:T(8,128)S(1)}, u32[]{:S(2)}, u32[]{:S(2)}) %collective-permute-start.22) | collective-permute-done | bytes 8224 | tf_op jit(solution)/shard_map/ppermute | solution.py:32
  110.4 7.3 %collective-permute-done.30.refs_1_.refs_6_ = bf16[2,128,2048]{2,1,0:T(8,128)(2,1)S(1)} collective-permute-done((bf16[2,128,2048]{2,1,0:T(8,128)(2,1)S(1)}, bf16[2,128,2048]{2,1,0:T(8,128)(2,1)S(1)}, u32[]{:S(2)}, u32[]{:S(2)}) %collective-permute-start.30) | collective-permute-done | bytes 1048608 | tf_op jit(solution)/shard_map/ppermute | solution.py:22
  117.7 3.4 %collective-permute-done.31.refs_0_.refs_8_ = bf16[2,128,2048]{2,1,0:T(8,128)(2,1)S(1)} collective-permute-done((bf16[2,128,2048]{2,1,0:T(8,128)(2,1)S(1)}, bf16[2,128,2048]{2,1,0:T(8,128)(2,1)S(1)}, u32[]{:S(2)}, u32[]{:S(2)}) %collective-permute-start.31) | collective-permute-done | bytes 1048608 | tf_op jit(solution)/shard_map/ppermute | solution.py:22
  121.3 3.2 %collective-permute-start.33 = (bf16[128,2048]{1,0:T(8,128)(2,1)S(1)}, bf16[128,2048]{1,0:T(8,128)(2,1)S(1)}, u32[]{:S(2)}, u32[]{:S(2)}) collective-permute-start(bf16[128,2048]{1,0:T(8,128)(2,1)S(1)} %get-tuple-element.65), channel_id=1, source_target_pairs={{0,96},{32,0},{64,32},{96,64},{1,97},{33,1},{65,33},{97,65},{2,98}... | collective-permute-start | bytes 1572872 | tf_op jit(solution)/shard_map/ppermute | solution.py:22
  125.3 2.0 collective-permute-start.24
  129.8 2.6 %collective-permute-done.25.refs_4_ = f32[8,256]{1,0:T(8,128)S(1)} collective-permute-done((f32[8,256]{1,0:T(8,128)S(1)}, f32[8,256]{1,0:T(8,128)S(1)}, u32[]{:S(2)}, u32[]{:S(2)}) %collective-permute-start.25) | collective-permute-done | bytes 8224 | tf_op jit(solution)/shard_map/ppermute | solution.py:32
  135.9 1.6 collective-permute-done.27.refs_2_
  137.6 1.6 collective-permute-done.28.refs_3_
  140.3 2.1 dlogit.2.refs_12_.refs_7_
  142.5 2.1 dlogit.3.refs_0_.refs_6_
  144.6 2.0 collective-permute-done.34.refs_1_
  146.7 9.6 %dnormed.2 = (bf16[4,32,2048]{2,1,0:T(8,128)(2,1)}, bf16[4,32,2048]{2,1,0:T(8,128)(2,1)}, bf16[4,32,2048]{2,1,0:T(8,128)(2,1)}, f32[8,2048]{1,0:T(8,128)S(1)}) custom-call(bf16[4,128,2048]{2,1,0:T(8,128)(2,1)S(1)} %dlogit.3.refs_0_.refs_6_, bf16[4,128,2048]{2,1,0:T(8,128)(2,1)S(1)} %collective-permute-done.34.refs_1_, ...), custom_call_target="tpu_custom_call" | custom-call | bytes 16777216 | tf_op jit(solution)/shard_map/dnormed/pallas_call | solution.py:57
  156.3 2.0 collective-permute-start.35
  158.3 3.2 %collective-permute-start.37 = (bf16[4,32,2048]{2,1,0:T(8,128)(2,1)}, bf16[4,32,2048]{2,1,0:T(8,128)(2,1)}, u32[]{:S(2)}, u32[]{:S(2)}) collective-permute-start(bf16[4,32,2048]{2,1,0:T(8,128)(2,1)} %get-tuple-element.71), channel_id=1, source_target_pairs={{0,6},{1,7},{2,0},{3,1},{4,2},{5,3},{6,4},{7,5},{8,14},{9,15},{10,... | collective-permute-start | bytes 1572872 | tf_op jit(solution)/shard_map/ppermute | solution.py:32
  161.5 7.0 %dnormed.3 = (f32[4,32,2048]{2,1,0:T(8,128)S(1)}, f32[8,2048]{1,0:T(8,128)S(1)}) custom-call(bf16[4,128,2048]{2,1,0:T(8,128)(2,1)S(1)} %dlogit.3.refs_0_.refs_6_, bf16[4,128,2048]{2,1,0:T(8,128)(2,1)S(1)} %collective-permute-done.34.refs_1_, bf16[2048,2048]{1,0:T(8,128)(2,1)S(1)} %get-tuple-element.53.refs_6_.refs_2_, ...), custom_call_target="tpu_custom_call" | custom-call | bytes 16777216 | tf_op jit(solution)/shard_map/dnormed/pallas_call | solution.py:57
  170.3 4.7 %all-to-all-start = ((f32[32,8,256]{2,1,0:T(8,128)}), f32[32,8,256]{2,1,0:T(8,128)S(1)}, u32[]{:S(2)}, u32[]{:S(2)}) async-start(f32[32,8,256]{2,1,0:T(8,128)} %gain_parts.1), calls=%async_computation | async-start | bytes 524288 | tf_op jit(solution)/shard_map/all_to_all | solution.py:679
  175.0 9.8 %head_grad.3 = (bf16[2048,2048]{1,0:T(8,128)(2,1)}, f32[8,128]{1,0:T(8,128)S(1)}) custom-call(bf16[4,32,2176]{2,1,0:T(8,128)(2,1)} %copy-done.3, bf16[4,64,2176]{2,1,0:T(8,128)(2,1)} %bitcast.28, bf16[4,32,2176]{2,1,0:T(8,128)(2,1)} %copy-done.4, bf16[4,32,2176]{2,1,0:T(8,128)(2,1)} %copy-done.6, bf16[4,64,2176]{2,1,0:T(8,128)(2,1)} %copy-done.1, ...), custom_call_target="tpu_custom_call" | custom-call | flops 4294967296 | bytes 12582912 | tf_op jit(solution)/shard_map/head_grad/pallas_call | solution.py:57
  185.6 1.5 over_x.1
  188.2 2.7 %collective-permute-start.39 = (bf16[32,2048]{1,0:T(8,128)(2,1)S(1)}, bf16[32,2048]{1,0:T(8,128)(2,1)S(1)}, u32[]{:S(2)}, u32[]{:S(2)}) collective-permute-start(bf16[32,2048]{1,0:T(8,128)(2,1)S(1)} %get-tuple-element.76), channel_id=1, source_target_pairs={{0,16},{1,17},{2,18},{3,19},{4,20},{5,21},{6,22},{7,23},{8,24},{9,... | collective-permute-start | bytes 393224 | tf_op jit(solution)/shard_map/ppermute | solution.py:32
  190.9 1.9 collective-permute-start.40
  192.8 6.9 %head_grad.4 = (bf16[2048,2048]{1,0:T(8,128)(2,1)}, f32[8,128]{1,0:T(8,128)S(1)}) custom-call(bf16[4,32,2176]{2,1,0:T(8,128)(2,1)} %copy-done.3, bf16[4,64,2176]{2,1,0:T(8,128)(2,1)} %bitcast.29, bf16[4,32,2176]{2,1,0:T(8,128)(2,1)} %copy-done.4, bf16[4,32,2176]{2,1,0:T(8,128)(2,1)} %copy-done.6, ...), custom_call_target="tpu_custom_call", output_to_operand_aliasing={{0}: (8, {})} | custom-call | flops 2147483648 | bytes 12582912 | tf_op jit(solution)/shard_map/head_grad/pallas_call | solution.py:57
  199.8 1.5 over_y.1.refs_9_
  201.3 3.5 %all-to-all-start.1 = ((f32[4,16,2048]{2,1,0:T(8,128)}), f32[4,16,2048]{2,1,0:T(8,128)S(1)}, u32[]{:S(2)}, u32[]{:S(2)}) async-start(f32[4,16,2048]{2,1,0:T(8,128)} %over_y.1.refs_9_), calls=%async_computation.1 | async-start | bytes 1048576 | tf_op jit(solution)/shard_map/all_to_all | solution.py:686
  204.8 7.0 %head_grad.5 = (bf16[2048,2048]{1,0:T(8,128)(2,1)}, f32[8,128]{1,0:T(8,128)S(1)}) custom-call(bf16[4,32,2176]{2,1,0:T(8,128)(2,1)} %copy-done.3, bf16[4,64,2176]{2,1,0:T(8,128)(2,1)} %bitcast.30, bf16[4,32,2176]{2,1,0:T(8,128)(2,1)} %copy-done.4, bf16[4,32,2176]{2,1,0:T(8,128)(2,1)} %copy-done.6, ...), custom_call_target="tpu_custom_call", output_to_operand_aliasing={{0}: (8, {})} | custom-call | flops 2147483648 | bytes 12582912 | tf_op jit(solution)/shard_map/head_grad/pallas_call | solution.py:57
  211.8 2.0 all-to-all-done.1.refs_2_
  (101 shorter events, 30.4 us)
Async XLA Ops:
  2.5 6.0 %collective-permute-start.2 = (bf16[8,2176]{1,0:T(8,128)(2,1)S(1)}, bf16[8,2176]{1,0:T(8,128)(2,1)S(1)}, u32[]{:S(2)}, u32[]{:S(2)}) collective-permute-start(bf16[8,2176]{1,0:T(8,128)(2,1)S(1)} %get-tuple-element.48), channel_id=1, source_target_pairs={{0,32},{32,64},{64,96},{96,0},{1,33},{33,65},{65,97},{97,1},{2,34}... | collective-permute-start | bytes 104456 | tf_op jit(solution)/shard_map/ppermute | solution.py:22
  4.2 5.4 %collective-permute-start.1 = (bf16[8,2176]{1,0:T(8,128)(2,1)S(1)}, bf16[8,2176]{1,0:T(8,128)(2,1)S(1)}, u32[]{:S(2)}, u32[]{:S(2)}) collective-permute-start(bf16[8,2176]{1,0:T(8,128)(2,1)S(1)} %get-tuple-element.47), channel_id=1, source_target_pairs={{0,64},{32,96},{64,0},{96,32},{1,65},{33,97},{65,1},{97,33},{2,66}... | collective-permute-start | bytes 104456 | tf_op jit(solution)/shard_map/ppermute | solution.py:22
  7.1 3.9 %collective-permute-start = (bf16[8,2176]{1,0:T(8,128)(2,1)S(1)}, bf16[8,2176]{1,0:T(8,128)(2,1)S(1)}, u32[]{:S(2)}, u32[]{:S(2)}) collective-permute-start(bf16[8,2176]{1,0:T(8,128)(2,1)S(1)} %get-tuple-element.46), channel_id=1, source_target_pairs={{0,96},{32,0},{64,32},{96,64},{1,97},{33,1},{65,33},{97,65},{2,98}... | collective-permute-start | bytes 104456 | tf_op jit(solution)/shard_map/ppermute | solution.py:22
  11.1 9.8 %collective-permute-start.7 = (bf16[4,8,2176]{2,1,0:T(8,128)(2,1)S(1)}, bf16[4,8,2176]{2,1,0:T(8,128)(2,1)S(1)}, u32[]{:S(2)}, u32[]{:S(2)}) collective-permute-start(bf16[4,8,2176]{2,1,0:T(8,128)(2,1)S(1)} %pad_maximum_fusion.3.refs_1_), channel_id=1, source_target_pairs={{0,2},{1,3},{2,4},{3,5},{4,6},{5,7},{6,0},{7,1},{8,10},{9,11},{10,... | collective-permute-start | bytes 417800 | tf_op jit(solution)/shard_map/ppermute | solution.py:32
  13.1 7.9 %collective-permute-start.6 = (bf16[4,8,2176]{2,1,0:T(8,128)(2,1)S(1)}, bf16[4,8,2176]{2,1,0:T(8,128)(2,1)S(1)}, u32[]{:S(2)}, u32[]{:S(2)}) collective-permute-start(bf16[4,8,2176]{2,1,0:T(8,128)(2,1)S(1)} %pad_maximum_fusion.3.refs_1_), channel_id=1, source_target_pairs={{0,6},{1,7},{2,0},{3,1},{4,2},{5,3},{6,4},{7,5},{8,14},{9,15},{10,... | collective-permute-start | bytes 417800 | tf_op jit(solution)/shard_map/ppermute | solution.py:32
  15.3 8.4 %collective-permute-start.5 = (bf16[4,8,2176]{2,1,0:T(8,128)(2,1)S(1)}, bf16[4,8,2176]{2,1,0:T(8,128)(2,1)S(1)}, u32[]{:S(2)}, u32[]{:S(2)}) collective-permute-start(bf16[4,8,2176]{2,1,0:T(8,128)(2,1)S(1)} %pad_maximum_fusion.3.refs_1_), channel_id=1, source_target_pairs={{0,8},{1,9},{2,10},{3,11},{4,12},{5,13},{6,14},{7,15},{8,16},{9,17... | collective-permute-start | bytes 417800 | tf_op jit(solution)/shard_map/ppermute | solution.py:32
  16.8 9.1 %collective-permute-start.4 = (bf16[4,8,2176]{2,1,0:T(8,128)(2,1)S(1)}, bf16[4,8,2176]{2,1,0:T(8,128)(2,1)S(1)}, u32[]{:S(2)}, u32[]{:S(2)}) collective-permute-start(bf16[4,8,2176]{2,1,0:T(8,128)(2,1)S(1)} %pad_maximum_fusion.3.refs_1_), channel_id=1, source_target_pairs={{0,16},{1,17},{2,18},{3,19},{4,20},{5,21},{6,22},{7,23},{8,24},{9,... | collective-permute-start | bytes 417800 | tf_op jit(solution)/shard_map/ppermute | solution.py:32
  19.5 7.4 %collective-permute-start.3 = (bf16[4,8,2176]{2,1,0:T(8,128)(2,1)S(1)}, bf16[4,8,2176]{2,1,0:T(8,128)(2,1)S(1)}, u32[]{:S(2)}, u32[]{:S(2)}) collective-permute-start(bf16[4,8,2176]{2,1,0:T(8,128)(2,1)S(1)} %pad_maximum_fusion.3.refs_1_), channel_id=1, source_target_pairs={{0,24},{1,25},{2,26},{3,27},{4,28},{5,29},{6,30},{7,31},{8,0},{9,1... | collective-permute-start | bytes 417800 | tf_op jit(solution)/shard_map/ppermute | solution.py:32
  21.0 11.9 %collective-permute-start.8 = (bf16[4,2,8,2176]{3,2,0,1:T(8,128)(2,1)S(1)}, bf16[4,2,8,2176]{3,2,0,1:T(8,128)(2,1)S(1)}, u32[]{:S(2)}, u32[]{:S(2)}) collective-permute-start(bf16[4,2,8,2176]{3,2,0,1:T(8,128)(2,1)S(1)} %pad_maximum_fusion.2), channel_id=1, source_target_pairs={{0,24},{1,25},{2,26},{3,27},{4,28},{5,29},{6,30},{7,31},{8,0},{9,1... | collective-permute-start | bytes 835592 | tf_op jit(solution)/shard_map/ppermute | solution.py:32
  21.1 11.8 %collective-permute-start.9 = (bf16[4,2,8,2176]{3,2,0,1:T(8,128)(2,1)S(1)}, bf16[4,2,8,2176]{3,2,0,1:T(8,128)(2,1)S(1)}, u32[]{:S(2)}, u32[]{:S(2)}) collective-permute-start(bf16[4,2,8,2176]{3,2,0,1:T(8,128)(2,1)S(1)} %pad_maximum_fusion.2), channel_id=1, source_target_pairs={{0,16},{1,17},{2,18},{3,19},{4,20},{5,21},{6,22},{7,23},{8,24},{9,... | collective-permute-start | bytes 835592 | tf_op jit(solution)/shard_map/ppermute | solution.py:32
  23.7 12.4 %collective-permute-start.10 = (bf16[4,2,8,2176]{3,2,0,1:T(8,128)(2,1)S(1)}, bf16[4,2,8,2176]{3,2,0,1:T(8,128)(2,1)S(1)}, u32[]{:S(2)}, u32[]{:S(2)}) collective-permute-start(bf16[4,2,8,2176]{3,2,0,1:T(8,128)(2,1)S(1)} %pad_maximum_fusion.2), channel_id=1, source_target_pairs={{0,8},{1,9},{2,10},{3,11},{4,12},{5,13},{6,14},{7,15},{8,16},{9,17... | collective-permute-start | bytes 835592 | tf_op jit(solution)/shard_map/ppermute | solution.py:32
  27.0 134.5 %copy-start.3 = (bf16[4,32,2176]{2,1,0:T(8,128)(2,1)}, bf16[4,32,2176]{2,1,0:T(8,128)(2,1)S(1)}, u32[]{:S(2)}) copy-start(bf16[4,32,2176]{2,1,0:T(8,128)(2,1)S(1)} %pad_maximum_fusion.1.refs_0_.refs_4_.refs_9_) | copy-start | bytes 1671172
  27.0 11.1 %collective-permute-start.11 = (bf16[4,32,2176]{2,1,0:T(8,128)(2,1)S(1)}, bf16[4,32,2176]{2,1,0:T(8,128)(2,1)S(1)}, u32[]{:S(2)}, u32[]{:S(2)}) collective-permute-start(bf16[4,32,2176]{2,1,0:T(8,128)(2,1)S(1)} %pad_maximum_fusion.1.refs_0_.refs_4_.refs_9_), channel_id=1, source_target_pairs={{0,4},{1,5},{2,6},{3,7},{4,0},{5,1},{6,2},{7,3},{8,12},{9,13},{10,... | collective-permute-start | bytes 1671176 | tf_op jit(solution)/shard_map/ppermute | solution.py:32
  36.4 110.2 %copy-start = (bf16[4,2,4,8,2176]{4,3,2,1,0:T(8,128)(2,1)}, bf16[4,2,4,8,2176]{4,3,2,1,0:T(8,128)(2,1)S(1)}, u32[]{:S(2)}) copy-start(bf16[4,2,4,8,2176]{4,3,2,1,0:T(8,128)(2,1)S(1)} %copy.13) | copy-start | bytes 3342340
  36.4 5.9 %collective-permute-start.13 = (bf16[4,64,2176]{2,1,0:T(8,128)(2,1)S(1)}, bf16[4,64,2176]{2,1,0:T(8,128)(2,1)S(1)}, u32[]{:S(2)}, u32[]{:S(2)}) collective-permute-start(bf16[4,64,2176]{2,1,0:T(8,128)(2,1)S(1)} %bitcast.21), channel_id=1, source_target_pairs={{0,1},{1,0},{2,3},{3,2},{4,5},{5,4},{6,7},{7,6},{8,9},{9,8},{10,11... | collective-permute-start | bytes 3342344 | tf_op jit(solution)/shard_map/ppermute | solution.py:32
  36.5 5.8 %collective-permute-start.12 = (bf16[4,32,2176]{2,1,0:T(8,128)(2,1)S(1)}, bf16[4,32,2176]{2,1,0:T(8,128)(2,1)S(1)}, u32[]{:S(2)}, u32[]{:S(2)}) collective-permute-start(bf16[4,32,2176]{2,1,0:T(8,128)(2,1)S(1)} %pad_maximum_fusion.1.refs_0_.refs_4_.refs_9_), channel_id=1, source_target_pairs={{0,1},{1,0},{2,3},{3,2},{4,5},{5,4},{6,7},{7,6},{8,9},{9,8},{10,11... | collective-permute-start | bytes 1671176 | tf_op jit(solution)/shard_map/ppermute | solution.py:32
  38.1 108.5 %copy-start.4 = (bf16[4,32,2176]{2,1,0:T(8,128)(2,1)}, bf16[4,32,2176]{2,1,0:T(8,128)(2,1)S(1)}, u32[]{:S(2)}) copy-start(bf16[4,32,2176]{2,1,0:T(8,128)(2,1)S(1)} %collective-permute-done.11.refs_2_.refs_6_.refs_11_.refs_5_) | copy-start | bytes 1671172
  38.1 4.2 %collective-permute-start.14 = (bf16[4,32,2176]{2,1,0:T(8,128)(2,1)S(1)}, bf16[4,32,2176]{2,1,0:T(8,128)(2,1)S(1)}, u32[]{:S(2)}, u32[]{:S(2)}) collective-permute-start(bf16[4,32,2176]{2,1,0:T(8,128)(2,1)S(1)} %collective-permute-done.11.refs_2_.refs_6_.refs_11_.refs_5_), channel_id=1, source_target_pairs={{0,1},{1,0},{2,3},{3,2},{4,5},{5,4},{6,7},{7,6},{8,9},{9,8},{10,11... | collective-permute-start | bytes 1671176 | tf_op jit(solution)/shard_map/ppermute | solution.py:32
  42.3 97.9 %copy-start.6 = (bf16[4,32,2176]{2,1,0:T(8,128)(2,1)}, bf16[4,32,2176]{2,1,0:T(8,128)(2,1)S(1)}, u32[]{:S(2)}) copy-start(bf16[4,32,2176]{2,1,0:T(8,128)(2,1)S(1)} %collective-permute-done.12.refs_3_.refs_7_.refs_9_) | copy-start | bytes 1671172
  42.3 97.9 %copy-start.7 = (bf16[4,32,2176]{2,1,0:T(8,128)(2,1)}, bf16[4,32,2176]{2,1,0:T(8,128)(2,1)S(1)}, u32[]{:S(2)}) copy-start(bf16[4,32,2176]{2,1,0:T(8,128)(2,1)S(1)} %collective-permute-done.14.refs_5_.refs_9_.refs_11_) | copy-start | bytes 1671172
  46.9 50.1 %collective-permute-start.19 = (bf16[2048,2048]{1,0:T(8,128)(2,1)}, bf16[2048,2048]{1,0:T(8,128)(2,1)}, u32[]{:S(2)}, u32[]{:S(2)}) collective-permute-start(bf16[2048,2048]{1,0:T(8,128)(2,1)} %refs_0_.2), channel_id=1, source_target_pairs={{0,1},{1,0},{2,3},{3,2},{4,5},{5,4},{6,7},{7,6},{8,9},{9,8},{10,11... | collective-permute-start | bytes 25165832 | tf_op jit(solution)/shard_map/ppermute | solution.py:32
  47.3 15.9 %collective-permute-start.15 = (s16[128,2176]{1,0:T(8,128)(2,1)S(1)}, s16[128,2176]{1,0:T(8,128)(2,1)S(1)}, u32[]{:S(2)}, u32[]{:S(2)}) collective-permute-start(s16[128,2176]{1,0:T(8,128)(2,1)S(1)} %get-tuple-element.54.refs_7_), channel_id=1, source_target_pairs={{0,32},{32,64},{64,96},{96,0},{1,33},{33,65},{65,97},{97,1},{2,34}... | collective-permute-start | bytes 1671176 | tf_op jit(solution)/shard_map/ppermute | solution.py:22
  47.4 15.8 %collective-permute-start.16 = (s16[128,2176]{1,0:T(8,128)(2,1)S(1)}, s16[128,2176]{1,0:T(8,128)(2,1)S(1)}, u32[]{:S(2)}, u32[]{:S(2)}) collective-permute-start(s16[128,2176]{1,0:T(8,128)(2,1)S(1)} %get-tuple-element.57), channel_id=1, source_target_pairs={{0,96},{32,0},{64,32},{96,64},{1,97},{33,1},{65,33},{97,65},{2,98}... | collective-permute-start | bytes 1671176 | tf_op jit(solution)/shard_map/ppermute | solution.py:22
  64.3 27.1 %collective-permute-start.17 = (s16[256,2176]{1,0:T(8,128)(2,1)S(1)}, s16[256,2176]{1,0:T(8,128)(2,1)S(1)}, u32[]{:S(2)}, u32[]{:S(2)}) collective-permute-start(s16[256,2176]{1,0:T(8,128)(2,1)S(1)} %get-tuple-element.58.refs_7_), channel_id=1, source_target_pairs={{0,32},{32,64},{64,96},{96,0},{1,33},{33,65},{65,97},{97,1},{2,34}... | collective-permute-start | bytes 3342344 | tf_op jit(solution)/shard_map/ppermute | solution.py:22
  65.2 26.2 %collective-permute-start.18 = (s16[256,2176]{1,0:T(8,128)(2,1)S(1)}, s16[256,2176]{1,0:T(8,128)(2,1)S(1)}, u32[]{:S(2)}, u32[]{:S(2)}) collective-permute-start(s16[256,2176]{1,0:T(8,128)(2,1)S(1)} %get-tuple-element.59), channel_id=1, source_target_pairs={{0,96},{32,0},{64,32},{96,64},{1,97},{33,1},{65,33},{97,65},{2,98}... | collective-permute-start | bytes 3342344 | tf_op jit(solution)/shard_map/ppermute | solution.py:22
  93.9 23.8 %collective-permute-start.30 = (bf16[2,128,2048]{2,1,0:T(8,128)(2,1)S(1)}, bf16[2,128,2048]{2,1,0:T(8,128)(2,1)S(1)}, u32[]{:S(2)}, u32[]{:S(2)}) collective-permute-start(bf16[2,128,2048]{2,1,0:T(8,128)(2,1)S(1)} %get-tuple-element.63.refs_5_), channel_id=1, source_target_pairs={{0,96},{32,0},{64,32},{96,64},{1,97},{33,1},{65,33},{97,65},{2,98}... | collective-permute-start | bytes 3145736 | tf_op jit(solution)/shard_map/ppermute | solution.py:22
  96.9 24.2 %collective-permute-start.31 = (bf16[2,128,2048]{2,1,0:T(8,128)(2,1)S(1)}, bf16[2,128,2048]{2,1,0:T(8,128)(2,1)S(1)}, u32[]{:S(2)}, u32[]{:S(2)}) collective-permute-start(bf16[2,128,2048]{2,1,0:T(8,128)(2,1)S(1)} %get-tuple-element.63.refs_5_), channel_id=1, source_target_pairs={{0,32},{32,64},{64,96},{96,0},{1,33},{33,65},{65,97},{97,1},{2,34}... | collective-permute-start | bytes 3145736 | tf_op jit(solution)/shard_map/ppermute | solution.py:22
  101.0 1.2 collective-permute-start.20
  102.3 4.6 %collective-permute-start.21 = (f32[8,256]{1,0:T(8,128)S(1)}, f32[8,256]{1,0:T(8,128)S(1)}, u32[]{:S(2)}, u32[]{:S(2)}) collective-permute-start(f32[8,256]{1,0:T(8,128)S(1)} %merge_statistics.2.refs_0_), channel_id=1, source_target_pairs={{0,24},{1,25},{2,26},{3,27},{4,28},{5,29},{6,30},{7,31},{8,0},{9,1... | collective-permute-start | bytes 24584 | tf_op jit(solution)/shard_map/ppermute | solution.py:32
  104.7 5.2 %collective-permute-start.22 = (f32[8,256]{1,0:T(8,128)S(1)}, f32[8,256]{1,0:T(8,128)S(1)}, u32[]{:S(2)}, u32[]{:S(2)}) collective-permute-start(f32[8,256]{1,0:T(8,128)S(1)} %merge_statistics.2.refs_0_), channel_id=1, source_target_pairs={{0,16},{1,17},{2,18},{3,19},{4,20},{5,21},{6,22},{7,23},{8,24},{9,... | collective-permute-start | bytes 24584 | tf_op jit(solution)/shard_map/ppermute | solution.py:32
  105.5 4.9 %collective-permute-start.23 = (f32[8,256]{1,0:T(8,128)S(1)}, f32[8,256]{1,0:T(8,128)S(1)}, u32[]{:S(2)}, u32[]{:S(2)}) collective-permute-start(f32[8,256]{1,0:T(8,128)S(1)} %merge_statistics.2.refs_0_), channel_id=1, source_target_pairs={{0,8},{1,9},{2,10},{3,11},{4,12},{5,13},{6,14},{7,15},{8,16},{9,17... | collective-permute-start | bytes 24584 | tf_op jit(solution)/shard_map/ppermute | solution.py:32
  121.2 19.1 %collective-permute-start.32 = (bf16[128,2048]{1,0:T(8,128)(2,1)S(1)}, bf16[128,2048]{1,0:T(8,128)(2,1)S(1)}, u32[]{:S(2)}, u32[]{:S(2)}) collective-permute-start(bf16[128,2048]{1,0:T(8,128)(2,1)S(1)} %get-tuple-element.64), channel_id=1, source_target_pairs={{0,32},{32,64},{64,96},{96,0},{1,33},{33,65},{65,97},{97,1},{2,34}... | collective-permute-start | bytes 1572872 | tf_op jit(solution)/shard_map/ppermute | solution.py:22
  121.3 19.0 %collective-permute-start.33 = (bf16[128,2048]{1,0:T(8,128)(2,1)S(1)}, bf16[128,2048]{1,0:T(8,128)(2,1)S(1)}, u32[]{:S(2)}, u32[]{:S(2)}) collective-permute-start(bf16[128,2048]{1,0:T(8,128)(2,1)S(1)} %get-tuple-element.65), channel_id=1, source_target_pairs={{0,96},{32,0},{64,32},{96,64},{1,97},{33,1},{65,33},{97,65},{2,98}... | collective-permute-start | bytes 1572872 | tf_op jit(solution)/shard_map/ppermute | solution.py:22
  125.3 4.5 %collective-permute-start.24 = (f32[8,256]{1,0:T(8,128)S(1)}, f32[8,256]{1,0:T(8,128)S(1)}, u32[]{:S(2)}, u32[]{:S(2)}) collective-permute-start(f32[8,256]{1,0:T(8,128)S(1)} %merge_statistics.3.refs_2_), channel_id=1, source_target_pairs={{0,6},{1,7},{2,0},{3,1},{4,2},{5,3},{6,4},{7,5},{8,14},{9,15},{10,... | collective-permute-start | bytes 24584 | tf_op jit(solution)/shard_map/ppermute | solution.py:32
  127.3 5.2 %collective-permute-start.25 = (f32[8,256]{1,0:T(8,128)S(1)}, f32[8,256]{1,0:T(8,128)S(1)}, u32[]{:S(2)}, u32[]{:S(2)}) collective-permute-start(f32[8,256]{1,0:T(8,128)S(1)} %merge_statistics.3.refs_2_), channel_id=1, source_target_pairs={{0,4},{1,5},{2,6},{3,7},{4,0},{5,1},{6,2},{7,3},{8,12},{9,13},{10,... | collective-permute-start | bytes 24584 | tf_op jit(solution)/shard_map/ppermute | solution.py:32
  127.3 5.2 %collective-permute-start.26 = (f32[8,256]{1,0:T(8,128)S(1)}, f32[8,256]{1,0:T(8,128)S(1)}, u32[]{:S(2)}, u32[]{:S(2)}) collective-permute-start(f32[8,256]{1,0:T(8,128)S(1)} %merge_statistics.3.refs_2_), channel_id=1, source_target_pairs={{0,2},{1,3},{2,4},{3,5},{4,6},{5,7},{6,0},{7,1},{8,10},{9,11},{10,... | collective-permute-start | bytes 24584 | tf_op jit(solution)/shard_map/ppermute | solution.py:32
  133.9 3.7 %collective-permute-start.27 = (f32[8,256]{1,0:T(8,128)S(1)}, f32[8,256]{1,0:T(8,128)S(1)}, u32[]{:S(2)}, u32[]{:S(2)}) collective-permute-start(f32[8,256]{1,0:T(8,128)S(1)} %combine_statistics.1.refs_1_.refs_6_), channel_id=1, source_target_pairs={{0,96},{32,0},{64,32},{96,64},{1,97},{33,1},{65,33},{97,65},{2,98}... | collective-permute-start | bytes 24584 | tf_op jit(solution)/shard_map/ppermute | solution.py:22
  133.9 5.2 %collective-permute-start.28 = (f32[8,256]{1,0:T(8,128)S(1)}, f32[8,256]{1,0:T(8,128)S(1)}, u32[]{:S(2)}, u32[]{:S(2)}) collective-permute-start(f32[8,256]{1,0:T(8,128)S(1)} %combine_statistics.1.refs_1_.refs_6_), channel_id=1, source_target_pairs={{0,64},{32,96},{64,0},{96,32},{1,65},{33,97},{65,1},{97,33},{2,66}... | collective-permute-start | bytes 24584 | tf_op jit(solution)/shard_map/ppermute | solution.py:22
  134.8 5.4 %collective-permute-start.29 = (f32[8,256]{1,0:T(8,128)S(1)}, f32[8,256]{1,0:T(8,128)S(1)}, u32[]{:S(2)}, u32[]{:S(2)}) collective-permute-start(f32[8,256]{1,0:T(8,128)S(1)} %combine_statistics.1.refs_1_.refs_6_), channel_id=1, source_target_pairs={{0,32},{32,64},{64,96},{96,0},{1,33},{33,65},{65,97},{97,1},{2,34}... | collective-permute-start | bytes 24584 | tf_op jit(solution)/shard_map/ppermute | solution.py:22
  142.4 4.2 %collective-permute-start.34 = (bf16[4,128,2048]{2,1,0:T(8,128)(2,1)S(1)}, bf16[4,128,2048]{2,1,0:T(8,128)(2,1)S(1)}, u32[]{:S(2)}, u32[]{:S(2)}) collective-permute-start(bf16[4,128,2048]{2,1,0:T(8,128)(2,1)S(1)} %dlogit.2.refs_12_.refs_7_), channel_id=1, source_target_pairs={{0,1},{1,0},{2,3},{3,2},{4,5},{5,4},{6,7},{7,6},{8,9},{9,8},{10,11... | collective-permute-start | bytes 6291464 | tf_op jit(solution)/shard_map/ppermute | solution.py:32
  156.3 28.6 %collective-permute-start.35 = (bf16[4,32,2048]{2,1,0:T(8,128)(2,1)}, bf16[4,32,2048]{2,1,0:T(8,128)(2,1)S(1)}, u32[]{:S(2)}, u32[]{:S(2)}) collective-permute-start(bf16[4,32,2048]{2,1,0:T(8,128)(2,1)} %get-tuple-element.69), channel_id=1, source_target_pairs={{0,4},{1,5},{2,6},{3,7},{4,0},{5,1},{6,2},{7,3},{8,12},{9,13},{10,... | collective-permute-start | bytes 1572872 | tf_op jit(solution)/shard_map/ppermute | solution.py:32
  158.3 27.3 %collective-permute-start.36 = (bf16[4,32,2048]{2,1,0:T(8,128)(2,1)}, bf16[4,32,2048]{2,1,0:T(8,128)(2,1)}, u32[]{:S(2)}, u32[]{:S(2)}) collective-permute-start(bf16[4,32,2048]{2,1,0:T(8,128)(2,1)} %get-tuple-element.70), channel_id=1, source_target_pairs={{0,2},{1,3},{2,4},{3,5},{4,6},{5,7},{6,0},{7,1},{8,10},{9,11},{10,... | collective-permute-start | bytes 1572872 | tf_op jit(solution)/shard_map/ppermute | solution.py:32
  158.3 27.3 %collective-permute-start.37 = (bf16[4,32,2048]{2,1,0:T(8,128)(2,1)}, bf16[4,32,2048]{2,1,0:T(8,128)(2,1)}, u32[]{:S(2)}, u32[]{:S(2)}) collective-permute-start(bf16[4,32,2048]{2,1,0:T(8,128)(2,1)} %get-tuple-element.71), channel_id=1, source_target_pairs={{0,6},{1,7},{2,0},{3,1},{4,2},{5,3},{6,4},{7,5},{8,14},{9,15},{10,... | collective-permute-start | bytes 1572872 | tf_op jit(solution)/shard_map/ppermute | solution.py:32
  170.3 29.5 %all-to-all-start = ((f32[32,8,256]{2,1,0:T(8,128)}), f32[32,8,256]{2,1,0:T(8,128)S(1)}, u32[]{:S(2)}, u32[]{:S(2)}) async-start(f32[32,8,256]{2,1,0:T(8,128)} %gain_parts.1), calls=%async_computation | async-start | bytes 524288 | tf_op jit(solution)/shard_map/all_to_all | solution.py:679
  187.1 12.7 %collective-permute-start.38 = (bf16[32,2048]{1,0:T(8,128)(2,1)S(1)}, bf16[32,2048]{1,0:T(8,128)(2,1)S(1)}, u32[]{:S(2)}, u32[]{:S(2)}) collective-permute-start(bf16[32,2048]{1,0:T(8,128)(2,1)S(1)} %get-tuple-element.75), channel_id=1, source_target_pairs={{0,8},{1,9},{2,10},{3,11},{4,12},{5,13},{6,14},{7,15},{8,16},{9,17... | collective-permute-start | bytes 393224 | tf_op jit(solution)/shard_map/ppermute | solution.py:32
  188.2 11.6 %collective-permute-start.39 = (bf16[32,2048]{1,0:T(8,128)(2,1)S(1)}, bf16[32,2048]{1,0:T(8,128)(2,1)S(1)}, u32[]{:S(2)}, u32[]{:S(2)}) collective-permute-start(bf16[32,2048]{1,0:T(8,128)(2,1)S(1)} %get-tuple-element.76), channel_id=1, source_target_pairs={{0,16},{1,17},{2,18},{3,19},{4,20},{5,21},{6,22},{7,23},{8,24},{9,... | collective-permute-start | bytes 393224 | tf_op jit(solution)/shard_map/ppermute | solution.py:32
  190.9 8.9 %collective-permute-start.40 = (bf16[32,2048]{1,0:T(8,128)(2,1)S(1)}, bf16[32,2048]{1,0:T(8,128)(2,1)S(1)}, u32[]{:S(2)}, u32[]{:S(2)}) collective-permute-start(bf16[32,2048]{1,0:T(8,128)(2,1)S(1)} %get-tuple-element.77), channel_id=1, source_target_pairs={{0,24},{1,25},{2,26},{3,27},{4,28},{5,29},{6,30},{7,31},{8,0},{9,1... | collective-permute-start | bytes 393224 | tf_op jit(solution)/shard_map/ppermute | solution.py:32
  201.3 12.4 %all-to-all-start.1 = ((f32[4,16,2048]{2,1,0:T(8,128)}), f32[4,16,2048]{2,1,0:T(8,128)S(1)}, u32[]{:S(2)}, u32[]{:S(2)}) async-start(f32[4,16,2048]{2,1,0:T(8,128)} %over_y.1.refs_9_), calls=%async_computation.1 | async-start | bytes 1048576 | tf_op jit(solution)/shard_map/all_to_all | solution.py:686
  (10 other events, 194.2 us)

commit v3 on v2

--- a/solution.py
+++ b/solution.py
@@ -430,16 +430,14 @@
     )
 
 
-def dnormed_kernel(first, count, left, right, head, other, *refs):
+def dnormed_kernel(count, left, right, head, other, *refs):
     normed, outs, gain = refs[: -1 - count], refs[-1 - count : -1], refs[-1]
     columns = head.shape[1]
     dims = (((1,), (1,)), ((), ()))
     cut = pl.ds(pl.multiple_of(pl.program_id(0) * TILE, TILE), TILE)
-    span = outs[0].shape[1]
-    rows = pl.ds(first, count * span)
-    part = lax.dot_general(left[:, rows, :].reshape(-1, columns), head[cut, :], dims, preferred_element_type=F32)
+    part = lax.dot_general(left[...].reshape(-1, columns), head[cut, :], dims, preferred_element_type=F32)
     part = part + lax.dot_general(
-        right[:, rows, :].reshape(-1, columns), other[cut, :], dims, preferred_element_type=F32
+        right[...].reshape(-1, columns), other[cut, :], dims, preferred_element_type=F32
     )
     x = jnp.concatenate([n[...] for n in normed], axis=1).reshape(part.shape).astype(F32)
     gain[...] = jnp.sum((part * x).reshape(-1, 8, TILE), axis=0)
@@ -448,16 +446,16 @@
         outs[k][...] = part[:, k].astype(outs[k].dtype)
 
 
-def dnormed_of(first, left, right, head, other, normed, span, dtype, after=()):
+def dnormed_of(left, right, head, other, normed, span, after=()):
     depth, columns = head.shape
     count = sum(n.shape[1] for n in normed) // span
     block = pl.BlockSpec((SIDE, span, TILE), lambda j: (0, 0, j))
     return launch(
-        functools.partial(dnormed_kernel, first, count),
+        functools.partial(dnormed_kernel, count),
         (left, right, in_vmem(head), in_vmem(other), *normed),
         after,
         grid=(depth // TILE,),
-        out_shape=[shape(SIDE, span, depth, dtype=dtype)] * count + [shape(8, depth)],
+        out_shape=[shape(SIDE, span, depth, dtype=BF16 if k else F32) for k in range(count)] + [shape(8, depth)],
         in_specs=[VMEM] * 4 + [pl.BlockSpec((SIDE, n.shape[1], TILE), lambda j: (0, 0, j)) for n in normed],
         out_specs=[block] * count + [pl.BlockSpec((8, TILE), lambda j: (0, j))],
         cost_estimate=cost(0, 4 * depth * columns),
@@ -484,45 +482,37 @@
     out[...] = lax.dot_general(x, y, (((0,), (0,)), ((), ())), preferred_element_type=F32).astype(BF16)
 
 
-def head_grad_of(pieces, ours, others, depth, start, stop, into=None, after=()):
+def head_grad_of(pieces, ours, others, depth, after=()):
     columns, rows = ours.shape[2], 2 * SIDE * ours.shape[1]
-    inputs = [in_hbm(x) for x in (*pieces, ours, others)]
-    specs = [pl.BlockSpec((SIDE, p.shape[1], TILE), lambda j: (0, 0, start + j)) for p in pieces] + [ANY] * 2
-    aliases = {}
-    if into is not None:
-        aliases = {len(inputs): 0}
-        inputs.append(in_hbm(into))
-        specs.append(ANY)
     return launch(
         functools.partial(head_grad_kernel, len(pieces)),
-        (*inputs,),
-        after,
-        grid=(stop - start,),
-        input_output_aliases=aliases,
+        tuple(in_hbm(x) for x in (*pieces, ours, others)),
+        after,
+        grid=(depth // TILE,),
         out_shape=[shape(depth, columns, dtype=BF16), shape(8, TAIL)],
-        in_specs=specs,
-        out_specs=[pl.BlockSpec((TILE, columns), lambda j: (start + j, 0)), pl.BlockSpec((8, TAIL), lambda j: (0, 0))],
+        in_specs=[pl.BlockSpec((SIDE, p.shape[1], TILE), lambda j: (0, 0, j)) for p in pieces] + [ANY] * 2,
+        out_specs=[pl.BlockSpec((TILE, columns), lambda j: (j, 0)), pl.BlockSpec((8, TAIL), lambda j: (0, 0))],
         scratch_shapes=[pltpu.VMEM((SIDE, 2, *ours.shape[1:]), BF16), pltpu.SemaphoreType.DMA((2,))],
-        cost_estimate=cost(2 * rows * (stop - start) * TILE * columns, depth * columns + 4 * rows * depth),
+        cost_estimate=cost(2 * rows * depth * columns, 2 * depth * columns + 4 * rows * depth),
         name="head_grad",
     )
 
 
-def spread_kernel(near, own, out):
-    gain = jnp.sum(near[...] + own[...], axis=0, keepdims=True)
+def spread_kernel(terms, out):
+    gain = jnp.sum(terms[...], axis=0, keepdims=True)
     wide = out.shape[2]
     gain = jnp.concatenate([gain[:, i * wide : (i + 1) * wide] for i in range(out.shape[1])], axis=0)
     out[...] = jnp.broadcast_to(gain, out.shape)
 
 
-def spread(near, own, after=()):
-    rows, depth = near.shape
+def spread(terms, after=()):
+    rows, depth = terms.shape
     return launch(
         spread_kernel,
-        (near, own),
+        (terms,),
         after,
         out_shape=shape(8 * SIDE, rows, depth // rows),
-        in_specs=[VMEM] * 2,
+        in_specs=[VMEM],
         out_specs=VMEM,
         cost_estimate=cost(rows * depth, 4 * 8 * SIDE * depth),
         name="gain_parts",
@@ -557,13 +547,11 @@
 def to_y_kernel(place, block, up, far, down, gains, loss, message):
     span, depth = block.shape
     total = (block[...] + far[...].astype(F32)) + (up[...].astype(F32) + down[...].astype(F32))
-    gain = jnp.sum(gains[...], axis=0)
-    gain = jnp.concatenate([gain[i : i + 1] for i in range(gain.shape[0])], axis=1)
     rows = span // SIDE
-    row = lax.broadcasted_iota(jnp.int32, (rows, depth), 0)
-    extra = jnp.where(row == 0, gain, jnp.where(row == 1, loss[2:3, :1], 0.0))
+    extra = jnp.broadcast_to(loss[2:3, :1], (rows, TAIL))
+    extra = jnp.concatenate([jnp.sum(gains[...], axis=0), extra], axis=1)
     for ds in range(SIDE):
-        filled = jnp.concatenate([total[ds * rows : (ds + 1) * rows], extra], axis=0)
+        filled = jnp.concatenate([total[ds * rows : (ds + 1) * rows], extra], axis=1)
         message[lax.rem(place[0] + ds, SIDE)] = filled
 
 
@@ -573,7 +561,7 @@
         to_y_kernel,
         (place, block, up, far, down, gains, loss),
         after,
-        out_shape=shape(SIDE, 2 * span // SIDE, depth),
+        out_shape=shape(SIDE, span // SIDE, depth + gains.shape[2] + TAIL),
         in_specs=[SMEM] + [VMEM] * 6,
         out_specs=VMEM,
         cost_estimate=cost(8 * span * depth, 16 * span * depth),
@@ -586,9 +574,11 @@
     depth = width // SIDE
     for s in range(SIDE):
         cut = pl.ds(s * depth, depth)
-        dnormed[:, cut] = message[s, :rows]
-        gain_out[:, cut] = message[s, rows : rows + 1] / gain[:, cut]
-    loss = message[:, rows + 1, :TAIL]
+        dnormed[:, cut] = message[s, :, :depth]
+        sums = message[s, :, depth:-TAIL]
+        sums = jnp.concatenate([sums[i : i + 1] for i in range(rows)], axis=1)
+        gain_out[:, cut] = sums / gain[:, cut]
+    loss = message[:, 0, -TAIL:]
     loss_out[...] = jnp.sum(loss, axis=0, keepdims=True)
     values = hidden[...].astype(F32)
     inverse = lax.rsqrt(jnp.mean(values * values, axis=1, keepdims=True) + EPS)
@@ -670,22 +660,14 @@
     swapped = over_vocab(others, dc=1)
     ours = dlogit_of(0, place, scales, exps, above, far_first, below, mine, (others,))
     span = mine[0].shape[1]
-    to_up, to_down, to_far, gain_near = dnormed_of(
-        span, ours, swapped, held_head, held_other, mine[1:], span, BF16
-    )
+    kept, to_up, to_down, to_far, gain = dnormed_of(ours, swapped, held_head, held_other, mine, span)
     moved = [over_vocab(to_far, dz=2), over_vocab(to_up, dz=1), over_vocab(to_down, dz=-1)]
-    kept, gain_own = dnormed_of(0, ours, swapped, held_head, held_other, mine[:1], span, F32, (gain_near,))
-
-    gains = lax.all_to_all(spread(gain_near, gain_own), "vocab", 0, 0)
-    tiles = depth // TILE
-    grad, token = head_grad_of(pieces, ours, others, depth, 0, tiles // 2, None, (gain_own,))
+    gains = lax.all_to_all(spread(gain), "vocab", 0, 0)
+    head_grad, token = head_grad_of(pieces, ours, others, depth, (gain,))
     block, *cuts = to_x(kept, *moved, (token,))
     cuts = [over_vocab(cuts[0], dx=1), over_vocab(cuts[1], dx=2), over_vocab(cuts[2], dx=-1)]
-    grad, token = head_grad_of(pieces, ours, others, depth, tiles // 2, 3 * tiles // 4, grad, (block,))
-    message = to_y(place, block, *cuts, gains, loss, (token,))
-    got = lax.all_to_all(message, "section", 0, 0)
-    head_grad, token = head_grad_of(pieces, ours, others, depth, 3 * tiles // 4, tiles, grad, (message,))
-    hidden_grad, gain_grad, total_loss = finish(hidden_rows, gain_row, got, (token,))
+    got = lax.all_to_all(to_y(place, block, *cuts, gains, loss), "section", 0, 0)
+    hidden_grad, gain_grad, total_loss = finish(hidden_rows, gain_row, got)
     return (hidden_grad, gain_grad.reshape(width), head_grad, total_loss[0, 0])
 
 

time: 215 us -> 211 us (0.981)
  Pallas kernels: 78.9 us -> 64.5 us
  blocking collectives: 0 us -> 10 us
  starting transfers between devices: 63.5 us -> 60 us
  local copies, waits for them, and re-layouts: 1.88 us -> 4.28 us
    pallas_call x24 -> x21, Pallas kernels: 78.9 us -> 64.5 us  [launch(): pl.pallas_call(body, in_specs=[*in_specs, *[ANY] * ignored], scratch_shap...]
    all_to_all x0 -> x1, blocking collectives: none -> 10 us  [local(): lax.all_to_all(to_y(place, block, *cuts, gains, loss), 'section', 0, 0)]
    ppermute x27, waiting for transfers between devices: 21.7 us -> 28.4 us  [over_vocab(): return lax.ppermute(x, 'vocab', pairs)]
    all_to_all x2 -> x1, starting transfers between devices: 8.19 us -> 4.77 us  [local(): gains = lax.all_to_all(spread(gain), 'vocab', 0, 0)]
    ppermute x14, waiting for transfers between devices: 43.3 us -> 40 us  [over_section(): lax.ppermute(x, 'section', [(i, (i + step) % SIDE) for i in range(SIDE)])]
    unnamed x30 -> x32, local copies, waits for them, and re-layouts: 1.71 us -> 4.11 us
  transfers between devices with their start and end apart: 43 -> 42, of which waited for: 21 -> 22; matrix products, arithmetic and copies ran while one was open for 1% -> 1% of each run, Pallas kernels for 28% -> 20%
where the time goes in v3:
time: 211 us
  waiting for transfers between devices  68.5 us (32%)
  Pallas kernels  64.5 us (31%)
  starting transfers between devices  60 us (28%)
  blocking collectives  10 us (5%)
  local copies, waits for them, and re-layouts  4.28 us (2%)
  other arithmetic  2.31 us (1%)
    pallas_call x21, Pallas kernels, launch(): pl.pallas_call(body, in_specs=[*in_specs, *[ANY] * ignored], scratch_shap...  64.5 us
    ppermute x14, waiting for transfers between devices, over_section(): lax.ppermute(x, 'section', [(i, (i + step) % SIDE) for i in range(SIDE)])  40 us
    ppermute x27, starting transfers between devices, over_vocab(): return lax.ppermute(x, 'vocab', pairs)  34.3 us
    ppermute x27, waiting for transfers between devices, over_vocab(): return lax.ppermute(x, 'vocab', pairs)  28.4 us
    ppermute x14, starting transfers between devices, over_section(): lax.ppermute(x, 'section', [(i, (i + step) % SIDE) for i in range(SIDE)])  20.9 us
    all_to_all x1, blocking collectives, local(): lax.all_to_all(to_y(place, block, *cuts, gains, loss), 'section', 0, 0)  10 us
    all_to_all x1, starting transfers between devices, local(): gains = lax.all_to_all(spread(gain), 'vocab', 0, 0)  4.77 us
  transfers between devices with their start and end apart: 42, of which 22 were waited for; matrix products, arithmetic and copies ran while one was open for 1% of the time, Pallas kernels for 20%

profile of v3, /device:TPU:0, one launch (start us, length us, event | category | flops | bytes accessed | tf_op | source)
XLA Modules:
  0.0 210.7 jit_solution(8543539125407526856)
XLA Ops:
  2.5 1.7 collective-permute-start.2
  4.2 2.9 %collective-permute-start.1 = (bf16[8,2176]{1,0:T(8,128)(2,1)S(1)}, bf16[8,2176]{1,0:T(8,128)(2,1)S(1)}, u32[]{:S(2)}, u32[]{:S(2)}) collective-permute-start(bf16[8,2176]{1,0:T(8,128)(2,1)S(1)} %get-tuple-element.42), channel_id=1, source_target_pairs={{0,64},{32,96},{64,0},{96,32},{1,65},{33,97},{65,1},{97,33},{2,66}... | collective-permute-start | bytes 104456 | tf_op jit(solution)/shard_map/ppermute | solution.py:22
  11.1 2.0 collective-permute-start.7
  13.1 2.2 %collective-permute-start.6 = (bf16[4,8,2176]{2,1,0:T(8,128)(2,1)S(1)}, bf16[4,8,2176]{2,1,0:T(8,128)(2,1)S(1)}, u32[]{:S(2)}, u32[]{:S(2)}) collective-permute-start(bf16[4,8,2176]{2,1,0:T(8,128)(2,1)S(1)} %pad_maximum_fusion.3.refs_1_), channel_id=1, source_target_pairs={{0,6},{1,7},{2,0},{3,1},{4,2},{5,3},{6,4},{7,5},{8,14},{9,15},{10,... | collective-permute-start | bytes 417800 | tf_op jit(solution)/shard_map/ppermute | solution.py:32
  15.3 1.5 collective-permute-start.5
  16.8 2.7 %collective-permute-start.4 = (bf16[4,8,2176]{2,1,0:T(8,128)(2,1)S(1)}, bf16[4,8,2176]{2,1,0:T(8,128)(2,1)S(1)}, u32[]{:S(2)}, u32[]{:S(2)}) collective-permute-start(bf16[4,8,2176]{2,1,0:T(8,128)(2,1)S(1)} %pad_maximum_fusion.3.refs_1_), channel_id=1, source_target_pairs={{0,16},{1,17},{2,18},{3,19},{4,20},{5,21},{6,22},{7,23},{8,24},{9,... | collective-permute-start | bytes 417800 | tf_op jit(solution)/shard_map/ppermute | solution.py:32
  19.5 1.4 collective-permute-start.3
  21.1 2.6 %collective-permute-start.9 = (bf16[4,2,8,2176]{3,2,0,1:T(8,128)(2,1)S(1)}, bf16[4,2,8,2176]{3,2,0,1:T(8,128)(2,1)S(1)}, u32[]{:S(2)}, u32[]{:S(2)}) collective-permute-start(bf16[4,2,8,2176]{3,2,0,1:T(8,128)(2,1)S(1)} %pad_maximum_fusion.2), channel_id=1, source_target_pairs={{0,16},{1,17},{2,18},{3,19},{4,20},{5,21},{6,22},{7,23},{8,24},{9,... | collective-permute-start | bytes 835592 | tf_op jit(solution)/shard_map/ppermute | solution.py:32
  23.7 2.1 %collective-permute-done.4 = bf16[4,8,2176]{2,1,0:T(8,128)(2,1)S(1)} collective-permute-done((bf16[4,8,2176]{2,1,0:T(8,128)(2,1)S(1)}, bf16[4,8,2176]{2,1,0:T(8,128)(2,1)S(1)}, u32[]{:S(2)}, u32[]{:S(2)}) %collective-permute-start.4) | collective-permute-done | bytes 139296 | tf_op jit(solution)/shard_map/ppermute | solution.py:32
  27.0 1.9 collective-permute-start.11
  28.9 4.0 %collective-permute-done.8 = bf16[4,2,8,2176]{3,2,0,1:T(8,128)(2,1)S(1)} collective-permute-done((bf16[4,2,8,2176]{3,2,0,1:T(8,128)(2,1)S(1)}, bf16[4,2,8,2176]{3,2,0,1:T(8,128)(2,1)S(1)}, u32[]{:S(2)}, u32[]{:S(2)}) %collective-permute-start.8) | collective-permute-done | bytes 278560 | tf_op jit(solution)/shard_map/ppermute | solution.py:32
  32.9 3.2 %collective-permute-done.10 = bf16[4,2,8,2176]{3,2,0,1:T(8,128)(2,1)S(1)} collective-permute-done((bf16[4,2,8,2176]{3,2,0,1:T(8,128)(2,1)S(1)}, bf16[4,2,8,2176]{3,2,0,1:T(8,128)(2,1)S(1)}, u32[]{:S(2)}, u32[]{:S(2)}) %collective-permute-start.10) | collective-permute-done | bytes 278560 | tf_op jit(solution)/shard_map/ppermute | solution.py:32
  38.1 4.2 %hold_head.2 = (bf16[2048,2048]{1,0:T(8,128)(2,1)S(1)}, f32[8,128]{1,0:T(8,128)}) custom-call(bf16[2048,2048]{1,0:T(8,128)(2,1)} %refs_0_.2, bf16[4,8,2176]{2,1,0:T(8,128)(2,1)S(1)} %pad_maximum_fusion.3.refs_1_), custom_call_target="tpu_custom_call" | custom-call | bytes 8388608 | tf_op jit(solution)/shard_map/hold_head/pallas_call | solution.py:57
  42.4 4.5 %partial_logits.3 = (s16[128,2176]{1,0:T(8,128)(2,1)S(1)}, s16[128,2176]{1,0:T(8,128)(2,1)S(1)}) custom-call(bf16[4,32,2176]{2,1,0:T(8,128)(2,1)S(1)} %pad_maximum_fusion.1.refs_0_.refs_4_.refs_9_, bf16[4,64,2176]{2,1,0:T(8,128)(2,1)S(1)} %bitcast.22, bf16[4,32,2176]{2,1,0:T(8,128)(2,1)S(1)} %collective-permute-done.11.refs_2_.refs_6_.refs_11_, ...), custom_call_target="tpu_custom_call" | custom-call | bytes 10485760 | tf_op jit(solution)/shard_map/partial_logits/pallas_call | solution.py:57
  47.4 3.0 %collective-permute-start.16 = (s16[128,2176]{1,0:T(8,128)(2,1)S(1)}, s16[128,2176]{1,0:T(8,128)(2,1)S(1)}, u32[]{:S(2)}, u32[]{:S(2)}) collective-permute-start(s16[128,2176]{1,0:T(8,128)(2,1)S(1)} %get-tuple-element.52), channel_id=1, source_target_pairs={{0,96},{32,0},{64,32},{96,64},{1,97},{33,1},{65,33},{97,65},{2,98}... | collective-permute-start | bytes 1671176 | tf_op jit(solution)/shard_map/ppermute | solution.py:22
  50.5 6.7 %partial_logits.4 = (f32[256,2048]{1,0:T(8,128)S(1)}, f32[256,2048]{1,0:T(8,128)S(1)}) custom-call(bf16[4,32,2176]{2,1,0:T(8,128)(2,1)S(1)} %pad_maximum_fusion.1.refs_0_.refs_4_.refs_9_, bf16[4,64,2176]{2,1,0:T(8,128)(2,1)S(1)} %bitcast.23, bf16[4,32,2176]{2,1,0:T(8,128)(2,1)S(1)} %collective-permute-done.11.refs_2_.refs_6_.refs_11_, ...), custom_call_target="tpu_custom_call" | custom-call | bytes 12582912 | tf_op jit(solution)/shard_map/partial_logits/pallas_call | solution.py:57
  57.2 6.0 %collective-permute-done.15.refs_2_ = s16[128,2176]{1,0:T(8,128)(2,1)S(1)} collective-permute-done((s16[128,2176]{1,0:T(8,128)(2,1)S(1)}, s16[128,2176]{1,0:T(8,128)(2,1)S(1)}, u32[]{:S(2)}, u32[]{:S(2)}) %collective-permute-start.15) | collective-permute-done | bytes 557088 | tf_op jit(solution)/shard_map/ppermute | solution.py:22
  65.2 2.4 %collective-permute-start.18 = (s16[256,2176]{1,0:T(8,128)(2,1)S(1)}, s16[256,2176]{1,0:T(8,128)(2,1)S(1)}, u32[]{:S(2)}, u32[]{:S(2)}) collective-permute-start(s16[256,2176]{1,0:T(8,128)(2,1)S(1)} %get-tuple-element.54), channel_id=1, source_target_pairs={{0,96},{32,0},{64,32},{96,64},{1,97},{33,1},{65,33},{97,65},{2,98}... | collective-permute-start | bytes 3342344 | tf_op jit(solution)/shard_map/ppermute | solution.py:22
  67.6 4.1 %partial_logits.5.refs_1_ = f32[256,2048]{1,0:T(8,128)S(1)} custom-call(bf16[4,32,2176]{2,1,0:T(8,128)(2,1)S(1)} %pad_maximum_fusion.1.refs_0_.refs_4_.refs_9_, bf16[4,64,2176]{2,1,0:T(8,128)(2,1)S(1)} %bitcast.24, bf16[4,32,2176]{2,1,0:T(8,128)(2,1)S(1)} %collective-permute-done.11.refs_2_.refs_6_.refs_11_, ...), custom_call_target="tpu_custom_call" | custom-call | bytes 10485760 | tf_op jit(solution)/shard_map/partial_logits/pallas_call | solution.py:57
  71.7 19.8 %collective-permute-done.17.refs_2_ = s16[256,2176]{1,0:T(8,128)(2,1)S(1)} collective-permute-done((s16[256,2176]{1,0:T(8,128)(2,1)S(1)}, s16[256,2176]{1,0:T(8,128)(2,1)S(1)}, u32[]{:S(2)}, u32[]{:S(2)}) %collective-permute-start.17) | collective-permute-done | bytes 1114144 | tf_op jit(solution)/shard_map/ppermute | solution.py:22
  91.4 2.6 %own_logits.1 = (bf16[2,128,2048]{2,1,0:T(8,128)(2,1)S(1)}, f32[256,128]{1,0:T(8,128)S(1)}) custom-call(s32[5]{0:T(128)S(1)} %stack.62.refs_0_, f32[256,2048]{1,0:T(8,128)S(1)} %partial_logits.5.refs_1_, s16[256,2176]{1,0:T(8,128)(2,1)S(1)} %collective-permute-done.17.refs_2_, s16[256,2176]{1,0:T(8,128)(2,1)S(1)} %collective-permute-done.18.refs_3_, ...), custom_call_target="tpu_custom_call" | custom-call | flops 10485760 | bytes 6291456 | tf_op jit(solution)/shard_map/own_logits/pallas_call | solution.py:57
  94.0 3.0 %collective-permute-start.30 = (bf16[2,128,2048]{2,1,0:T(8,128)(2,1)S(1)}, bf16[2,128,2048]{2,1,0:T(8,128)(2,1)S(1)}, u32[]{:S(2)}, u32[]{:S(2)}) collective-permute-start(bf16[2,128,2048]{2,1,0:T(8,128)(2,1)S(1)} %get-tuple-element.58.refs_5_), channel_id=1, source_target_pairs={{0,96},{32,0},{64,32},{96,64},{1,97},{33,1},{65,33},{97,65},{2,98}... | collective-permute-start | bytes 3145736 | tf_op jit(solution)/shard_map/ppermute | solution.py:22
  97.0 3.4 %hold_head.3 = (bf16[2048,2048]{1,0:T(8,128)(2,1)S(1)}, f32[8,128]{1,0:T(8,128)S(1)}) custom-call(bf16[2048,2048]{1,0:T(8,128)(2,1)} %collective-permute-done.19.refs_0_, f32[256,128]{1,0:T(8,128)S(1)} %get-tuple-element.55.refs_1_.refs_6_), custom_call_target="tpu_custom_call" | custom-call | bytes 8388608 | tf_op jit(solution)/shard_map/hold_head/pallas_call | solution.py:57
  100.4 3.4 %copy-done.7 = bf16[2048,2048]{1,0:T(8,128)(2,1)} copy-done((bf16[2048,2048]{1,0:T(8,128)(2,1)}, bf16[2048,2048]{1,0:T(8,128)(2,1)S(1)}, u32[]{:S(2)}) %copy-start.7) | copy-done | bytes 8388632
  105.8 2.3 %collective-permute-start.21 = (f32[8,256]{1,0:T(8,128)S(1)}, f32[8,256]{1,0:T(8,128)S(1)}, u32[]{:S(2)}, u32[]{:S(2)}) collective-permute-start(f32[8,256]{1,0:T(8,128)S(1)} %merge_statistics.2.refs_0_), channel_id=1, source_target_pairs={{0,24},{1,25},{2,26},{3,27},{4,28},{5,29},{6,30},{7,31},{8,0},{9,1... | collective-permute-start | bytes 24584 | tf_op jit(solution)/shard_map/ppermute | solution.py:32
  110.3 2.9 %collective-permute-done.22.refs_2_ = f32[8,256]{1,0:T(8,128)S(1)} collective-permute-done((f32[8,256]{1,0:T(8,128)S(1)}, f32[8,256]{1,0:T(8,128)S(1)}, u32[]{:S(2)}, u32[]{:S(2)}) %collective-permute-start.22) | collective-permute-done | bytes 8224 | tf_op jit(solution)/shard_map/ppermute | solution.py:32
  113.8 4.0 %collective-permute-done.30.refs_1_.refs_6_ = bf16[2,128,2048]{2,1,0:T(8,128)(2,1)S(1)} collective-permute-done((bf16[2,128,2048]{2,1,0:T(8,128)(2,1)S(1)}, bf16[2,128,2048]{2,1,0:T(8,128)(2,1)S(1)}, u32[]{:S(2)}, u32[]{:S(2)}) %collective-permute-start.30) | collective-permute-done | bytes 1048608 | tf_op jit(solution)/shard_map/ppermute | solution.py:22
  117.8 3.4 %collective-permute-done.31.refs_0_.refs_8_ = bf16[2,128,2048]{2,1,0:T(8,128)(2,1)S(1)} collective-permute-done((bf16[2,128,2048]{2,1,0:T(8,128)(2,1)S(1)}, bf16[2,128,2048]{2,1,0:T(8,128)(2,1)S(1)}, u32[]{:S(2)}, u32[]{:S(2)}) %collective-permute-start.31) | collective-permute-done | bytes 1048608 | tf_op jit(solution)/shard_map/ppermute | solution.py:22
  121.4 3.2 %collective-permute-start.33 = (bf16[128,2048]{1,0:T(8,128)(2,1)S(1)}, bf16[128,2048]{1,0:T(8,128)(2,1)S(1)}, u32[]{:S(2)}, u32[]{:S(2)}) collective-permute-start(bf16[128,2048]{1,0:T(8,128)(2,1)S(1)} %get-tuple-element.60), channel_id=1, source_target_pairs={{0,96},{32,0},{64,32},{96,64},{1,97},{33,1},{65,33},{97,65},{2,98}... | collective-permute-start | bytes 1572872 | tf_op jit(solution)/shard_map/ppermute | solution.py:22
  125.4 1.9 collective-permute-start.24
  129.8 2.6 %collective-permute-done.25.refs_4_ = f32[8,256]{1,0:T(8,128)S(1)} collective-permute-done((f32[8,256]{1,0:T(8,128)S(1)}, f32[8,256]{1,0:T(8,128)S(1)}, u32[]{:S(2)}, u32[]{:S(2)}) %collective-permute-start.25) | collective-permute-done | bytes 8224 | tf_op jit(solution)/shard_map/ppermute | solution.py:32
  132.4 1.4 combine_statistics.1.refs_1_.refs_6_
  135.9 1.6 collective-permute-done.27.refs_2_
  137.5 1.6 collective-permute-done.28.refs_3_
  140.2 2.1 %dlogit.2.refs_12_.refs_7_ = bf16[4,128,2048]{2,1,0:T(8,128)(2,1)S(1)} custom-call(s32[5]{0:T(128)S(1)} %stack.62.refs_0_, f32[8,256]{1,0:T(8,128)S(1)} %combine_statistics.1.refs_1_.refs_6_, f32[8,256]{1,0:T(8,128)S(1)} %collective-permute-done.27.refs_2_, f32[8,256]{1,0:T(8,128)S(1)} %collective-permute-done.28.refs_3_, ...), custom_call_target="tpu_custom_call" | custom-call | flops 10485760 | bytes 4194304 | tf_op jit(solution)/shard_map/dlogit/pallas_call | solution.py:57
  142.5 2.1 %dlogit.3.refs_0_.refs_6_ = bf16[4,128,2048]{2,1,0:T(8,128)(2,1)S(1)} custom-call(s32[5]{0:T(128)S(1)} %stack.62.refs_0_, f32[8,256]{1,0:T(8,128)S(1)} %combine_statistics.1.refs_1_.refs_6_, f32[8,256]{1,0:T(8,128)S(1)} %collective-permute-done.27.refs_2_, f32[8,256]{1,0:T(8,128)S(1)} %collective-permute-done.28.refs_3_, ...), custom_call_target="tpu_custom_call" | custom-call | flops 10485760 | bytes 4194304 | tf_op jit(solution)/shard_map/dlogit/pallas_call | solution.py:57
  144.6 2.0 collective-permute-done.34.refs_1_
  146.7 12.2 %dnormed.1 = (f32[4,32,2048]{2,1,0:T(8,128)S(1)}, bf16[4,32,2048]{2,1,0:T(8,128)(2,1)}, bf16[4,32,2048]{2,1,0:T(8,128)(2,1)}, bf16[4,32,2048]{2,1,0:T(8,128)(2,1)}, f32[8,2048]{1,0:T(8,128)S(1)}) custom-call(bf16[4,128,2048]{2,1,0:T(8,128)(2,1)S(1)} %dlogit.3.refs_0_.refs_6_, bf16[4,128,2048]{2,1,0:T(8,128)(2,1)S(1)} %collective-permute-done.34.refs_1_, ...), custom_call_target="tpu_custom_call" | custom-call | bytes 16777216 | tf_op jit(solution)/shard_map/dnormed/pallas_call | solution.py:57
  158.8 2.0 collective-permute-start.35
  161.0 3.1 %collective-permute-start.37 = (bf16[4,32,2048]{2,1,0:T(8,128)(2,1)}, bf16[4,32,2048]{2,1,0:T(8,128)(2,1)S(1)}, u32[]{:S(2)}, u32[]{:S(2)}) collective-permute-start(bf16[4,32,2048]{2,1,0:T(8,128)(2,1)} %get-tuple-element.65), channel_id=1, source_target_pairs={{0,6},{1,7},{2,0},{3,1},{4,2},{5,3},{6,4},{7,5},{8,14},{9,15},{10,... | collective-permute-start | bytes 1572872 | tf_op jit(solution)/shard_map/ppermute | solution.py:32
  164.9 4.8 %all-to-all-start = ((f32[32,8,256]{2,1,0:T(8,128)}), f32[32,8,256]{2,1,0:T(8,128)S(1)}, u32[]{:S(2)}, u32[]{:S(2)}) async-start(f32[32,8,256]{2,1,0:T(8,128)} %gain_parts.1), calls=%async_computation | async-start | bytes 524288 | tf_op jit(solution)/shard_map/all_to_all | solution.py:665
  169.6 15.3 %head_grad.1 = (bf16[2048,2048]{1,0:T(8,128)(2,1)}, f32[8,128]{1,0:T(8,128)S(1)}) custom-call(bf16[4,32,2176]{2,1,0:T(8,128)(2,1)} %copy-done.2, bf16[4,64,2176]{2,1,0:T(8,128)(2,1)} %bitcast.28, bf16[4,32,2176]{2,1,0:T(8,128)(2,1)} %copy-done.3, bf16[4,32,2176]{2,1,0:T(8,128)(2,1)} %copy-done.4, bf16[4,64,2176]{2,1,0:T(8,128)(2,1)} %copy-done.1, ...), custom_call_target="tpu_custom_call" | custom-call | flops 8589934592 | bytes 16777216 | tf_op jit(solution)/shard_map/head_grad/pallas_call | solution.py:57
  184.9 3.2 %collective-permute-done.36.refs_2_ = bf16[4,32,2048]{2,1,0:T(8,128)(2,1)S(1)} collective-permute-done((bf16[4,32,2048]{2,1,0:T(8,128)(2,1)}, bf16[4,32,2048]{2,1,0:T(8,128)(2,1)S(1)}, u32[]{:S(2)}, u32[]{:S(2)}) %collective-permute-start.36) | collective-permute-done | bytes 524320 | tf_op jit(solution)/shard_map/ppermute | solution.py:32
  189.8 3.0 %collective-permute-start.39 = (bf16[32,2048]{1,0:T(8,128)(2,1)S(1)}, bf16[32,2048]{1,0:T(8,128)(2,1)S(1)}, u32[]{:S(2)}, u32[]{:S(2)}) collective-permute-start(bf16[32,2048]{1,0:T(8,128)(2,1)S(1)} %get-tuple-element.70), channel_id=1, source_target_pairs={{0,16},{1,17},{2,18},{3,19},{4,20},{5,21},{6,22},{7,23},{8,24},{9,... | collective-permute-start | bytes 393224 | tf_op jit(solution)/shard_map/ppermute | solution.py:32
  192.8 1.9 collective-permute-start.40
  194.7 1.5 collective-permute-done.38.refs_2_
  196.2 2.9 %collective-permute-done.39.refs_3_ = bf16[32,2048]{1,0:T(8,128)(2,1)S(1)} collective-permute-done((bf16[32,2048]{1,0:T(8,128)(2,1)S(1)}, bf16[32,2048]{1,0:T(8,128)(2,1)S(1)}, u32[]{:S(2)}, u32[]{:S(2)}) %collective-permute-start.39) | collective-permute-done | bytes 131104 | tf_op jit(solution)/shard_map/ppermute | solution.py:32
  199.7 10.0 %all_to_all.10.refs_2_ = f32[4,8,2432]{2,1,0:T(8,128)S(1)} all-to-all(f32[4,8,2432]{2,1,0:T(8,128)S(1)} %over_y.1), channel_id=1, replica_groups=mesh['section'=4,'vocab'=32] {'section'}, dimensions={0} | all-to-all | bytes 622592 | tf_op jit(solution)/shard_map/all_to_all | solution.py:669
  (100 shorter events, 27.3 us)
Async XLA Ops:
  2.5 6.0 %collective-permute-start.2 = (bf16[8,2176]{1,0:T(8,128)(2,1)S(1)}, bf16[8,2176]{1,0:T(8,128)(2,1)S(1)}, u32[]{:S(2)}, u32[]{:S(2)}) collective-permute-start(bf16[8,2176]{1,0:T(8,128)(2,1)S(1)} %get-tuple-element.43), channel_id=1, source_target_pairs={{0,32},{32,64},{64,96},{96,0},{1,33},{33,65},{65,97},{97,1},{2,34}... | collective-permute-start | bytes 104456 | tf_op jit(solution)/shard_map/ppermute | solution.py:22
  4.2 5.4 %collective-permute-start.1 = (bf16[8,2176]{1,0:T(8,128)(2,1)S(1)}, bf16[8,2176]{1,0:T(8,128)(2,1)S(1)}, u32[]{:S(2)}, u32[]{:S(2)}) collective-permute-start(bf16[8,2176]{1,0:T(8,128)(2,1)S(1)} %get-tuple-element.42), channel_id=1, source_target_pairs={{0,64},{32,96},{64,0},{96,32},{1,65},{33,97},{65,1},{97,33},{2,66}... | collective-permute-start | bytes 104456 | tf_op jit(solution)/shard_map/ppermute | solution.py:22
  7.1 3.9 %collective-permute-start = (bf16[8,2176]{1,0:T(8,128)(2,1)S(1)}, bf16[8,2176]{1,0:T(8,128)(2,1)S(1)}, u32[]{:S(2)}, u32[]{:S(2)}) collective-permute-start(bf16[8,2176]{1,0:T(8,128)(2,1)S(1)} %get-tuple-element.41), channel_id=1, source_target_pairs={{0,96},{32,0},{64,32},{96,64},{1,97},{33,1},{65,33},{97,65},{2,98}... | collective-permute-start | bytes 104456 | tf_op jit(solution)/shard_map/ppermute | solution.py:22
  11.1 9.8 %collective-permute-start.7 = (bf16[4,8,2176]{2,1,0:T(8,128)(2,1)S(1)}, bf16[4,8,2176]{2,1,0:T(8,128)(2,1)S(1)}, u32[]{:S(2)}, u32[]{:S(2)}) collective-permute-start(bf16[4,8,2176]{2,1,0:T(8,128)(2,1)S(1)} %pad_maximum_fusion.3.refs_1_), channel_id=1, source_target_pairs={{0,2},{1,3},{2,4},{3,5},{4,6},{5,7},{6,0},{7,1},{8,10},{9,11},{10,... | collective-permute-start | bytes 417800 | tf_op jit(solution)/shard_map/ppermute | solution.py:32
  13.1 7.9 %collective-permute-start.6 = (bf16[4,8,2176]{2,1,0:T(8,128)(2,1)S(1)}, bf16[4,8,2176]{2,1,0:T(8,128)(2,1)S(1)}, u32[]{:S(2)}, u32[]{:S(2)}) collective-permute-start(bf16[4,8,2176]{2,1,0:T(8,128)(2,1)S(1)} %pad_maximum_fusion.3.refs_1_), channel_id=1, source_target_pairs={{0,6},{1,7},{2,0},{3,1},{4,2},{5,3},{6,4},{7,5},{8,14},{9,15},{10,... | collective-permute-start | bytes 417800 | tf_op jit(solution)/shard_map/ppermute | solution.py:32
  15.3 8.4 %collective-permute-start.5 = (bf16[4,8,2176]{2,1,0:T(8,128)(2,1)S(1)}, bf16[4,8,2176]{2,1,0:T(8,128)(2,1)S(1)}, u32[]{:S(2)}, u32[]{:S(2)}) collective-permute-start(bf16[4,8,2176]{2,1,0:T(8,128)(2,1)S(1)} %pad_maximum_fusion.3.refs_1_), channel_id=1, source_target_pairs={{0,8},{1,9},{2,10},{3,11},{4,12},{5,13},{6,14},{7,15},{8,16},{9,17... | collective-permute-start | bytes 417800 | tf_op jit(solution)/shard_map/ppermute | solution.py:32
  16.8 9.1 %collective-permute-start.4 = (bf16[4,8,2176]{2,1,0:T(8,128)(2,1)S(1)}, bf16[4,8,2176]{2,1,0:T(8,128)(2,1)S(1)}, u32[]{:S(2)}, u32[]{:S(2)}) collective-permute-start(bf16[4,8,2176]{2,1,0:T(8,128)(2,1)S(1)} %pad_maximum_fusion.3.refs_1_), channel_id=1, source_target_pairs={{0,16},{1,17},{2,18},{3,19},{4,20},{5,21},{6,22},{7,23},{8,24},{9,... | collective-permute-start | bytes 417800 | tf_op jit(solution)/shard_map/ppermute | solution.py:32
  19.5 7.4 %collective-permute-start.3 = (bf16[4,8,2176]{2,1,0:T(8,128)(2,1)S(1)}, bf16[4,8,2176]{2,1,0:T(8,128)(2,1)S(1)}, u32[]{:S(2)}, u32[]{:S(2)}) collective-permute-start(bf16[4,8,2176]{2,1,0:T(8,128)(2,1)S(1)} %pad_maximum_fusion.3.refs_1_), channel_id=1, source_target_pairs={{0,24},{1,25},{2,26},{3,27},{4,28},{5,29},{6,30},{7,31},{8,0},{9,1... | collective-permute-start | bytes 417800 | tf_op jit(solution)/shard_map/ppermute | solution.py:32
  21.0 11.9 %collective-permute-start.8 = (bf16[4,2,8,2176]{3,2,0,1:T(8,128)(2,1)S(1)}, bf16[4,2,8,2176]{3,2,0,1:T(8,128)(2,1)S(1)}, u32[]{:S(2)}, u32[]{:S(2)}) collective-permute-start(bf16[4,2,8,2176]{3,2,0,1:T(8,128)(2,1)S(1)} %pad_maximum_fusion.2), channel_id=1, source_target_pairs={{0,24},{1,25},{2,26},{3,27},{4,28},{5,29},{6,30},{7,31},{8,0},{9,1... | collective-permute-start | bytes 835592 | tf_op jit(solution)/shard_map/ppermute | solution.py:32
  21.1 11.8 %collective-permute-start.9 = (bf16[4,2,8,2176]{3,2,0,1:T(8,128)(2,1)S(1)}, bf16[4,2,8,2176]{3,2,0,1:T(8,128)(2,1)S(1)}, u32[]{:S(2)}, u32[]{:S(2)}) collective-permute-start(bf16[4,2,8,2176]{3,2,0,1:T(8,128)(2,1)S(1)} %pad_maximum_fusion.2), channel_id=1, source_target_pairs={{0,16},{1,17},{2,18},{3,19},{4,20},{5,21},{6,22},{7,23},{8,24},{9,... | collective-permute-start | bytes 835592 | tf_op jit(solution)/shard_map/ppermute | solution.py:32
  23.7 12.4 %collective-permute-start.10 = (bf16[4,2,8,2176]{3,2,0,1:T(8,128)(2,1)S(1)}, bf16[4,2,8,2176]{3,2,0,1:T(8,128)(2,1)S(1)}, u32[]{:S(2)}, u32[]{:S(2)}) collective-permute-start(bf16[4,2,8,2176]{3,2,0,1:T(8,128)(2,1)S(1)} %pad_maximum_fusion.2), channel_id=1, source_target_pairs={{0,8},{1,9},{2,10},{3,11},{4,12},{5,13},{6,14},{7,15},{8,16},{9,17... | collective-permute-start | bytes 835592 | tf_op jit(solution)/shard_map/ppermute | solution.py:32
  27.0 119.7 %copy-start.2 = (bf16[4,32,2176]{2,1,0:T(8,128)(2,1)}, bf16[4,32,2176]{2,1,0:T(8,128)(2,1)S(1)}, u32[]{:S(2)}) copy-start(bf16[4,32,2176]{2,1,0:T(8,128)(2,1)S(1)} %pad_maximum_fusion.1.refs_0_.refs_4_.refs_9_) | copy-start | bytes 1671172
  27.0 11.1 %collective-permute-start.11 = (bf16[4,32,2176]{2,1,0:T(8,128)(2,1)S(1)}, bf16[4,32,2176]{2,1,0:T(8,128)(2,1)S(1)}, u32[]{:S(2)}, u32[]{:S(2)}) collective-permute-start(bf16[4,32,2176]{2,1,0:T(8,128)(2,1)S(1)} %pad_maximum_fusion.1.refs_0_.refs_4_.refs_9_), channel_id=1, source_target_pairs={{0,4},{1,5},{2,6},{3,7},{4,0},{5,1},{6,2},{7,3},{8,12},{9,13},{10,... | collective-permute-start | bytes 1671176 | tf_op jit(solution)/shard_map/ppermute | solution.py:32
  36.4 110.2 %copy-start = (bf16[4,2,4,8,2176]{4,3,2,1,0:T(8,128)(2,1)}, bf16[4,2,4,8,2176]{4,3,2,1,0:T(8,128)(2,1)S(1)}, u32[]{:S(2)}) copy-start(bf16[4,2,4,8,2176]{4,3,2,1,0:T(8,128)(2,1)S(1)} %copy.11) | copy-start | bytes 3342340
  36.4 5.9 %collective-permute-start.13 = (bf16[4,64,2176]{2,1,0:T(8,128)(2,1)S(1)}, bf16[4,64,2176]{2,1,0:T(8,128)(2,1)S(1)}, u32[]{:S(2)}, u32[]{:S(2)}) collective-permute-start(bf16[4,64,2176]{2,1,0:T(8,128)(2,1)S(1)} %bitcast.21), channel_id=1, source_target_pairs={{0,1},{1,0},{2,3},{3,2},{4,5},{5,4},{6,7},{7,6},{8,9},{9,8},{10,11... | collective-permute-start | bytes 3342344 | tf_op jit(solution)/shard_map/ppermute | solution.py:32
  36.5 5.8 %collective-permute-start.12 = (bf16[4,32,2176]{2,1,0:T(8,128)(2,1)S(1)}, bf16[4,32,2176]{2,1,0:T(8,128)(2,1)S(1)}, u32[]{:S(2)}, u32[]{:S(2)}) collective-permute-start(bf16[4,32,2176]{2,1,0:T(8,128)(2,1)S(1)} %pad_maximum_fusion.1.refs_0_.refs_4_.refs_9_), channel_id=1, source_target_pairs={{0,1},{1,0},{2,3},{3,2},{4,5},{5,4},{6,7},{7,6},{8,9},{9,8},{10,11... | collective-permute-start | bytes 1671176 | tf_op jit(solution)/shard_map/ppermute | solution.py:32
  38.1 108.5 %copy-start.3 = (bf16[4,32,2176]{2,1,0:T(8,128)(2,1)}, bf16[4,32,2176]{2,1,0:T(8,128)(2,1)S(1)}, u32[]{:S(2)}) copy-start(bf16[4,32,2176]{2,1,0:T(8,128)(2,1)S(1)} %collective-permute-done.11.refs_2_.refs_6_.refs_11_) | copy-start | bytes 1671172
  38.1 4.2 %collective-permute-start.14 = (bf16[4,32,2176]{2,1,0:T(8,128)(2,1)S(1)}, bf16[4,32,2176]{2,1,0:T(8,128)(2,1)S(1)}, u32[]{:S(2)}, u32[]{:S(2)}) collective-permute-start(bf16[4,32,2176]{2,1,0:T(8,128)(2,1)S(1)} %collective-permute-done.11.refs_2_.refs_6_.refs_11_), channel_id=1, source_target_pairs={{0,1},{1,0},{2,3},{3,2},{4,5},{5,4},{6,7},{7,6},{8,9},{9,8},{10,11... | collective-permute-start | bytes 1671176 | tf_op jit(solution)/shard_map/ppermute | solution.py:32
  42.3 97.9 %copy-start.4 = (bf16[4,32,2176]{2,1,0:T(8,128)(2,1)}, bf16[4,32,2176]{2,1,0:T(8,128)(2,1)S(1)}, u32[]{:S(2)}) copy-start(bf16[4,32,2176]{2,1,0:T(8,128)(2,1)S(1)} %collective-permute-done.12.refs_3_.refs_7_.refs_9_) | copy-start | bytes 1671172
  42.3 97.9 %copy-start.5 = (bf16[4,32,2176]{2,1,0:T(8,128)(2,1)}, bf16[4,32,2176]{2,1,0:T(8,128)(2,1)S(1)}, u32[]{:S(2)}) copy-start(bf16[4,32,2176]{2,1,0:T(8,128)(2,1)S(1)} %collective-permute-done.14.refs_5_.refs_9_.refs_11_) | copy-start | bytes 1671172
  42.4 97.9 %copy-start.1 = (bf16[4,64,2176]{2,1,0:T(8,128)(2,1)}, bf16[4,64,2176]{2,1,0:T(8,128)(2,1)S(1)}, u32[]{:S(2)}) copy-start(bf16[4,64,2176]{2,1,0:T(8,128)(2,1)S(1)} %collective-permute-done.13.refs_4_.refs_8_.refs_10_) | copy-start | bytes 3342340
  46.9 50.1 %collective-permute-start.19 = (bf16[2048,2048]{1,0:T(8,128)(2,1)}, bf16[2048,2048]{1,0:T(8,128)(2,1)}, u32[]{:S(2)}, u32[]{:S(2)}) collective-permute-start(bf16[2048,2048]{1,0:T(8,128)(2,1)} %refs_0_.2), channel_id=1, source_target_pairs={{0,1},{1,0},{2,3},{3,2},{4,5},{5,4},{6,7},{7,6},{8,9},{9,8},{10,11... | collective-permute-start | bytes 25165832 | tf_op jit(solution)/shard_map/ppermute | solution.py:32
  47.2 16.0 %collective-permute-start.15 = (s16[128,2176]{1,0:T(8,128)(2,1)S(1)}, s16[128,2176]{1,0:T(8,128)(2,1)S(1)}, u32[]{:S(2)}, u32[]{:S(2)}) collective-permute-start(s16[128,2176]{1,0:T(8,128)(2,1)S(1)} %get-tuple-element.49.refs_7_), channel_id=1, source_target_pairs={{0,32},{32,64},{64,96},{96,0},{1,33},{33,65},{65,97},{97,1},{2,34}... | collective-permute-start | bytes 1671176 | tf_op jit(solution)/shard_map/ppermute | solution.py:22
  47.4 15.8 %collective-permute-start.16 = (s16[128,2176]{1,0:T(8,128)(2,1)S(1)}, s16[128,2176]{1,0:T(8,128)(2,1)S(1)}, u32[]{:S(2)}, u32[]{:S(2)}) collective-permute-start(s16[128,2176]{1,0:T(8,128)(2,1)S(1)} %get-tuple-element.52), channel_id=1, source_target_pairs={{0,96},{32,0},{64,32},{96,64},{1,97},{33,1},{65,33},{97,65},{2,98}... | collective-permute-start | bytes 1671176 | tf_op jit(solution)/shard_map/ppermute | solution.py:22
  64.3 27.1 %collective-permute-start.17 = (s16[256,2176]{1,0:T(8,128)(2,1)S(1)}, s16[256,2176]{1,0:T(8,128)(2,1)S(1)}, u32[]{:S(2)}, u32[]{:S(2)}) collective-permute-start(s16[256,2176]{1,0:T(8,128)(2,1)S(1)} %get-tuple-element.53.refs_7_), channel_id=1, source_target_pairs={{0,32},{32,64},{64,96},{96,0},{1,33},{33,65},{65,97},{97,1},{2,34}... | collective-permute-start | bytes 3342344 | tf_op jit(solution)/shard_map/ppermute | solution.py:22
  65.2 26.3 %collective-permute-start.18 = (s16[256,2176]{1,0:T(8,128)(2,1)S(1)}, s16[256,2176]{1,0:T(8,128)(2,1)S(1)}, u32[]{:S(2)}, u32[]{:S(2)}) collective-permute-start(s16[256,2176]{1,0:T(8,128)(2,1)S(1)} %get-tuple-element.54), channel_id=1, source_target_pairs={{0,96},{32,0},{64,32},{96,64},{1,97},{33,1},{65,33},{97,65},{2,98}... | collective-permute-start | bytes 3342344 | tf_op jit(solution)/shard_map/ppermute | solution.py:22
  94.0 23.8 %collective-permute-start.30 = (bf16[2,128,2048]{2,1,0:T(8,128)(2,1)S(1)}, bf16[2,128,2048]{2,1,0:T(8,128)(2,1)S(1)}, u32[]{:S(2)}, u32[]{:S(2)}) collective-permute-start(bf16[2,128,2048]{2,1,0:T(8,128)(2,1)S(1)} %get-tuple-element.58.refs_5_), channel_id=1, source_target_pairs={{0,96},{32,0},{64,32},{96,64},{1,97},{33,1},{65,33},{97,65},{2,98}... | collective-permute-start | bytes 3145736 | tf_op jit(solution)/shard_map/ppermute | solution.py:22
  97.0 24.2 %collective-permute-start.31 = (bf16[2,128,2048]{2,1,0:T(8,128)(2,1)S(1)}, bf16[2,128,2048]{2,1,0:T(8,128)(2,1)S(1)}, u32[]{:S(2)}, u32[]{:S(2)}) collective-permute-start(bf16[2,128,2048]{2,1,0:T(8,128)(2,1)S(1)} %get-tuple-element.58.refs_5_), channel_id=1, source_target_pairs={{0,32},{32,64},{64,96},{96,0},{1,33},{33,65},{65,97},{97,1},{2,34}... | collective-permute-start | bytes 3145736 | tf_op jit(solution)/shard_map/ppermute | solution.py:22
  104.5 1.2 collective-permute-start.20
  105.8 4.5 %collective-permute-start.21 = (f32[8,256]{1,0:T(8,128)S(1)}, f32[8,256]{1,0:T(8,128)S(1)}, u32[]{:S(2)}, u32[]{:S(2)}) collective-permute-start(f32[8,256]{1,0:T(8,128)S(1)} %merge_statistics.2.refs_0_), channel_id=1, source_target_pairs={{0,24},{1,25},{2,26},{3,27},{4,28},{5,29},{6,30},{7,31},{8,0},{9,1... | collective-permute-start | bytes 24584 | tf_op jit(solution)/shard_map/ppermute | solution.py:32
  108.1 5.2 %collective-permute-start.22 = (f32[8,256]{1,0:T(8,128)S(1)}, f32[8,256]{1,0:T(8,128)S(1)}, u32[]{:S(2)}, u32[]{:S(2)}) collective-permute-start(f32[8,256]{1,0:T(8,128)S(1)} %merge_statistics.2.refs_0_), channel_id=1, source_target_pairs={{0,16},{1,17},{2,18},{3,19},{4,20},{5,21},{6,22},{7,23},{8,24},{9,... | collective-permute-start | bytes 24584 | tf_op jit(solution)/shard_map/ppermute | solution.py:32
  108.9 4.9 %collective-permute-start.23 = (f32[8,256]{1,0:T(8,128)S(1)}, f32[8,256]{1,0:T(8,128)S(1)}, u32[]{:S(2)}, u32[]{:S(2)}) collective-permute-start(f32[8,256]{1,0:T(8,128)S(1)} %merge_statistics.2.refs_0_), channel_id=1, source_target_pairs={{0,8},{1,9},{2,10},{3,11},{4,12},{5,13},{6,14},{7,15},{8,16},{9,17... | collective-permute-start | bytes 24584 | tf_op jit(solution)/shard_map/ppermute | solution.py:32
  121.3 18.9 %collective-permute-start.32 = (bf16[128,2048]{1,0:T(8,128)(2,1)S(1)}, bf16[128,2048]{1,0:T(8,128)(2,1)S(1)}, u32[]{:S(2)}, u32[]{:S(2)}) collective-permute-start(bf16[128,2048]{1,0:T(8,128)(2,1)S(1)} %get-tuple-element.59), channel_id=1, source_target_pairs={{0,32},{32,64},{64,96},{96,0},{1,33},{33,65},{65,97},{97,1},{2,34}... | collective-permute-start | bytes 1572872 | tf_op jit(solution)/shard_map/ppermute | solution.py:22
  121.4 18.9 %collective-permute-start.33 = (bf16[128,2048]{1,0:T(8,128)(2,1)S(1)}, bf16[128,2048]{1,0:T(8,128)(2,1)S(1)}, u32[]{:S(2)}, u32[]{:S(2)}) collective-permute-start(bf16[128,2048]{1,0:T(8,128)(2,1)S(1)} %get-tuple-element.60), channel_id=1, source_target_pairs={{0,96},{32,0},{64,32},{96,64},{1,97},{33,1},{65,33},{97,65},{2,98}... | collective-permute-start | bytes 1572872 | tf_op jit(solution)/shard_map/ppermute | solution.py:22
  125.4 4.5 %collective-permute-start.24 = (f32[8,256]{1,0:T(8,128)S(1)}, f32[8,256]{1,0:T(8,128)S(1)}, u32[]{:S(2)}, u32[]{:S(2)}) collective-permute-start(f32[8,256]{1,0:T(8,128)S(1)} %merge_statistics.3.refs_2_), channel_id=1, source_target_pairs={{0,6},{1,7},{2,0},{3,1},{4,2},{5,3},{6,4},{7,5},{8,14},{9,15},{10,... | collective-permute-start | bytes 24584 | tf_op jit(solution)/shard_map/ppermute | solution.py:32
  127.2 5.2 %collective-permute-start.25 = (f32[8,256]{1,0:T(8,128)S(1)}, f32[8,256]{1,0:T(8,128)S(1)}, u32[]{:S(2)}, u32[]{:S(2)}) collective-permute-start(f32[8,256]{1,0:T(8,128)S(1)} %merge_statistics.3.refs_2_), channel_id=1, source_target_pairs={{0,4},{1,5},{2,6},{3,7},{4,0},{5,1},{6,2},{7,3},{8,12},{9,13},{10,... | collective-permute-start | bytes 24584 | tf_op jit(solution)/shard_map/ppermute | solution.py:32
  127.3 5.1 %collective-permute-start.26 = (f32[8,256]{1,0:T(8,128)S(1)}, f32[8,256]{1,0:T(8,128)S(1)}, u32[]{:S(2)}, u32[]{:S(2)}) collective-permute-start(f32[8,256]{1,0:T(8,128)S(1)} %merge_statistics.3.refs_2_), channel_id=1, source_target_pairs={{0,2},{1,3},{2,4},{3,5},{4,6},{5,7},{6,0},{7,1},{8,10},{9,11},{10,... | collective-permute-start | bytes 24584 | tf_op jit(solution)/shard_map/ppermute | solution.py:32
  133.8 3.7 %collective-permute-start.27 = (f32[8,256]{1,0:T(8,128)S(1)}, f32[8,256]{1,0:T(8,128)S(1)}, u32[]{:S(2)}, u32[]{:S(2)}) collective-permute-start(f32[8,256]{1,0:T(8,128)S(1)} %combine_statistics.1.refs_1_.refs_6_), channel_id=1, source_target_pairs={{0,96},{32,0},{64,32},{96,64},{1,97},{33,1},{65,33},{97,65},{2,98}... | collective-permute-start | bytes 24584 | tf_op jit(solution)/shard_map/ppermute | solution.py:22
  133.9 5.2 %collective-permute-start.28 = (f32[8,256]{1,0:T(8,128)S(1)}, f32[8,256]{1,0:T(8,128)S(1)}, u32[]{:S(2)}, u32[]{:S(2)}) collective-permute-start(f32[8,256]{1,0:T(8,128)S(1)} %combine_statistics.1.refs_1_.refs_6_), channel_id=1, source_target_pairs={{0,64},{32,96},{64,0},{96,32},{1,65},{33,97},{65,1},{97,33},{2,66}... | collective-permute-start | bytes 24584 | tf_op jit(solution)/shard_map/ppermute | solution.py:22
  134.8 5.4 %collective-permute-start.29 = (f32[8,256]{1,0:T(8,128)S(1)}, f32[8,256]{1,0:T(8,128)S(1)}, u32[]{:S(2)}, u32[]{:S(2)}) collective-permute-start(f32[8,256]{1,0:T(8,128)S(1)} %combine_statistics.1.refs_1_.refs_6_), channel_id=1, source_target_pairs={{0,32},{32,64},{64,96},{96,0},{1,33},{33,65},{65,97},{97,1},{2,34}... | collective-permute-start | bytes 24584 | tf_op jit(solution)/shard_map/ppermute | solution.py:22
  142.4 4.2 %collective-permute-start.34 = (bf16[4,128,2048]{2,1,0:T(8,128)(2,1)S(1)}, bf16[4,128,2048]{2,1,0:T(8,128)(2,1)S(1)}, u32[]{:S(2)}, u32[]{:S(2)}) collective-permute-start(bf16[4,128,2048]{2,1,0:T(8,128)(2,1)S(1)} %dlogit.2.refs_12_.refs_7_), channel_id=1, source_target_pairs={{0,1},{1,0},{2,3},{3,2},{4,5},{5,4},{6,7},{7,6},{8,9},{9,8},{10,11... | collective-permute-start | bytes 6291464 | tf_op jit(solution)/shard_map/ppermute | solution.py:32
  158.8 26.1 %collective-permute-start.35 = (bf16[4,32,2048]{2,1,0:T(8,128)(2,1)}, bf16[4,32,2048]{2,1,0:T(8,128)(2,1)S(1)}, u32[]{:S(2)}, u32[]{:S(2)}) collective-permute-start(bf16[4,32,2048]{2,1,0:T(8,128)(2,1)} %get-tuple-element.63), channel_id=1, source_target_pairs={{0,4},{1,5},{2,6},{3,7},{4,0},{5,1},{6,2},{7,3},{8,12},{9,13},{10,... | collective-permute-start | bytes 1572872 | tf_op jit(solution)/shard_map/ppermute | solution.py:32
  160.9 27.3 %collective-permute-start.36 = (bf16[4,32,2048]{2,1,0:T(8,128)(2,1)}, bf16[4,32,2048]{2,1,0:T(8,128)(2,1)S(1)}, u32[]{:S(2)}, u32[]{:S(2)}) collective-permute-start(bf16[4,32,2048]{2,1,0:T(8,128)(2,1)} %get-tuple-element.64), channel_id=1, source_target_pairs={{0,2},{1,3},{2,4},{3,5},{4,6},{5,7},{6,0},{7,1},{8,10},{9,11},{10,... | collective-permute-start | bytes 1572872 | tf_op jit(solution)/shard_map/ppermute | solution.py:32
  161.0 27.1 %collective-permute-start.37 = (bf16[4,32,2048]{2,1,0:T(8,128)(2,1)}, bf16[4,32,2048]{2,1,0:T(8,128)(2,1)S(1)}, u32[]{:S(2)}, u32[]{:S(2)}) collective-permute-start(bf16[4,32,2048]{2,1,0:T(8,128)(2,1)} %get-tuple-element.65), channel_id=1, source_target_pairs={{0,6},{1,7},{2,0},{3,1},{4,2},{5,3},{6,4},{7,5},{8,14},{9,15},{10,... | collective-permute-start | bytes 1572872 | tf_op jit(solution)/shard_map/ppermute | solution.py:32
  164.9 29.8 %all-to-all-start = ((f32[32,8,256]{2,1,0:T(8,128)}), f32[32,8,256]{2,1,0:T(8,128)S(1)}, u32[]{:S(2)}, u32[]{:S(2)}) async-start(f32[32,8,256]{2,1,0:T(8,128)} %gain_parts.1), calls=%async_computation | async-start | bytes 524288 | tf_op jit(solution)/shard_map/all_to_all | solution.py:665
  188.9 7.2 %collective-permute-start.38 = (bf16[32,2048]{1,0:T(8,128)(2,1)}, bf16[32,2048]{1,0:T(8,128)(2,1)S(1)}, u32[]{:S(2)}, u32[]{:S(2)}) collective-permute-start(bf16[32,2048]{1,0:T(8,128)(2,1)} %get-tuple-element.69), channel_id=1, source_target_pairs={{0,8},{1,9},{2,10},{3,11},{4,12},{5,13},{6,14},{7,15},{8,16},{9,17... | collective-permute-start | bytes 393224 | tf_op jit(solution)/shard_map/ppermute | solution.py:32
  189.8 9.3 %collective-permute-start.39 = (bf16[32,2048]{1,0:T(8,128)(2,1)S(1)}, bf16[32,2048]{1,0:T(8,128)(2,1)S(1)}, u32[]{:S(2)}, u32[]{:S(2)}) collective-permute-start(bf16[32,2048]{1,0:T(8,128)(2,1)S(1)} %get-tuple-element.70), channel_id=1, source_target_pairs={{0,16},{1,17},{2,18},{3,19},{4,20},{5,21},{6,22},{7,23},{8,24},{9,... | collective-permute-start | bytes 393224 | tf_op jit(solution)/shard_map/ppermute | solution.py:32
  192.8 6.3 %collective-permute-start.40 = (bf16[32,2048]{1,0:T(8,128)(2,1)S(1)}, bf16[32,2048]{1,0:T(8,128)(2,1)S(1)}, u32[]{:S(2)}, u32[]{:S(2)}) collective-permute-start(bf16[32,2048]{1,0:T(8,128)(2,1)S(1)} %get-tuple-element.71), channel_id=1, source_target_pairs={{0,24},{1,25},{2,26},{3,27},{4,28},{5,29},{6,30},{7,31},{8,0},{9,1... | collective-permute-start | bytes 393224 | tf_op jit(solution)/shard_map/ppermute | solution.py:32
  (10 other events, 113.1 us)

commit v4 on v3

--- a/solution.py
+++ b/solution.py
@@ -239,7 +239,7 @@
 
 
 def own_logits_kernel(count, place, own, below, above, *refs):
-    digits, (exps, stats) = refs[: 2 * count], refs[2 * count :]
+    digits, exps, stats = refs[: 2 * count], refs[2 * count : -1], refs[-1]
     per, columns = own.shape
     at = 0
     for digit in digits:
@@ -248,7 +248,7 @@
         x = own[pl.ds(at, span), :] + (decode(below, at, span) + decode(above, at, span))
         top = jnp.max(x, axis=1, keepdims=True)
         exp = jnp.exp(x - top)
-        exps[at // (per // 2), pl.ds(at % (per // 2), span), :] = exp.astype(BF16)
+        exps[at // (per // 2)][pl.ds(at % (per // 2), span), :] = exp.astype(BF16)
         total = jnp.sum(exp, axis=1, keepdims=True)
         pick = jnp.sum(jnp.where(onehot_of(place, digit[0], columns), x, 0.0), axis=1, keepdims=True)
         stats[pl.ds(at, span), :] = jnp.where(lane == 0, top, jnp.where(lane == 1, total, pick))
@@ -269,9 +269,9 @@
         (place, own, below, above, *mine, *theirs),
         after,
         grid=(1,),
-        out_shape=[shape(2, per // 2, columns, dtype=BF16), shape(per, TAIL)],
+        out_shape=[shape(per // 2, columns, dtype=BF16)] * 2 + [shape(per, TAIL)],
         in_specs=[SMEM, full, coded, coded] + digit_specs([*mine, *theirs]),
-        out_specs=[pl.BlockSpec((2, per // 2, columns), lambda j: (0, 0, 0)), pl.BlockSpec((per, TAIL), lambda j: (0, 0))],
+        out_specs=[pl.BlockSpec((per // 2, columns), lambda j: (0, 0))] * 2 + [pl.BlockSpec((per, TAIL), lambda j: (0, 0))],
         cost_estimate=cost(20 * per * columns, 12 * per * columns),
         name="own_logits",
     )
@@ -374,25 +374,6 @@
     )
 
 
-def halves_kernel(below, above, first, last):
-    first[...] = below[0]
-    last[...] = above[1]
-
-
-def halves(below, above, after=()):
-    out = shape(*below.shape[1:], dtype=below.dtype)
-    return launch(
-        halves_kernel,
-        (below, above),
-        after,
-        out_shape=[out] * 2,
-        in_specs=[VMEM] * 2,
-        out_specs=[VMEM] * 2,
-        cost_estimate=cost(0, 4 * below.size),
-        name="halves",
-    )
-
-
 def dlogit_kernel(dc, place, *refs):
     scales, (own, above, far, below), digits, out = refs[:SIDE], refs[SIDE : 2 * SIDE], refs[2 * SIDE : -1], refs[-1]
     half, columns = far.shape
@@ -402,7 +383,7 @@
         at = 0
         for digit in digits:
             span = digit.shape[1]
-            exp = far[pl.ds(at, span), :] if ds == 2 else (own, above, None, below)[ds][0, pl.ds(at, span), :]
+            exp = (own, above, far, below)[ds][pl.ds(at, span), :]
             hit = onehot_of(place, digit[ds], columns)
             factor = scale[dc * half + at : dc * half + at + span, :1]
             grad = exp.astype(F32) * factor - jnp.where(hit, weight, 0.0)
@@ -413,7 +394,6 @@
 def dlogit_of(dc, place, scales, own, above, far, below, pieces, after=()):
     half, columns = far.shape
     at = pieces[0].shape[2] // TAIL - 1
-    one = pl.BlockSpec((1, half, columns), lambda j: (dc, 0, 0))
     return launch(
         functools.partial(dlogit_kernel, dc),
         (place, *scales, own, above, far, below, *pieces),
@@ -422,7 +402,7 @@
         out_shape=shape(SIDE, half, columns, dtype=BF16),
         in_specs=[SMEM]
         + [pl.BlockSpec(scales[0].shape, lambda j: (0, 0))] * SIDE
-        + [one, one, pl.BlockSpec((half, columns), lambda j: (0, 0)), one]
+        + [pl.BlockSpec((half, columns), lambda j: (0, 0))] * 4
         + [pl.BlockSpec((SIDE, p.shape[1], TAIL), lambda j: (0, 0, at)) for p in pieces],
         out_specs=pl.BlockSpec((SIDE, half, columns), lambda j: (0, 0, 0)),
         cost_estimate=cost(40 * half * columns, 16 * half * columns),
@@ -619,15 +599,17 @@
     weight = jnp.sum(jnp.where(jnp.arange(SIDE) == section, weights, 0.0)).reshape(1)
 
     cuts = normalise(place, in_hbm(hidden_rows), in_hbm(gain_row), targets)
-    own = jnp.stack([cuts[0], over_section(cuts[3], -1), over_section(cuts[2], 2), over_section(cuts[1], 1)])
+    held_head, token = hold(head_weight, (cuts[0],))
+    *cuts, _ = lax.optimization_barrier(
+        (cuts[0], over_section(cuts[3], -1), over_section(cuts[2], 2), over_section(cuts[1], 1), token)
+    )
+    own = jnp.stack(cuts)
     def along_x(x):
         return [x, over_vocab(x, dx=-1), over_vocab(x, dx=2), over_vocab(x, dx=1)]
 
     pair = jnp.stack([over_vocab(own, dz=-1), over_vocab(own, dz=1)], axis=1)
     mine = [jnp.concatenate(along_x(own), axis=1)]
-    held_head, token = hold(head_weight, (own,))
-    *pair, _ = lax.optimization_barrier((*along_x(pair), token))
-    mine.append(jnp.stack(pair, axis=2).reshape(SIDE, -1, own.shape[2]))
+    mine.append(jnp.stack(along_x(pair), axis=2).reshape(SIDE, -1, own.shape[2]))
     mine.append(over_vocab(mine[0], dz=2))
     theirs = [over_vocab(m, dc=1) for m in mine]
     pieces = (*mine, *theirs)
@@ -642,23 +624,23 @@
     first, last = pass_on(first, last, up, down)
     (kept,) = logits_of((0,), pieces, held_head, (first,))
     below, above = over_section(first, 1), over_section(last, -1)
-    exps, stats = own_logits(place, kept, below, above, mine, theirs)
-
-    below, above = over_section(exps, 1), over_section(exps, -1)
+    *exps, stats = own_logits(place, kept, below, above, mine, theirs)
+
+    below_0, above_1 = over_section(exps[0], 1), over_section(exps[1], -1)
+    below_1, above_0 = over_section(exps[1], 1), over_section(exps[0], -1)
+    far_0, far_1 = over_section(below_0, 1), over_section(above_1, -1)
     held_other, token = hold(other_head, (stats,))
     parts = pack(place, [stats], everything, own_rows, (token,))
     parts = merge([parts, over_vocab(parts, dc=1)])
     parts = merge(along_x(parts))
-    far_first, far_last = halves(below, above, (parts, token))
-    far_first, far_last = over_section(far_first, 1), over_section(far_last, -1)
     parts = [parts, over_vocab(parts, dz=-1), over_vocab(parts, dz=2), over_vocab(parts, dz=1)]
     scales = combine(place, weight, parts, stats, everything[0], own_rows)
     loss = scales
     scales = [scales, over_section(scales, -1), over_section(scales, 2), over_section(scales, 1)]
 
-    others = dlogit_of(1, place, scales, exps, above, far_last, below, theirs, (far_first,))
+    others = dlogit_of(1, place, scales, exps[1], above_1, far_1, below_1, theirs, (far_0,))
     swapped = over_vocab(others, dc=1)
-    ours = dlogit_of(0, place, scales, exps, above, far_first, below, mine, (others,))
+    ours = dlogit_of(0, place, scales, exps[0], above_0, far_0, below_0, mine, (others,))
     span = mine[0].shape[1]
     kept, to_up, to_down, to_far, gain = dnormed_of(ours, swapped, held_head, held_other, mine, span)
     moved = [over_vocab(to_far, dz=2), over_vocab(to_up, dz=1), over_vocab(to_down, dz=-1)]

time: 211 us -> 237 us (1.12)
  waiting for transfers between devices: 68.5 us -> 94.5 us
    ppermute x14 -> x16, waiting for transfers between devices: 40 us -> 59.1 us  [over_section(): lax.ppermute(x, 'section', [(i, (i + step) % SIDE) for i in range(SIDE)])]
    ppermute x27, waiting for transfers between devices: 28.4 us -> 35.4 us  [over_vocab(): return lax.ppermute(x, 'vocab', pairs)]
    ppermute x14 -> x16, starting transfers between devices: 20.9 us -> 22.2 us  [over_section(): lax.ppermute(x, 'section', [(i, (i + step) % SIDE) for i in range(SIDE)])]
    pallas_call x21 -> x20, Pallas kernels: 64.5 us -> 64.4 us  [launch(): pl.pallas_call(body, in_specs=[*in_specs, *[ANY] * ignored], scratch_shap...]
  transfers between devices with their start and end apart: 42 -> 44, of which waited for: 22 -> 25; matrix products, arithmetic and copies ran while one was open for 1% -> 1% of each run, Pallas kernels for 20% -> 18%
where the time goes in v4:
time: 237 us
  waiting for transfers between devices  94.5 us (40%)
  Pallas kernels  64.4 us (27%)
  starting transfers between devices  58.7 us (25%)
  blocking collectives  11.2 us (5%)
  local copies, waits for them, and re-layouts  4.28 us (2%)
    pallas_call x20, Pallas kernels, launch(): pl.pallas_call(body, in_specs=[*in_specs, *[ANY] * ignored], scratch_shap...  64.4 us
    ppermute x16, waiting for transfers between devices, over_section(): lax.ppermute(x, 'section', [(i, (i + step) % SIDE) for i in range(SIDE)])  59.1 us
    ppermute x27, waiting for transfers between devices, over_vocab(): return lax.ppermute(x, 'vocab', pairs)  35.4 us
    ppermute x27, starting transfers between devices, over_vocab(): return lax.ppermute(x, 'vocab', pairs)  32.6 us
    ppermute x16, starting transfers between devices, over_section(): lax.ppermute(x, 'section', [(i, (i + step) % SIDE) for i in range(SIDE)])  22.2 us
    all_to_all x1, blocking collectives, local(): lax.all_to_all(to_y(place, block, *cuts, gains, loss), 'section', 0, 0)  11.2 us
  transfers between devices with their start and end apart: 44, of which 25 were waited for; matrix products, arithmetic and copies ran while one was open for 1% of the time, Pallas kernels for 18%

profile of v4, /device:TPU:0, one launch (start us, length us, event | category | flops | bytes accessed | tf_op | source)
XLA Modules:
  0.0 236.6 jit_solution(8091733057686935536)
XLA Ops:
  2.5 3.2 %collective-permute-start = (bf16[8,2176]{1,0:T(8,128)(2,1)S(1)}, bf16[8,2176]{1,0:T(8,128)(2,1)S(1)}, u32[]{:S(2)}, u32[]{:S(2)}) collective-permute-start(bf16[8,2176]{1,0:T(8,128)(2,1)S(1)} %get-tuple-element.40), channel_id=1, source_target_pairs={{0,96},{32,0},{64,32},{96,64},{1,97},{33,1},{65,33},{97,65},{2,98}... | collective-permute-start | bytes 104456 | tf_op jit(solution)/shard_map/ppermute | solution.py:22
  7.3 3.8 %collective-permute-done.1 = bf16[8,2176]{1,0:T(8,128)(2,1)S(1)} collective-permute-done((bf16[8,2176]{1,0:T(8,128)(2,1)S(1)}, bf16[8,2176]{1,0:T(8,128)(2,1)S(1)}, u32[]{:S(2)}, u32[]{:S(2)}) %collective-permute-start.1) | collective-permute-done | bytes 34848 | tf_op jit(solution)/shard_map/ppermute | solution.py:22
  11.5 4.1 %collective-permute-start.6 = (bf16[4,8,2176]{2,1,0:T(8,128)(2,1)S(1)}, bf16[4,8,2176]{2,1,0:T(8,128)(2,1)S(1)}, u32[]{:S(2)}, u32[]{:S(2)}) collective-permute-start(bf16[4,8,2176]{2,1,0:T(8,128)(2,1)S(1)} %pad_maximum_fusion.3), channel_id=1, source_target_pairs={{0,6},{1,7},{2,0},{3,1},{4,2},{5,3},{6,4},{7,5},{8,14},{9,15},{10,... | collective-permute-start | bytes 417800 | tf_op jit(solution)/shard_map/ppermute | solution.py:32
  15.6 2.8 %collective-permute-start.3 = (bf16[4,8,2176]{2,1,0:T(8,128)(2,1)S(1)}, bf16[4,8,2176]{2,1,0:T(8,128)(2,1)S(1)}, u32[]{:S(2)}, u32[]{:S(2)}) collective-permute-start(bf16[4,8,2176]{2,1,0:T(8,128)(2,1)S(1)} %pad_maximum_fusion.3), channel_id=1, source_target_pairs={{0,24},{1,25},{2,26},{3,27},{4,28},{5,29},{6,30},{7,31},{8,0},{9,1... | collective-permute-start | bytes 417800 | tf_op jit(solution)/shard_map/ppermute | solution.py:32
  20.1 1.8 collective-permute-done.7
  21.9 2.8 %collective-permute-start.8 = (bf16[4,2,8,2176]{3,2,0,1:T(8,128)(2,1)S(1)}, bf16[4,2,8,2176]{3,2,0,1:T(8,128)(2,1)S(1)}, u32[]{:S(2)}, u32[]{:S(2)}) collective-permute-start(bf16[4,2,8,2176]{3,2,0,1:T(8,128)(2,1)S(1)} %get-tuple-element.75), channel_id=1, source_target_pairs={{0,24},{1,25},{2,26},{3,27},{4,28},{5,29},{6,30},{7,31},{8,0},{9,1... | collective-permute-start | bytes 835592 | tf_op jit(solution)/shard_map/ppermute | solution.py:32
  26.5 3.8 %collective-permute-done.5 = bf16[4,8,2176]{2,1,0:T(8,128)(2,1)S(1)} collective-permute-done((bf16[4,8,2176]{2,1,0:T(8,128)(2,1)S(1)}, bf16[4,8,2176]{2,1,0:T(8,128)(2,1)S(1)}, u32[]{:S(2)}, u32[]{:S(2)}) %collective-permute-start.5) | collective-permute-done | bytes 139296 | tf_op jit(solution)/shard_map/ppermute | solution.py:32
  30.3 3.8 %collective-permute-start.11 = (bf16[4,32,2176]{2,1,0:T(8,128)(2,1)S(1)}, bf16[4,32,2176]{2,1,0:T(8,128)(2,1)S(1)}, u32[]{:S(2)}, u32[]{:S(2)}) collective-permute-start(bf16[4,32,2176]{2,1,0:T(8,128)(2,1)S(1)} %pad_maximum_fusion.1.refs_0_.refs_4_.refs_9_), channel_id=1, source_target_pairs={{0,4},{1,5},{2,6},{3,7},{4,0},{5,1},{6,2},{7,3},{8,12},{9,13},{10,... | collective-permute-start | bytes 1671176 | tf_op jit(solution)/shard_map/ppermute | solution.py:32
  35.5 2.9 %collective-permute-done.10 = bf16[4,2,8,2176]{3,2,0,1:T(8,128)(2,1)S(1)} collective-permute-done((bf16[4,2,8,2176]{3,2,0,1:T(8,128)(2,1)S(1)}, bf16[4,2,8,2176]{3,2,0,1:T(8,128)(2,1)S(1)}, u32[]{:S(2)}, u32[]{:S(2)}) %collective-permute-start.10) | collective-permute-done | bytes 278560 | tf_op jit(solution)/shard_map/ppermute | solution.py:32
  39.3 2.4 %collective-permute-done.11.refs_2_.refs_6_.refs_11_ = bf16[4,32,2176]{2,1,0:T(8,128)(2,1)S(1)} collective-permute-done((bf16[4,32,2176]{2,1,0:T(8,128)(2,1)S(1)}, bf16[4,32,2176]{2,1,0:T(8,128)(2,1)S(1)}, u32[]{:S(2)}, u32[]{:S(2)}) %collective-permute-start.11) | collective-permute-done | bytes 557088 | tf_op jit(solution)/shard_map/ppermute | solution.py:32
  41.7 4.2 %hold_head.2 = (bf16[2048,2048]{1,0:T(8,128)(2,1)S(1)}, f32[8,128]{1,0:T(8,128)}) custom-call(bf16[2048,2048]{1,0:T(8,128)(2,1)} %refs_0_.2, bf16[8,2176]{1,0:T(8,128)(2,1)S(1)} %get-tuple-element.43.refs_1_), custom_call_target="tpu_custom_call" | custom-call | bytes 8388608 | tf_op jit(solution)/shard_map/hold_head/pallas_call | solution.py:57
  45.9 4.5 %partial_logits.3 = (s16[128,2176]{1,0:T(8,128)(2,1)S(1)}, s16[128,2176]{1,0:T(8,128)(2,1)S(1)}) custom-call(bf16[4,32,2176]{2,1,0:T(8,128)(2,1)S(1)} %pad_maximum_fusion.1.refs_0_.refs_4_.refs_9_, bf16[4,64,2176]{2,1,0:T(8,128)(2,1)S(1)} %bitcast.23, bf16[4,32,2176]{2,1,0:T(8,128)(2,1)S(1)} %collective-permute-done.11.refs_2_.refs_6_.refs_11_, ...), custom_call_target="tpu_custom_call" | custom-call | bytes 10485760 | tf_op jit(solution)/shard_map/partial_logits/pallas_call | solution.py:57
  50.9 3.2 %collective-permute-start.16 = (s16[128,2176]{1,0:T(8,128)(2,1)S(1)}, s16[128,2176]{1,0:T(8,128)(2,1)S(1)}, u32[]{:S(2)}, u32[]{:S(2)}) collective-permute-start(s16[128,2176]{1,0:T(8,128)(2,1)S(1)} %get-tuple-element.51), channel_id=1, source_target_pairs={{0,96},{32,0},{64,32},{96,64},{1,97},{33,1},{65,33},{97,65},{2,98}... | collective-permute-start | bytes 1671176 | tf_op jit(solution)/shard_map/ppermute | solution.py:22
  54.0 6.7 %partial_logits.4 = (f32[256,2048]{1,0:T(8,128)S(1)}, f32[256,2048]{1,0:T(8,128)S(1)}) custom-call(bf16[4,32,2176]{2,1,0:T(8,128)(2,1)S(1)} %pad_maximum_fusion.1.refs_0_.refs_4_.refs_9_, bf16[4,64,2176]{2,1,0:T(8,128)(2,1)S(1)} %bitcast.24, bf16[4,32,2176]{2,1,0:T(8,128)(2,1)S(1)} %collective-permute-done.11.refs_2_.refs_6_.refs_11_, ...), custom_call_target="tpu_custom_call" | custom-call | bytes 12582912 | tf_op jit(solution)/shard_map/partial_logits/pallas_call | solution.py:57
  60.7 6.0 %collective-permute-done.15.refs_2_ = s16[128,2176]{1,0:T(8,128)(2,1)S(1)} collective-permute-done((s16[128,2176]{1,0:T(8,128)(2,1)S(1)}, s16[128,2176]{1,0:T(8,128)(2,1)S(1)}, u32[]{:S(2)}, u32[]{:S(2)}) %collective-permute-start.15) | collective-permute-done | bytes 557088 | tf_op jit(solution)/shard_map/ppermute | solution.py:22
  68.1 3.1 %collective-permute-start.18 = (s16[256,2176]{1,0:T(8,128)(2,1)S(1)}, s16[256,2176]{1,0:T(8,128)(2,1)S(1)}, u32[]{:S(2)}, u32[]{:S(2)}) collective-permute-start(s16[256,2176]{1,0:T(8,128)(2,1)S(1)} %get-tuple-element.53), channel_id=1, source_target_pairs={{0,96},{32,0},{64,32},{96,64},{1,97},{33,1},{65,33},{97,65},{2,98}... | collective-permute-start | bytes 3342344 | tf_op jit(solution)/shard_map/ppermute | solution.py:22
  71.1 4.1 %partial_logits.5.refs_1_ = f32[256,2048]{1,0:T(8,128)S(1)} custom-call(bf16[4,32,2176]{2,1,0:T(8,128)(2,1)S(1)} %pad_maximum_fusion.1.refs_0_.refs_4_.refs_9_, bf16[4,64,2176]{2,1,0:T(8,128)(2,1)S(1)} %bitcast.25, bf16[4,32,2176]{2,1,0:T(8,128)(2,1)S(1)} %collective-permute-done.11.refs_2_.refs_6_.refs_11_, ...), custom_call_target="tpu_custom_call" | custom-call | bytes 10485760 | tf_op jit(solution)/shard_map/partial_logits/pallas_call | solution.py:57
  75.2 19.7 %collective-permute-done.17.refs_2_ = s16[256,2176]{1,0:T(8,128)(2,1)S(1)} collective-permute-done((s16[256,2176]{1,0:T(8,128)(2,1)S(1)}, s16[256,2176]{1,0:T(8,128)(2,1)S(1)}, u32[]{:S(2)}, u32[]{:S(2)}) %collective-permute-start.17) | collective-permute-done | bytes 1114144 | tf_op jit(solution)/shard_map/ppermute | solution.py:22
  95.0 2.5 %own_logits.1 = (bf16[128,2048]{1,0:T(8,128)(2,1)S(1)}, bf16[128,2048]{1,0:T(8,128)(2,1)S(1)}, f32[256,128]{1,0:T(8,128)S(1)}) custom-call(s32[5]{0:T(128)S(1)} %stack.62.refs_0_, f32[256,2048]{1,0:T(8,128)S(1)} %partial_logits.5.refs_1_, s16[256,2176]{1,0:T(8,128)(2,1)S(1)} %collective-permute-done.17.refs_2_, ...), custom_call_target="tpu_custom_call" | custom-call | flops 10485760 | bytes 6291456 | tf_op jit(solution)/shard_map/own_logits/pallas_call | solution.py:57
  98.4 2.4 %collective-permute-start.33 = (bf16[128,2048]{1,0:T(8,128)(2,1)S(1)}, bf16[128,2048]{1,0:T(8,128)(2,1)S(1)}, u32[]{:S(2)}, u32[]{:S(2)}) collective-permute-start(bf16[128,2048]{1,0:T(8,128)(2,1)S(1)} %get-tuple-element.58.refs_5_), channel_id=1, source_target_pairs={{0,96},{32,0},{64,32},{96,64},{1,97},{33,1},{65,33},{97,65},{2,98}... | collective-permute-start | bytes 1572872 | tf_op jit(solution)/shard_map/ppermute | solution.py:22
  100.8 12.8 %collective-permute-done.31.refs_8_ = bf16[128,2048]{1,0:T(8,128)(2,1)S(1)} collective-permute-done((bf16[128,2048]{1,0:T(8,128)(2,1)S(1)}, bf16[128,2048]{1,0:T(8,128)(2,1)S(1)}, u32[]{:S(2)}, u32[]{:S(2)}) %collective-permute-start.31) | collective-permute-done | bytes 524320 | tf_op jit(solution)/shard_map/ppermute | solution.py:22
  113.7 3.2 %collective-permute-start.34 = (bf16[128,2048]{1,0:T(8,128)(2,1)S(1)}, bf16[128,2048]{1,0:T(8,128)(2,1)S(1)}, u32[]{:S(2)}, u32[]{:S(2)}) collective-permute-start(bf16[128,2048]{1,0:T(8,128)(2,1)S(1)} %collective-permute-done.33.refs_6_), channel_id=1, source_target_pairs={{0,96},{32,0},{64,32},{96,64},{1,97},{33,1},{65,33},{97,65},{2,98}... | collective-permute-start | bytes 1572872 | tf_op jit(solution)/shard_map/ppermute | solution.py:22
  116.9 3.4 %hold_head.3 = (bf16[2048,2048]{1,0:T(8,128)(2,1)S(1)}, f32[8,128]{1,0:T(8,128)S(1)}) custom-call(bf16[2048,2048]{1,0:T(8,128)(2,1)} %collective-permute-done.19.refs_0_, f32[256,128]{1,0:T(8,128)S(1)} %get-tuple-element.54.refs_1_.refs_6_), custom_call_target="tpu_custom_call" | custom-call | bytes 8388608 | tf_op jit(solution)/shard_map/hold_head/pallas_call | solution.py:57
  120.3 3.4 %copy-done.7 = bf16[2048,2048]{1,0:T(8,128)(2,1)} copy-done((bf16[2048,2048]{1,0:T(8,128)(2,1)}, bf16[2048,2048]{1,0:T(8,128)(2,1)S(1)}, u32[]{:S(2)}) %copy-start.7) | copy-done | bytes 8388632
  125.7 1.8 collective-permute-start.22
  127.5 1.9 collective-permute-done.21.refs_1_
  129.6 1.3 collective-permute-done.22.refs_2_
  131.0 3.3 %collective-permute-done.23.refs_3_ = f32[8,256]{1,0:T(8,128)S(1)} collective-permute-done((f32[8,256]{1,0:T(8,128)S(1)}, f32[8,256]{1,0:T(8,128)S(1)}, u32[]{:S(2)}, u32[]{:S(2)}) %collective-permute-start.23) | collective-permute-done | bytes 8224 | tf_op jit(solution)/shard_map/ppermute | solution.py:32
  134.3 4.9 %collective-permute-start.24 = (f32[8,256]{1,0:T(8,128)S(1)}, f32[8,256]{1,0:T(8,128)S(1)}, u32[]{:S(2)}, u32[]{:S(2)}) collective-permute-start(f32[8,256]{1,0:T(8,128)S(1)} %merge_statistics.3.refs_2_), channel_id=1, source_target_pairs={{0,6},{1,7},{2,0},{3,1},{4,2},{5,3},{6,4},{7,5},{8,14},{9,15},{10,... | collective-permute-start | bytes 24584 | tf_op jit(solution)/shard_map/ppermute | solution.py:32
  142.0 3.0 %collective-permute-done.25.refs_4_ = f32[8,256]{1,0:T(8,128)S(1)} collective-permute-done((f32[8,256]{1,0:T(8,128)S(1)}, f32[8,256]{1,0:T(8,128)S(1)}, u32[]{:S(2)}, u32[]{:S(2)}) %collective-permute-start.25) | collective-permute-done | bytes 8224 | tf_op jit(solution)/shard_map/ppermute | solution.py:32
  145.7 1.4 combine_statistics.1.refs_1_.refs_6_
  149.2 1.6 collective-permute-done.27.refs_2_
  150.9 2.0 collective-permute-done.28.refs_3_
  153.6 2.1 dlogit.2.refs_12_.refs_7_
  155.8 2.3 collective-permute-start.30
  158.1 12.0 %collective-permute-done.30.refs_6_ = bf16[128,2048]{1,0:T(8,128)(2,1)S(1)} collective-permute-done((bf16[128,2048]{1,0:T(8,128)(2,1)S(1)}, bf16[128,2048]{1,0:T(8,128)(2,1)S(1)}, u32[]{:S(2)}, u32[]{:S(2)}) %collective-permute-start.30) | collective-permute-done | bytes 524320 | tf_op jit(solution)/shard_map/ppermute | solution.py:22
  170.1 2.1 dlogit.3.refs_0_.refs_6_
  172.3 12.2 %dnormed.1 = (f32[4,32,2048]{2,1,0:T(8,128)S(1)}, bf16[4,32,2048]{2,1,0:T(8,128)(2,1)}, bf16[4,32,2048]{2,1,0:T(8,128)(2,1)}, bf16[4,32,2048]{2,1,0:T(8,128)(2,1)}, f32[8,2048]{1,0:T(8,128)S(1)}) custom-call(bf16[4,128,2048]{2,1,0:T(8,128)(2,1)S(1)} %dlogit.3.refs_0_.refs_6_, bf16[4,128,2048]{2,1,0:T(8,128)(2,1)S(1)} %collective-permute-done.36.refs_1_, ...), custom_call_target="tpu_custom_call" | custom-call | bytes 16777216 | tf_op jit(solution)/shard_map/dnormed/pallas_call | solution.py:57
  184.5 1.3 collective-permute-start.37
  185.8 1.6 collective-permute-start.38
  187.4 1.6 collective-permute-start.39
  189.8 3.9 %all-to-all-start = ((f32[32,8,256]{2,1,0:T(8,128)}), f32[32,8,256]{2,1,0:T(8,128)S(1)}, u32[]{:S(2)}, u32[]{:S(2)}) async-start(f32[32,8,256]{2,1,0:T(8,128)} %gain_parts.1), calls=%async_computation | async-start | bytes 524288 | tf_op jit(solution)/shard_map/all_to_all | solution.py:647
  193.6 15.3 %head_grad.1 = (bf16[2048,2048]{1,0:T(8,128)(2,1)}, f32[8,128]{1,0:T(8,128)S(1)}) custom-call(bf16[4,32,2176]{2,1,0:T(8,128)(2,1)} %copy-done.2, bf16[4,64,2176]{2,1,0:T(8,128)(2,1)} %bitcast.29, bf16[4,32,2176]{2,1,0:T(8,128)(2,1)} %copy-done.3, bf16[4,32,2176]{2,1,0:T(8,128)(2,1)} %copy-done.4, bf16[4,64,2176]{2,1,0:T(8,128)(2,1)} %copy-done.1, ...), custom_call_target="tpu_custom_call" | custom-call | flops 8589934592 | bytes 16777216 | tf_op jit(solution)/shard_map/head_grad/pallas_call | solution.py:57
  208.9 4.1 %collective-permute-done.38.refs_2_ = bf16[4,32,2048]{2,1,0:T(8,128)(2,1)S(1)} collective-permute-done((bf16[4,32,2048]{2,1,0:T(8,128)(2,1)}, bf16[4,32,2048]{2,1,0:T(8,128)(2,1)S(1)}, u32[]{:S(2)}, u32[]{:S(2)}) %collective-permute-start.38) | collective-permute-done | bytes 524320 | tf_op jit(solution)/shard_map/ppermute | solution.py:32
  213.8 1.4 collective-permute-start.41
  215.3 1.8 collective-permute-start.42
  217.1 6.3 %collective-permute-done.40.refs_2_ = bf16[32,2048]{1,0:T(8,128)(2,1)S(1)} collective-permute-done((bf16[32,2048]{1,0:T(8,128)(2,1)}, bf16[32,2048]{1,0:T(8,128)(2,1)S(1)}, u32[]{:S(2)}, u32[]{:S(2)}) %collective-permute-start.40) | collective-permute-done | bytes 131104 | tf_op jit(solution)/shard_map/ppermute | solution.py:32
  224.5 11.2 %all_to_all.10.refs_2_ = f32[4,8,2432]{2,1,0:T(8,128)S(1)} all-to-all(f32[4,8,2432]{2,1,0:T(8,128)S(1)} %over_y.1), channel_id=1, replica_groups=mesh['section'=4,'vocab'=32] {'section'}, dimensions={0} | all-to-all | bytes 622592 | tf_op jit(solution)/shard_map/all_to_all | solution.py:651
  (103 shorter events, 24.2 us)
Async XLA Ops:
  2.5 4.8 %collective-permute-start = (bf16[8,2176]{1,0:T(8,128)(2,1)S(1)}, bf16[8,2176]{1,0:T(8,128)(2,1)S(1)}, u32[]{:S(2)}, u32[]{:S(2)}) collective-permute-start(bf16[8,2176]{1,0:T(8,128)(2,1)S(1)} %get-tuple-element.40), channel_id=1, source_target_pairs={{0,96},{32,0},{64,32},{96,64},{1,97},{33,1},{65,33},{97,65},{2,98}... | collective-permute-start | bytes 104456 | tf_op jit(solution)/shard_map/ppermute | solution.py:22
  5.7 5.4 %collective-permute-start.1 = (bf16[8,2176]{1,0:T(8,128)(2,1)S(1)}, bf16[8,2176]{1,0:T(8,128)(2,1)S(1)}, u32[]{:S(2)}, u32[]{:S(2)}) collective-permute-start(bf16[8,2176]{1,0:T(8,128)(2,1)S(1)} %get-tuple-element.41), channel_id=1, source_target_pairs={{0,64},{32,96},{64,0},{96,32},{1,65},{33,97},{65,1},{97,33},{2,66}... | collective-permute-start | bytes 104456 | tf_op jit(solution)/shard_map/ppermute | solution.py:22
  6.3 5.2 %collective-permute-start.2 = (bf16[8,2176]{1,0:T(8,128)(2,1)S(1)}, bf16[8,2176]{1,0:T(8,128)(2,1)S(1)}, u32[]{:S(2)}, u32[]{:S(2)}) collective-permute-start(bf16[8,2176]{1,0:T(8,128)(2,1)S(1)} %get-tuple-element.42), channel_id=1, source_target_pairs={{0,32},{32,64},{64,96},{96,0},{1,33},{33,65},{65,97},{97,1},{2,34}... | collective-permute-start | bytes 104456 | tf_op jit(solution)/shard_map/ppermute | solution.py:22
  11.5 8.6 %collective-permute-start.6 = (bf16[4,8,2176]{2,1,0:T(8,128)(2,1)S(1)}, bf16[4,8,2176]{2,1,0:T(8,128)(2,1)S(1)}, u32[]{:S(2)}, u32[]{:S(2)}) collective-permute-start(bf16[4,8,2176]{2,1,0:T(8,128)(2,1)S(1)} %pad_maximum_fusion.3), channel_id=1, source_target_pairs={{0,6},{1,7},{2,0},{3,1},{4,2},{5,3},{6,4},{7,5},{8,14},{9,15},{10,... | collective-permute-start | bytes 417800 | tf_op jit(solution)/shard_map/ppermute | solution.py:32
  15.6 6.3 %collective-permute-start.7 = (bf16[4,8,2176]{2,1,0:T(8,128)(2,1)S(1)}, bf16[4,8,2176]{2,1,0:T(8,128)(2,1)S(1)}, u32[]{:S(2)}, u32[]{:S(2)}) collective-permute-start(bf16[4,8,2176]{2,1,0:T(8,128)(2,1)S(1)} %pad_maximum_fusion.3), channel_id=1, source_target_pairs={{0,2},{1,3},{2,4},{3,5},{4,6},{5,7},{6,0},{7,1},{8,10},{9,11},{10,... | collective-permute-start | bytes 417800 | tf_op jit(solution)/shard_map/ppermute | solution.py:32
  15.6 9.9 %collective-permute-start.3 = (bf16[4,8,2176]{2,1,0:T(8,128)(2,1)S(1)}, bf16[4,8,2176]{2,1,0:T(8,128)(2,1)S(1)}, u32[]{:S(2)}, u32[]{:S(2)}) collective-permute-start(bf16[4,8,2176]{2,1,0:T(8,128)(2,1)S(1)} %pad_maximum_fusion.3), channel_id=1, source_target_pairs={{0,24},{1,25},{2,26},{3,27},{4,28},{5,29},{6,30},{7,31},{8,0},{9,1... | collective-permute-start | bytes 417800 | tf_op jit(solution)/shard_map/ppermute | solution.py:32
  18.4 8.1 %collective-permute-start.4 = (bf16[4,8,2176]{2,1,0:T(8,128)(2,1)S(1)}, bf16[4,8,2176]{2,1,0:T(8,128)(2,1)S(1)}, u32[]{:S(2)}, u32[]{:S(2)}) collective-permute-start(bf16[4,8,2176]{2,1,0:T(8,128)(2,1)S(1)} %pad_maximum_fusion.3), channel_id=1, source_target_pairs={{0,16},{1,17},{2,18},{3,19},{4,20},{5,21},{6,22},{7,23},{8,24},{9,... | collective-permute-start | bytes 417800 | tf_op jit(solution)/shard_map/ppermute | solution.py:32
  19.2 11.1 %collective-permute-start.5 = (bf16[4,8,2176]{2,1,0:T(8,128)(2,1)S(1)}, bf16[4,8,2176]{2,1,0:T(8,128)(2,1)S(1)}, u32[]{:S(2)}, u32[]{:S(2)}) collective-permute-start(bf16[4,8,2176]{2,1,0:T(8,128)(2,1)S(1)} %pad_maximum_fusion.3), channel_id=1, source_target_pairs={{0,8},{1,9},{2,10},{3,11},{4,12},{5,13},{6,14},{7,15},{8,16},{9,17... | collective-permute-start | bytes 417800 | tf_op jit(solution)/shard_map/ppermute | solution.py:32
  21.9 12.7 %collective-permute-start.8 = (bf16[4,2,8,2176]{3,2,0,1:T(8,128)(2,1)S(1)}, bf16[4,2,8,2176]{3,2,0,1:T(8,128)(2,1)S(1)}, u32[]{:S(2)}, u32[]{:S(2)}) collective-permute-start(bf16[4,2,8,2176]{3,2,0,1:T(8,128)(2,1)S(1)} %get-tuple-element.75), channel_id=1, source_target_pairs={{0,24},{1,25},{2,26},{3,27},{4,28},{5,29},{6,30},{7,31},{8,0},{9,1... | collective-permute-start | bytes 835592 | tf_op jit(solution)/shard_map/ppermute | solution.py:32
  24.8 10.7 %collective-permute-start.9 = (bf16[4,2,8,2176]{3,2,0,1:T(8,128)(2,1)S(1)}, bf16[4,2,8,2176]{3,2,0,1:T(8,128)(2,1)S(1)}, u32[]{:S(2)}, u32[]{:S(2)}) collective-permute-start(bf16[4,2,8,2176]{3,2,0,1:T(8,128)(2,1)S(1)} %get-tuple-element.75), channel_id=1, source_target_pairs={{0,16},{1,17},{2,18},{3,19},{4,20},{5,21},{6,22},{7,23},{8,24},{9,... | collective-permute-start | bytes 835592 | tf_op jit(solution)/shard_map/ppermute | solution.py:32
  25.6 12.8 %collective-permute-start.10 = (bf16[4,2,8,2176]{3,2,0,1:T(8,128)(2,1)S(1)}, bf16[4,2,8,2176]{3,2,0,1:T(8,128)(2,1)S(1)}, u32[]{:S(2)}, u32[]{:S(2)}) collective-permute-start(bf16[4,2,8,2176]{3,2,0,1:T(8,128)(2,1)S(1)} %get-tuple-element.75), channel_id=1, source_target_pairs={{0,8},{1,9},{2,10},{3,11},{4,12},{5,13},{6,14},{7,15},{8,16},{9,17... | collective-permute-start | bytes 835592 | tf_op jit(solution)/shard_map/ppermute | solution.py:32
  30.3 141.9 %copy-start.2 = (bf16[4,32,2176]{2,1,0:T(8,128)(2,1)}, bf16[4,32,2176]{2,1,0:T(8,128)(2,1)S(1)}, u32[]{:S(2)}) copy-start(bf16[4,32,2176]{2,1,0:T(8,128)(2,1)S(1)} %pad_maximum_fusion.1.refs_0_.refs_4_.refs_9_) | copy-start | bytes 1671172
  30.3 11.3 %collective-permute-start.11 = (bf16[4,32,2176]{2,1,0:T(8,128)(2,1)S(1)}, bf16[4,32,2176]{2,1,0:T(8,128)(2,1)S(1)}, u32[]{:S(2)}, u32[]{:S(2)}) collective-permute-start(bf16[4,32,2176]{2,1,0:T(8,128)(2,1)S(1)} %pad_maximum_fusion.1.refs_0_.refs_4_.refs_9_), channel_id=1, source_target_pairs={{0,4},{1,5},{2,6},{3,7},{4,0},{5,1},{6,2},{7,3},{8,12},{9,13},{10,... | collective-permute-start | bytes 1671176 | tf_op jit(solution)/shard_map/ppermute | solution.py:32
  38.7 133.6 %copy-start = (bf16[4,2,4,8,2176]{4,3,2,1,0:T(8,128)(2,1)}, bf16[4,2,4,8,2176]{4,3,2,1,0:T(8,128)(2,1)S(1)}, u32[]{:S(2)}) copy-start(bf16[4,2,4,8,2176]{4,3,2,1,0:T(8,128)(2,1)S(1)} %copy.11) | copy-start | bytes 3342340
  38.7 7.2 %collective-permute-start.13 = (bf16[4,64,2176]{2,1,0:T(8,128)(2,1)S(1)}, bf16[4,64,2176]{2,1,0:T(8,128)(2,1)S(1)}, u32[]{:S(2)}, u32[]{:S(2)}) collective-permute-start(bf16[4,64,2176]{2,1,0:T(8,128)(2,1)S(1)} %bitcast.22), channel_id=1, source_target_pairs={{0,1},{1,0},{2,3},{3,2},{4,5},{5,4},{6,7},{7,6},{8,9},{9,8},{10,11... | collective-permute-start | bytes 3342344 | tf_op jit(solution)/shard_map/ppermute | solution.py:32
  38.8 7.1 %collective-permute-start.12 = (bf16[4,32,2176]{2,1,0:T(8,128)(2,1)S(1)}, bf16[4,32,2176]{2,1,0:T(8,128)(2,1)S(1)}, u32[]{:S(2)}, u32[]{:S(2)}) collective-permute-start(bf16[4,32,2176]{2,1,0:T(8,128)(2,1)S(1)} %pad_maximum_fusion.1.refs_0_.refs_4_.refs_9_), channel_id=1, source_target_pairs={{0,1},{1,0},{2,3},{3,2},{4,5},{5,4},{6,7},{7,6},{8,9},{9,8},{10,11... | collective-permute-start | bytes 1671176 | tf_op jit(solution)/shard_map/ppermute | solution.py:32
  41.6 130.6 %copy-start.3 = (bf16[4,32,2176]{2,1,0:T(8,128)(2,1)}, bf16[4,32,2176]{2,1,0:T(8,128)(2,1)S(1)}, u32[]{:S(2)}) copy-start(bf16[4,32,2176]{2,1,0:T(8,128)(2,1)S(1)} %collective-permute-done.11.refs_2_.refs_6_.refs_11_) | copy-start | bytes 1671172
  41.7 4.2 %collective-permute-start.14 = (bf16[4,32,2176]{2,1,0:T(8,128)(2,1)S(1)}, bf16[4,32,2176]{2,1,0:T(8,128)(2,1)S(1)}, u32[]{:S(2)}, u32[]{:S(2)}) collective-permute-start(bf16[4,32,2176]{2,1,0:T(8,128)(2,1)S(1)} %collective-permute-done.11.refs_2_.refs_6_.refs_11_), channel_id=1, source_target_pairs={{0,1},{1,0},{2,3},{3,2},{4,5},{5,4},{6,7},{7,6},{8,9},{9,8},{10,11... | collective-permute-start | bytes 1671176 | tf_op jit(solution)/shard_map/ppermute | solution.py:32
  45.9 107.7 %copy-start.4 = (bf16[4,32,2176]{2,1,0:T(8,128)(2,1)}, bf16[4,32,2176]{2,1,0:T(8,128)(2,1)S(1)}, u32[]{:S(2)}) copy-start(bf16[4,32,2176]{2,1,0:T(8,128)(2,1)S(1)} %collective-permute-done.12.refs_3_.refs_7_.refs_9_) | copy-start | bytes 1671172
  50.4 66.5 %collective-permute-start.19 = (bf16[2048,2048]{1,0:T(8,128)(2,1)}, bf16[2048,2048]{1,0:T(8,128)(2,1)}, u32[]{:S(2)}, u32[]{:S(2)}) collective-permute-start(bf16[2048,2048]{1,0:T(8,128)(2,1)} %refs_0_.2), channel_id=1, source_target_pairs={{0,1},{1,0},{2,3},{3,2},{4,5},{5,4},{6,7},{7,6},{8,9},{9,8},{10,11... | collective-permute-start | bytes 25165832 | tf_op jit(solution)/shard_map/ppermute | solution.py:32
  50.8 16.0 %collective-permute-start.15 = (s16[128,2176]{1,0:T(8,128)(2,1)S(1)}, s16[128,2176]{1,0:T(8,128)(2,1)S(1)}, u32[]{:S(2)}, u32[]{:S(2)}) collective-permute-start(s16[128,2176]{1,0:T(8,128)(2,1)S(1)} %get-tuple-element.48.refs_7_), channel_id=1, source_target_pairs={{0,32},{32,64},{64,96},{96,0},{1,33},{33,65},{65,97},{97,1},{2,34}... | collective-permute-start | bytes 1671176 | tf_op jit(solution)/shard_map/ppermute | solution.py:22
  50.9 15.9 %collective-permute-start.16 = (s16[128,2176]{1,0:T(8,128)(2,1)S(1)}, s16[128,2176]{1,0:T(8,128)(2,1)S(1)}, u32[]{:S(2)}, u32[]{:S(2)}) collective-permute-start(s16[128,2176]{1,0:T(8,128)(2,1)S(1)} %get-tuple-element.51), channel_id=1, source_target_pairs={{0,96},{32,0},{64,32},{96,64},{1,97},{33,1},{65,33},{97,65},{2,98}... | collective-permute-start | bytes 1671176 | tf_op jit(solution)/shard_map/ppermute | solution.py:22
  67.8 27.1 %collective-permute-start.17 = (s16[256,2176]{1,0:T(8,128)(2,1)S(1)}, s16[256,2176]{1,0:T(8,128)(2,1)S(1)}, u32[]{:S(2)}, u32[]{:S(2)}) collective-permute-start(s16[256,2176]{1,0:T(8,128)(2,1)S(1)} %get-tuple-element.52.refs_7_), channel_id=1, source_target_pairs={{0,32},{32,64},{64,96},{96,0},{1,33},{33,65},{65,97},{97,1},{2,34}... | collective-permute-start | bytes 3342344 | tf_op jit(solution)/shard_map/ppermute | solution.py:22
  68.1 26.9 %collective-permute-start.18 = (s16[256,2176]{1,0:T(8,128)(2,1)S(1)}, s16[256,2176]{1,0:T(8,128)(2,1)S(1)}, u32[]{:S(2)}, u32[]{:S(2)}) collective-permute-start(s16[256,2176]{1,0:T(8,128)(2,1)S(1)} %get-tuple-element.53), channel_id=1, source_target_pairs={{0,96},{32,0},{64,32},{96,64},{1,97},{33,1},{65,33},{97,65},{2,98}... | collective-permute-start | bytes 3342344 | tf_op jit(solution)/shard_map/ppermute | solution.py:22
  97.5 16.1 %collective-permute-start.31 = (bf16[128,2048]{1,0:T(8,128)(2,1)S(1)}, bf16[128,2048]{1,0:T(8,128)(2,1)S(1)}, u32[]{:S(2)}, u32[]{:S(2)}) collective-permute-start(bf16[128,2048]{1,0:T(8,128)(2,1)S(1)} %get-tuple-element.57.refs_5_), channel_id=1, source_target_pairs={{0,32},{32,64},{64,96},{96,0},{1,33},{33,65},{65,97},{97,1},{2,34}... | collective-permute-start | bytes 1572872 | tf_op jit(solution)/shard_map/ppermute | solution.py:22
  98.4 15.3 %collective-permute-start.33 = (bf16[128,2048]{1,0:T(8,128)(2,1)S(1)}, bf16[128,2048]{1,0:T(8,128)(2,1)S(1)}, u32[]{:S(2)}, u32[]{:S(2)}) collective-permute-start(bf16[128,2048]{1,0:T(8,128)(2,1)S(1)} %get-tuple-element.58.refs_5_), channel_id=1, source_target_pairs={{0,96},{32,0},{64,32},{96,64},{1,97},{33,1},{65,33},{97,65},{2,98}... | collective-permute-start | bytes 1572872 | tf_op jit(solution)/shard_map/ppermute | solution.py:22
  100.8 47.2 %collective-permute-start.35 = (bf16[128,2048]{1,0:T(8,128)(2,1)S(1)}, bf16[128,2048]{1,0:T(8,128)(2,1)S(1)}, u32[]{:S(2)}, u32[]{:S(2)}) collective-permute-start(bf16[128,2048]{1,0:T(8,128)(2,1)S(1)} %get-tuple-element.58.refs_5_), channel_id=1, source_target_pairs={{0,32},{32,64},{64,96},{96,0},{1,33},{33,65},{65,97},{97,1},{2,34}... | collective-permute-start | bytes 1572872 | tf_op jit(solution)/shard_map/ppermute | solution.py:22
  113.6 35.6 %collective-permute-start.32 = (bf16[128,2048]{1,0:T(8,128)(2,1)S(1)}, bf16[128,2048]{1,0:T(8,128)(2,1)S(1)}, u32[]{:S(2)}, u32[]{:S(2)}) collective-permute-start(bf16[128,2048]{1,0:T(8,128)(2,1)S(1)} %collective-permute-done.31.refs_8_), channel_id=1, source_target_pairs={{0,32},{32,64},{64,96},{96,0},{1,33},{33,65},{65,97},{97,1},{2,34}... | collective-permute-start | bytes 1572872 | tf_op jit(solution)/shard_map/ppermute | solution.py:22
  113.7 35.6 %collective-permute-start.34 = (bf16[128,2048]{1,0:T(8,128)(2,1)S(1)}, bf16[128,2048]{1,0:T(8,128)(2,1)S(1)}, u32[]{:S(2)}, u32[]{:S(2)}) collective-permute-start(bf16[128,2048]{1,0:T(8,128)(2,1)S(1)} %collective-permute-done.33.refs_6_), channel_id=1, source_target_pairs={{0,96},{32,0},{64,32},{96,64},{1,97},{33,1},{65,33},{97,65},{2,98}... | collective-permute-start | bytes 1572872 | tf_op jit(solution)/shard_map/ppermute | solution.py:22
  124.4 1.2 collective-permute-start.20
  125.6 3.8 %collective-permute-start.21 = (f32[8,256]{1,0:T(8,128)S(1)}, f32[8,256]{1,0:T(8,128)S(1)}, u32[]{:S(2)}, u32[]{:S(2)}) collective-permute-start(f32[8,256]{1,0:T(8,128)S(1)} %merge_statistics.2.refs_0_), channel_id=1, source_target_pairs={{0,24},{1,25},{2,26},{3,27},{4,28},{5,29},{6,30},{7,31},{8,0},{9,1... | collective-permute-start | bytes 24584 | tf_op jit(solution)/shard_map/ppermute | solution.py:32
  125.7 5.2 %collective-permute-start.22 = (f32[8,256]{1,0:T(8,128)S(1)}, f32[8,256]{1,0:T(8,128)S(1)}, u32[]{:S(2)}, u32[]{:S(2)}) collective-permute-start(f32[8,256]{1,0:T(8,128)S(1)} %merge_statistics.2.refs_0_), channel_id=1, source_target_pairs={{0,16},{1,17},{2,18},{3,19},{4,20},{5,21},{6,22},{7,23},{8,24},{9,... | collective-permute-start | bytes 24584 | tf_op jit(solution)/shard_map/ppermute | solution.py:32
  129.4 4.9 %collective-permute-start.23 = (f32[8,256]{1,0:T(8,128)S(1)}, f32[8,256]{1,0:T(8,128)S(1)}, u32[]{:S(2)}, u32[]{:S(2)}) collective-permute-start(f32[8,256]{1,0:T(8,128)S(1)} %merge_statistics.2.refs_0_), channel_id=1, source_target_pairs={{0,8},{1,9},{2,10},{3,11},{4,12},{5,13},{6,14},{7,15},{8,16},{9,17... | collective-permute-start | bytes 24584 | tf_op jit(solution)/shard_map/ppermute | solution.py:32
  134.3 6.3 %collective-permute-start.24 = (f32[8,256]{1,0:T(8,128)S(1)}, f32[8,256]{1,0:T(8,128)S(1)}, u32[]{:S(2)}, u32[]{:S(2)}) collective-permute-start(f32[8,256]{1,0:T(8,128)S(1)} %merge_statistics.3.refs_2_), channel_id=1, source_target_pairs={{0,6},{1,7},{2,0},{3,1},{4,2},{5,3},{6,4},{7,5},{8,14},{9,15},{10,... | collective-permute-start | bytes 24584 | tf_op jit(solution)/shard_map/ppermute | solution.py:32
  139.8 5.2 %collective-permute-start.25 = (f32[8,256]{1,0:T(8,128)S(1)}, f32[8,256]{1,0:T(8,128)S(1)}, u32[]{:S(2)}, u32[]{:S(2)}) collective-permute-start(f32[8,256]{1,0:T(8,128)S(1)} %merge_statistics.3.refs_2_), channel_id=1, source_target_pairs={{0,4},{1,5},{2,6},{3,7},{4,0},{5,1},{6,2},{7,3},{8,12},{9,13},{10,... | collective-permute-start | bytes 24584 | tf_op jit(solution)/shard_map/ppermute | solution.py:32
  140.6 5.1 %collective-permute-start.26 = (f32[8,256]{1,0:T(8,128)S(1)}, f32[8,256]{1,0:T(8,128)S(1)}, u32[]{:S(2)}, u32[]{:S(2)}) collective-permute-start(f32[8,256]{1,0:T(8,128)S(1)} %merge_statistics.3.refs_2_), channel_id=1, source_target_pairs={{0,2},{1,3},{2,4},{3,5},{4,6},{5,7},{6,0},{7,1},{8,10},{9,11},{10,... | collective-permute-start | bytes 24584 | tf_op jit(solution)/shard_map/ppermute | solution.py:32
  147.2 3.7 %collective-permute-start.27 = (f32[8,256]{1,0:T(8,128)S(1)}, f32[8,256]{1,0:T(8,128)S(1)}, u32[]{:S(2)}, u32[]{:S(2)}) collective-permute-start(f32[8,256]{1,0:T(8,128)S(1)} %combine_statistics.1.refs_1_.refs_6_), channel_id=1, source_target_pairs={{0,96},{32,0},{64,32},{96,64},{1,97},{33,1},{65,33},{97,65},{2,98}... | collective-permute-start | bytes 24584 | tf_op jit(solution)/shard_map/ppermute | solution.py:22
  147.7 5.2 %collective-permute-start.28 = (f32[8,256]{1,0:T(8,128)S(1)}, f32[8,256]{1,0:T(8,128)S(1)}, u32[]{:S(2)}, u32[]{:S(2)}) collective-permute-start(f32[8,256]{1,0:T(8,128)S(1)} %combine_statistics.1.refs_1_.refs_6_), channel_id=1, source_target_pairs={{0,64},{32,96},{64,0},{96,32},{1,65},{33,97},{65,1},{97,33},{2,66}... | collective-permute-start | bytes 24584 | tf_op jit(solution)/shard_map/ppermute | solution.py:22
  148.1 5.5 %collective-permute-start.29 = (f32[8,256]{1,0:T(8,128)S(1)}, f32[8,256]{1,0:T(8,128)S(1)}, u32[]{:S(2)}, u32[]{:S(2)}) collective-permute-start(f32[8,256]{1,0:T(8,128)S(1)} %combine_statistics.1.refs_1_.refs_6_), channel_id=1, source_target_pairs={{0,32},{32,64},{64,96},{96,0},{1,33},{33,65},{65,97},{97,1},{2,34}... | collective-permute-start | bytes 24584 | tf_op jit(solution)/shard_map/ppermute | solution.py:22
  155.7 16.6 %collective-permute-start.36 = (bf16[4,128,2048]{2,1,0:T(8,128)(2,1)S(1)}, bf16[4,128,2048]{2,1,0:T(8,128)(2,1)S(1)}, u32[]{:S(2)}, u32[]{:S(2)}) collective-permute-start(bf16[4,128,2048]{2,1,0:T(8,128)(2,1)S(1)} %dlogit.2.refs_12_.refs_7_), channel_id=1, source_target_pairs={{0,1},{1,0},{2,3},{3,2},{4,5},{5,4},{6,7},{7,6},{8,9},{9,8},{10,11... | collective-permute-start | bytes 6291464 | tf_op jit(solution)/shard_map/ppermute | solution.py:32
  155.8 14.3 %collective-permute-start.30 = (bf16[128,2048]{1,0:T(8,128)(2,1)S(1)}, bf16[128,2048]{1,0:T(8,128)(2,1)S(1)}, u32[]{:S(2)}, u32[]{:S(2)}) collective-permute-start(bf16[128,2048]{1,0:T(8,128)(2,1)S(1)} %get-tuple-element.57.refs_5_), channel_id=1, source_target_pairs={{0,96},{32,0},{64,32},{96,64},{1,97},{33,1},{65,33},{97,65},{2,98}... | collective-permute-start | bytes 1572872 | tf_op jit(solution)/shard_map/ppermute | solution.py:22
  184.5 24.4 %collective-permute-start.37 = (bf16[4,32,2048]{2,1,0:T(8,128)(2,1)}, bf16[4,32,2048]{2,1,0:T(8,128)(2,1)S(1)}, u32[]{:S(2)}, u32[]{:S(2)}) collective-permute-start(bf16[4,32,2048]{2,1,0:T(8,128)(2,1)} %get-tuple-element.61), channel_id=1, source_target_pairs={{0,4},{1,5},{2,6},{3,7},{4,0},{5,1},{6,2},{7,3},{8,12},{9,13},{10,... | collective-permute-start | bytes 1572872 | tf_op jit(solution)/shard_map/ppermute | solution.py:32
  185.8 27.2 %collective-permute-start.38 = (bf16[4,32,2048]{2,1,0:T(8,128)(2,1)}, bf16[4,32,2048]{2,1,0:T(8,128)(2,1)S(1)}, u32[]{:S(2)}, u32[]{:S(2)}) collective-permute-start(bf16[4,32,2048]{2,1,0:T(8,128)(2,1)} %get-tuple-element.62), channel_id=1, source_target_pairs={{0,2},{1,3},{2,4},{3,5},{4,6},{5,7},{6,0},{7,1},{8,10},{9,11},{10,... | collective-permute-start | bytes 1572872 | tf_op jit(solution)/shard_map/ppermute | solution.py:32
  187.4 25.7 %collective-permute-start.39 = (bf16[4,32,2048]{2,1,0:T(8,128)(2,1)}, bf16[4,32,2048]{2,1,0:T(8,128)(2,1)S(1)}, u32[]{:S(2)}, u32[]{:S(2)}) collective-permute-start(bf16[4,32,2048]{2,1,0:T(8,128)(2,1)} %get-tuple-element.63), channel_id=1, source_target_pairs={{0,6},{1,7},{2,0},{3,1},{4,2},{5,3},{6,4},{7,5},{8,14},{9,15},{10,... | collective-permute-start | bytes 1572872 | tf_op jit(solution)/shard_map/ppermute | solution.py:32
  189.8 27.3 %all-to-all-start = ((f32[32,8,256]{2,1,0:T(8,128)}), f32[32,8,256]{2,1,0:T(8,128)S(1)}, u32[]{:S(2)}, u32[]{:S(2)}) async-start(f32[32,8,256]{2,1,0:T(8,128)} %gain_parts.1), calls=%async_computation | async-start | bytes 524288 | tf_op jit(solution)/shard_map/all_to_all | solution.py:647
  213.8 9.6 %collective-permute-start.40 = (bf16[32,2048]{1,0:T(8,128)(2,1)}, bf16[32,2048]{1,0:T(8,128)(2,1)S(1)}, u32[]{:S(2)}, u32[]{:S(2)}) collective-permute-start(bf16[32,2048]{1,0:T(8,128)(2,1)} %get-tuple-element.67), channel_id=1, source_target_pairs={{0,8},{1,9},{2,10},{3,11},{4,12},{5,13},{6,14},{7,15},{8,16},{9,17... | collective-permute-start | bytes 393224 | tf_op jit(solution)/shard_map/ppermute | solution.py:32
  213.8 9.6 %collective-permute-start.41 = (bf16[32,2048]{1,0:T(8,128)(2,1)S(1)}, bf16[32,2048]{1,0:T(8,128)(2,1)S(1)}, u32[]{:S(2)}, u32[]{:S(2)}) collective-permute-start(bf16[32,2048]{1,0:T(8,128)(2,1)S(1)} %get-tuple-element.68), channel_id=1, source_target_pairs={{0,16},{1,17},{2,18},{3,19},{4,20},{5,21},{6,22},{7,23},{8,24},{9,... | collective-permute-start | bytes 393224 | tf_op jit(solution)/shard_map/ppermute | solution.py:32
  215.3 8.5 %collective-permute-start.42 = (bf16[32,2048]{1,0:T(8,128)(2,1)S(1)}, bf16[32,2048]{1,0:T(8,128)(2,1)S(1)}, u32[]{:S(2)}, u32[]{:S(2)}) collective-permute-start(bf16[32,2048]{1,0:T(8,128)(2,1)S(1)} %get-tuple-element.69), channel_id=1, source_target_pairs={{0,24},{1,25},{2,26},{3,27},{4,28},{5,29},{6,30},{7,31},{8,0},{9,1... | collective-permute-start | bytes 393224 | tf_op jit(solution)/shard_map/ppermute | solution.py:32
  (12 other events, 352.4 us)
